TPU v7x, 32 devices: a whole 2x2x4 slice. The times are simulated.
32 devices in a mesh: dp: 8 (over z, x), chan: 4 (over y, core).
Axes of the slice: x: 2, y: 2, z: 4, core: 2. Of those that a mesh axis runs over, the one named last changes fastest.
Arguments:
- features_in: float32 [64, 14, 14, 1024], P('dp', None, None, 'chan')
- image_counts: int32 [8], replicated, may hold values from 4 to 8, as said below
- reduce_weight: float32 [1024, 256], P('chan'), may hold values from -0.1875 to 0.1875
- reduce_gain: float32 [256], P('chan'), may hold values from 0.5 to 1.5
- reduce_shift: float32 [256], P('chan'), may hold values from -3 to 3
- split_weight: float32 [3, 3, 128, 2, 256], P(None, None, None, None, 'chan'), may hold values from -0.1875 to 0.1875
- split_gain: float32 [2, 256], P(None, 'chan'), may hold values from 0.5 to 1.5
- split_shift: float32 [2, 256], P(None, 'chan'), may hold values from -3 to 3
- squeeze_weight: float32 [256, 128], P('chan'), may hold values from -0.375 to 0.375
- squeeze_gain: float32 [128], replicated, may hold values from 0.5 to 1.5
- squeeze_shift: float32 [128], replicated, may hold values from -3 to 3
- attend_weight: float32 [128, 2, 256], P(None, None, 'chan'), may hold values from -0.5 to 0.5
- attend_bias: float32 [2, 256], P(None, 'chan'), may hold values from -3 to 3
- expand_weight: float32 [256, 1024], P(None, 'chan'), may hold values from -0.375 to 0.375
- expand_gain: float32 [1024], P('chan'), may hold values from 0.5 to 1.5
- expand_shift: float32 [1024], P('chan'), may hold values from -3 to 3
- grad_out: float32 [64, 14, 14, 1024], P('dp', None, None, 'chan'), may hold values from -6 to 6
Outputs:
- block_out: float32 [64, 14, 14, 1024], P('dp', None, None, 'chan')
- grad_input: float32 [64, 14, 14, 1024], P('dp', None, None, 'chan')
- grad_reduce_weight: float32 [1024, 256], P('chan')
- grad_reduce_gain: float32 [256], P('chan')
- grad_reduce_shift: float32 [256], P('chan')
- grad_split_weight: float32 [3, 3, 128, 2, 256], P(None, None, None, None, 'chan')
- grad_split_gain: float32 [2, 256], P(None, 'chan')
- grad_split_shift: float32 [2, 256], P(None, 'chan')
- grad_squeeze_weight: float32 [256, 128], P('chan')
- grad_squeeze_gain: float32 [128], replicated
- grad_squeeze_shift: float32 [128], replicated
- grad_attend_weight: float32 [128, 2, 256], P(None, None, 'chan')
- grad_attend_bias: float32 [2, 256], P(None, 'chan')
- grad_expand_weight: float32 [256, 1024], P(None, 'chan')
- grad_expand_gain: float32 [1024], P('chan')
- grad_expand_shift: float32 [1024], P('chan')
Inputs may be any that keep to these rules, and one draw needn't show every extreme that they name: image_counts[k] valid images fill the first slots of dp index k; in every draw some index holds 8 valid images and some other exactly 4.
All inputs are finite; a program needn't handle non-finite values.
Results may differ from a plain program's by a relative error of at most 0.012.
Values sent between devices are 32-bit elements; how exact they have to be, the bound alone decides.
No kernel may reach another device: no remote copies, remote signals or barrier semaphores. Data moves between devices by JAX's collectives and lax.ppermute only.
A program may use at most 64 MiB of HBM per device.

v0:
```python
import functools

import jax
import jax.numpy as jnp
from jax import lax
from jax.experimental import pallas as pl
from jax.experimental.pallas import tpu as pltpu
from jax.sharding import PartitionSpec as P

EPSILON = 1e-05
F32, BF16 = jnp.float32, jnp.bfloat16
PAD = 16
VMEM_LIMIT = 44 * 1024 * 1024


def bits_of(n):
    out, k = [], 1
    while k < n:
        out.append(k)
        k *= 2
    return out


def split2(x):
    hi = x.astype(BF16)
    return hi, (x - hi.astype(F32)).astype(BF16)


def mm(a, b, dims=((1,), (0,))):
    return lax.dot_general(a, b, (dims, ((), ())), preferred_element_type=F32)


def mm3(ah, al, bh, bl):
    return mm(ah, bh) + (mm(ah, bl) + mm(al, bh))


def exact(a, b, dims=((1,), (0,))):
    return lax.dot_general(
        a, b, (dims, ((), ())), precision=lax.Precision.HIGHEST, preferred_element_type=F32
    )


def call(body, ins, outs, scratch=(), scalars=None, specs=None, flops=0):
    out_shape = [jax.ShapeDtypeStruct(s, d) for s, d in outs]
    whole = lambda n: lambda *_: (0,) * n
    in_specs = []
    for k, a in enumerate(ins):
        s = None if specs is None else specs.get(k)
        in_specs.append(s or pl.BlockSpec(a.shape, whole(a.ndim)))
    moved = sum(a.size * a.dtype.itemsize for a in ins) + sum(
        int(jnp.dtype(d).itemsize) * functools.reduce(lambda x, y: x * y, s, 1) for s, d in outs
    )
    return pl.pallas_call(
        body,
        out_shape=out_shape,
        grid_spec=pltpu.PrefetchScalarGridSpec(
            num_scalar_prefetch=1,
            grid=(1,),
            in_specs=in_specs,
            out_specs=[pl.BlockSpec(s, whole(len(s))) for s, _ in outs],
            scratch_shapes=list(scratch),
        ),
        compiler_params=pltpu.CompilerParams(vmem_limit_bytes=VMEM_LIMIT),
        cost_estimate=pl.CostEstimate(flops=flops, bytes_accessed=moved, transcendentals=0),
    )(scalars, *ins)


def mask_of(nv, rows, cols, edge):
    r = lax.broadcasted_iota(jnp.int32, (rows, cols), 0)
    return ((r & (PAD - 1)) < edge) & (r < nv * (edge * PAD))


def padded(ref, scr, mask):
    n, e, _, w = ref.shape
    scr[:, :e, :] = ref[...].reshape(n * e, e, w)
    return jnp.where(mask, scr[...].reshape(n * e * PAD, w), 0.0)


def colsum(x):
    return jnp.sum(x, axis=0, keepdims=True)


def build(mesh):
    nd, nc = mesh.shape["dp"], mesh.shape["chan"]
    both = ("dp", "chan")
    cbits, dbits = bits_of(nc), bits_of(nd)
    all_bits = [1] + [k | 1 for k in bits_of(nd * nc)[1:]]
    sum_order = [all_bits[0]] + all_bits[:0:-1]

    def swap(x, axis, k):
        n = {"dp": nd, "chan": nc}[axis] if isinstance(axis, str) else nd * nc
        return lax.ppermute(x, axis, [(i, i ^ k) for i in range(n)])

    def sum_all(x):
        for k in sum_order:
            x = x + swap(x, both, k)
        return x

    def gather_all(x):
        for k in all_bits[::-1]:
            x = jnp.concatenate([x, swap(x, both, k)], axis=0)
        return x

    def order_all():
        me = lax.axis_index("dp") * nc + lax.axis_index("chan")
        rel = [0]
        for k in all_bits[::-1]:
            rel = rel + [r ^ k for r in rel]
        return jnp.bitwise_xor(me, jnp.array(rel, jnp.int32))

    def pick(x, i):
        return lax.dynamic_index_in_dim(x, i, 0, False)

    def big_sum_dp(x):
        d = lax.axis_index("dp")
        h = x.reshape((nd, x.shape[0] // nd) + x.shape[1:])
        if nd <= 8:
            acc = pick(h, d)
            for k in range(1, nd):
                acc = acc + swap(pick(h, d ^ k), "dp", k)
            parts = [acc] + [swap(acc, "dp", k) for k in range(1, nd)]
            o = jnp.zeros_like(h)
            for k in range(nd):
                o = lax.dynamic_update_index_in_dim(o, parts[k], d ^ k, 0)
            return o.reshape(x.shape)
        cur = h
        for k in dbits:
            b = (d // k) % 2
            g = cur.reshape((2, cur.shape[0] // 2) + cur.shape[1:])
            cur = pick(g, b) + swap(pick(g, 1 - b), "dp", k)
        for k in dbits[::-1]:
            b = (d // k) % 2
            o = swap(cur, "dp", k)
            cur = jnp.where(b == 0, jnp.concatenate([cur, o]), jnp.concatenate([o, cur]))
        return cur.reshape(x.shape)

    def quarter_of(chan):
        q = chan * 0
        for k in cbits:
            q = q * 2 + (chan // k) % 2
        return q

    def per_device(
        features_in,
        image_counts,
        reduce_weight,
        reduce_gain,
        reduce_shift,
        split_weight,
        split_gain,
        split_shift,
        squeeze_weight,
        squeeze_gain,
        squeeze_shift,
        attend_weight,
        attend_bias,
        expand_weight,
        expand_gain,
        expand_shift,
        grad_out,
    ):
        slots, edge = features_in.shape[0], features_in.shape[1]
        area = edge * edge
        win = features_in.shape[3]
        mid = reduce_weight.shape[1]
        half = mid // 2
        lw = split_weight.shape[4]
        inner = squeeze_gain.shape[0]
        own = slots // nc
        span = edge * PAD
        R = own * span
        ni = nd * slots
        d, c = lax.axis_index("dp"), lax.axis_index("chan")
        q = quarter_of(c)
        owned = lax.dynamic_index_in_dim(image_counts, d, 0, False)
        nv = [jnp.clip(owned - (q ^ r) * own, 0, own) for r in range(nc)]
        isc = jnp.stack([c, q] + nv + [d * slots + q * own]).astype(jnp.int32)
        NV, G0 = 2, 2 + nc
        images = jnp.sum(image_counts).astype(F32)
        fsc = jnp.stack([1.0 / (images * area), 1.0 / images, images * area, images])
        fsc = jnp.broadcast_to(fsc[:, None], (4, 128))

        TAPS = [(u, v) for u in range(3) for v in range(3)]

        def stats(sum_ref, fs, gains=None):
            avg = sum_ref[0:1] * fs[0:1, 0:1]
            inv = lax.rsqrt(sum_ref[1:2] * fs[0:1, 0:1] - avg * avg + EPSILON)
            return avg, inv

        def quarter_spec(r):
            return pl.BlockSpec((own, edge, edge, win), lambda i, s: (s[1] ^ r, 0, 0, 0))

        pa = jnp.concatenate(
            [
                split_weight.reshape(-1, 2 * lw),
                attend_weight.reshape(-1, 2 * lw),
                jnp.stack(
                    [
                        split_gain.reshape(-1),
                        split_shift.reshape(-1),
                        attend_bias.reshape(-1),
                        jnp.concatenate([reduce_gain, reduce_shift]),
                    ]
                ),
                jnp.zeros((4, 2 * lw), F32),
                squeeze_weight,
            ]
        )
        pb = jnp.concatenate([expand_weight, expand_gain[None], jnp.zeros((7, win), F32)])
        nw = 9 * half

        def reduce_body(rels, s, *refs):
            n = len(rels)
            w_ref, outs, scr = refs[n], refs[n + 1 : n + 1 + n], refs[-1]
            wh, wl = split2(w_ref[...])
            for k, r in enumerate(rels):
                x = padded(refs[k], scr, mask_of(s[NV + r], R, win, edge))
                xh, xl = split2(x)
                outs[k][...] = mm3(xh, xl, wh, wl)

        def reduce_call(rels):
            return call(
                functools.partial(reduce_body, rels),
                [features_in] * len(rels) + [reduce_weight],
                [((R, mid), F32)] * len(rels),
                [pltpu.VMEM((own * edge, PAD, win), F32)],
                isc,
                {k: quarter_spec(r) for k, r in enumerate(rels)},
                flops=6 * R * win * mid * len(rels),
            )

        p3, p1 = reduce_call((3, 1))
        p2, p0 = reduce_call((2, 0))
        y1 = p1 + swap(p3, "chan", 1)
        ys = swap(y1, "chan", 2)
        rc = swap(p2, "chan", 1)

        def red_body(s, a, b, y, red, sums):
            v = a[...] + b[...] + y[...]
            red[...] = v
            sums[0:1] = colsum(v)
            sums[1:2] = colsum(v * v)

        red, s1 = call(red_body, [p0, rc, ys], [((R, mid), F32), ((2, mid), F32)], scalars=isc)
        s1 = sum_all(s1)

        def gather3(x):
            y = swap(x, "chan", 2)
            return [x, y, swap(x, "chan", 1), swap(y, "chan", 1)]

        pa, _ = lax.optimization_barrier((pa, y1))
        pa_all = gather3(pa)

        def pa_body(s, p0, p1, p2, p3, wh, wl, wat, vec, wsq, scr):
            c = s[0]
            scr[c] = p0[...]
            scr[c ^ 2] = p1[...]
            scr[c ^ 1] = p2[...]
            scr[c ^ 3] = p3[...]

            def wide(lo, n):
                lane = lax.broadcasted_iota(jnp.int32, (n, 2 * lw), 1)
                out = [[], []]
                for pair in range(nc // 2):
                    a, b = scr[2 * pair, lo : lo + n, :], scr[2 * pair + 1, lo : lo + n, :]
                    out[0].append(jnp.where(lane < lw, a, pltpu.roll(b, lw, 1)))
                    out[1].append(jnp.where(lane < lw, pltpu.roll(a, lw, 1), b))
                return [jnp.concatenate(o, axis=1) for o in out]

            for t in range(9):
                for r, z in enumerate(wide(t * half, half)):
                    h, low = split2(z)
                    wh[r, t * half : (t + 1) * half, :] = h
                    wl[r, t * half : (t + 1) * half, :] = low
            for r, z in enumerate(wide(nw, inner)):
                wat[r] = z
            for r, z in enumerate(wide(nw + inner, 8)):
                vec[r] = z
            for k in range(nc):
                wsq[k * lw : (k + 1) * lw, :] = scr[k, nw + inner + 8 :, :]

        wh, wl, wat, vec, wsq = call(
            pa_body,
            pa_all,
            [
                ((2, nw, mid), BF16),
                ((2, nw, mid), BF16),
                ((2, inner, mid), F32),
                ((2, 8, mid), F32),
                ((mid, inner), F32),
            ],
            [pltpu.VMEM((nc,) + pa.shape, F32)],
            isc,
        )

        def taps_in(z, scrs, n):
            w = z.shape[1]
            rows = n * span
            for v in range(3):
                zz = z if v == 1 else pltpu.roll(z, 1 if v == 0 else rows - 1, 0)
                parts = split2(zz) if len(scrs) == 2 else [zz.astype(BF16)]
                for scr, part in zip(scrs, parts):
                    scr[v, :, 0] = jnp.zeros((n, PAD, w), BF16)
                    scr[v, :, edge + 1] = jnp.zeros((n, PAD, w), BF16)
                    scr[v, :, 1 : edge + 1] = part.reshape(n, edge, PAD, w)

        def conv_body(s, red, sums, fs, vec, wh, wl, out, sums2, zh, zl):
            avg, inv = stats(sums, fs)
            mask = mask_of(s[NV], R, mid, edge)
            z = jnp.maximum((red[...] - avg) * inv * vec[0, 3:4] + vec[1, 3:4], 0.0)
            z = jnp.where(mask, z, 0.0)
            taps_in(z, (zh, zl), own)
            for r in range(2):
                cols = slice(r * half, (r + 1) * half)
                hi = jnp.concatenate([zh[v, :, u : u + edge, :, cols].reshape(R, half) for u, v in TAPS], axis=1)
                lo = jnp.concatenate([zl[v, :, u : u + edge, :, cols].reshape(R, half) for u, v in TAPS], axis=1)
                y = mm3(hi, lo, wh[r], wl[r])
                out[:, r * mid : (r + 1) * mid] = y
                y = jnp.where(mask, y, 0.0)
                sums2[0:1, r * mid : (r + 1) * mid] = colsum(y)
                sums2[1:2, r * mid : (r + 1) * mid] = colsum(y * y)

        spl, s2 = call(
            conv_body,
            [red, s1, fsc, vec, wh, wl],
            [((R, 2 * mid), F32), ((2, 2 * mid), F32)],
            [pltpu.VMEM((3, own, PAD, PAD, mid), BF16)] * 2,
            isc,
            flops=12 * R * nw * mid,
        )
        red_r = gather3(lax.optimization_barrier((red, spl))[0])
        s2 = sum_all(s2)

        def second(spl, sums, fs, vec, r, mask):
            cols = slice(r * mid, (r + 1) * mid)
            avg = sums[0:1, cols] * fs[0:1, 0:1]
            inv = lax.rsqrt(sums[1:2, cols] * fs[0:1, 0:1] - avg * avg + EPSILON)
            norm = (spl[:, cols] - avg) * inv
            act = norm * vec[r, 0:1] + vec[r, 1:2]
            return norm, act, (act > 0) & mask, inv

        def per_image(z):
            return [colsum(z[b * span : (b + 1) * span]) for b in range(own)]

        def pool_body(s, spl, sums, fs, vec, wsq, c12, sq, sfc):
            mask = mask_of(s[NV], R, mid, edge)
            pooled = [0.0] * own
            nb = mid // 128
            for r in range(2):
                norm, act, on, _ = second(spl, sums, fs, vec, r, mask)
                c1 = per_image(jnp.where(on, 1.0, 0.0))
                c2 = per_image(jnp.where(on, norm, 0.0))
                for b in range(own):
                    for i in range(nb):
                        sl = slice(i * 128, (i + 1) * 128)
                        c12[b, r * nb + i : r * nb + i + 1, :] = c1[b][:, sl]
                        c12[b, (2 + r) * nb + i : (2 + r) * nb + i + 1, :] = c2[b][:, sl]
                    pooled[b] = pooled[b] + vec[r, 0:1] * c2[b] + vec[r, 1:2] * c1[b]
            p = jnp.concatenate(pooled + [jnp.zeros((8 - own, mid), F32)], axis=0) * (1.0 / area)
            v = exact(p, wsq[...])
            sq[...] = v
            live = lax.broadcasted_iota(jnp.int32, (8, inner), 0) < s[NV]
            v = jnp.where(live, v, 0.0)
            sfc[0:1] = colsum(v)
            sfc[1:2] = colsum(v * v)

        c12, sq, sfc = call(
            pool_body,
            [spl, s2, fsc, vec, wsq],
            [((own, 4 * mid // 128, 128), F32), ((8, inner), F32), ((2, inner), F32)],
            scalars=isc,
        )
        sfc = sum_all(sfc)
        ids = order_all()
        first_row = (ids // nc) * slots + quarter_of(ids % nc) * own
        c12_rel = gather_all(lax.optimization_barrier((c12, sfc))[0])
        sgb = jnp.stack([squeeze_gain, squeeze_shift])

        pb_all = gather3(lax.optimization_barrier((pb, s2))[0])

        def pb_body(s, p0, p1, p2, p3, wh, wl, g3):
            c = s[0]
            row = lax.broadcasted_iota(jnp.int32, (8, win), 0)
            g = jnp.zeros((8, win), F32)
            for k, p in ((0, p0), (2, p1), (1, p2), (3, p3)):
                h, low = split2(p[0:mid])
                wh[c ^ k] = h
                wl[c ^ k] = low
                g = jnp.where(row == (c ^ k), p[mid : mid + 1], g)
            g3[...] = g

        weh, wel, g3 = call(
            pb_body,
            pb_all,
            [((nc, mid, win), BF16), ((nc, mid, win), BF16), ((8, win), F32)],
            scalars=isc,
        )

        def squeeze_norm(sq, sums, fs, sgb):
            avg = sums[0:1] * fs[1:2, 0:1]
            inv = lax.rsqrt(sums[1:2] * fs[1:2, 0:1] - avg * avg + EPSILON)
            norm = (sq - avg) * inv
            return norm, norm * sgb[0:1] + sgb[1:2], inv

        def attend_body(s, spl, sums, fs, vec, sfc, sq, sgb, wat, att, wts):
            mask = mask_of(s[NV], R, mid, edge)
            _, actf, _ = squeeze_norm(sq[...], sfc, fs, sgb)
            hidden = jnp.maximum(actf, 0.0)
            lg = [exact(hidden, wat[r]) + vec[r, 2:3] for r in range(2)]
            top = jnp.maximum(lg[0], lg[1])
            e = [jnp.exp(z - top) for z in lg]
            total = e[0] + e[1]
            acc = 0.0
            imgs = lax.broadcasted_iota(jnp.int32, (R, mid), 0)
            for r in range(2):
                w = e[r] / total
                wts[r] = w
                _, act, on, _ = second(spl, sums, fs, vec, r, mask)
                wrow = w[0:1]
                for b in range(1, own):
                    wrow = jnp.where(imgs >= b * span, w[b : b + 1], wrow)
                acc = acc + jnp.where(on, act * wrow, 0.0)
            att[...] = acc

        att, wts = call(
            attend_body,
            [spl, s2, fsc, vec, sfc, sq, sgb, wat],
            [((R, mid), F32), ((2, 8, mid), F32)],
            scalars=isc,
        )
        att_r = gather3(att)

        def own_expand_body(s, att, wh, wl, sums):
            ah, al = split2(att[...])
            for k in range(nc):
                y = mm3(ah, al, wh[k], wl[k])
                sums[2 * k : 2 * k + 1] = colsum(y)
                sums[2 * k + 1 : 2 * k + 2] = colsum(y * y)

        (s3,) = call(
            own_expand_body, [att, weh, wel], [((2 * nc, win), F32)], scalars=isc, flops=6 * R * mid * win * nc
        )
        s3 = sum_all(s3)
        s3l = lax.dynamic_slice_in_dim(s3, 2 * c, 2, 0)
        eg = jnp.stack([expand_gain, expand_shift])

        def expand_body(rels, s, *refs):
            n = len(rels)
            atts, xs, gs = refs[:n], refs[n : 2 * n], refs[2 * n : 3 * n]
            w_ref, sums, fs, eg = refs[3 * n : 3 * n + 4]
            bos, gas = refs[3 * n + 4 : 4 * n + 4], refs[4 * n + 4 : 5 * n + 4]
            sg, t1, t2, u1 = refs[5 * n + 4 : 5 * n + 8]
            scr = refs[-1]
            avg, inv = stats(sums, fs)
            wh, wl = split2(w_ref[...])
            sg_acc, t1_acc, t2_acc, u_acc = [0.0, 0.0], 0.0, 0.0, 0.0
            for k, r in enumerate(rels):
                mask = mask_of(s[NV + r], R, win, edge)
                a = atts[k][...]
                ah, al = split2(a)
                norm = (mm3(ah, al, wh, wl) - avg) * inv
                x = padded(xs[k], scr, mask)
                pre = norm * eg[0:1] + eg[1:2] + x
                on = (pre > 0) & mask
                out = jnp.where(on, pre, 0.0)
                scr[...] = out.reshape(own * edge, PAD, win)
                bos[k][...] = scr[:, :edge, :].reshape(own, edge, edge, win)
                g = padded(gs[k], scr, on)
                sg_acc[0] += colsum(g)
                sg_acc[1] += colsum(g * norm)
                gb = g.astype(BF16)
                nb = jnp.where(mask, norm, 0.0).astype(BF16)
                gas[k][...] = mm((g * (eg[0:1] * inv)).astype(BF16), wh, ((1,), (1,)))
                t1_acc += mm(ah, gb, ((0,), (0,)))
                t2_acc += mm(ah, nb, ((0,), (0,)))
                u_acc += colsum(a)
            row = lax.broadcasted_iota(jnp.int32, (2 * nc, win), 0)
            z = jnp.where(row == 2 * s[0], sg_acc[0], 0.0)
            sg[...] = jnp.where(row == 2 * s[0] + 1, sg_acc[1], z)
            t1[...] = t1_acc
            t2[...] = t2_acc
            u1[...] = u_acc

        def expand_call(rels):
            n = len(rels)
            specs = {n + k: quarter_spec(r) for k, r in enumerate(rels)}
            specs.update({2 * n + k: quarter_spec(r) for k, r in enumerate(rels)})
            return call(
                functools.partial(expand_body, rels),
                [att_r[r] for r in rels] + [features_in] * n + [grad_out] * n + [expand_weight, s3l, fsc, eg],
                [((own, edge, edge, win), F32)] * n
                + [((R, mid), F32)] * n
                + [((2 * nc, win), F32), ((mid, win), F32), ((mid, win), F32), ((1, mid), F32)],
                [pltpu.VMEM((own * edge, PAD, win), F32)],
                isc,
                specs,
                flops=12 * R * mid * win * n,
            )

        bo3, bo1, ga3, ga1, sga, t1a, t2a, ua = expand_call((3, 1))
        bo2, bo0, ga2, ga0, sgb3, t1b, t2b, ub = expand_call((2, 0))
        gy1 = ga1 + swap(ga3, "chan", 1)
        gys = swap(gy1, "chan", 2)
        grc = swap(ga2, "chan", 1)
        sg3 = sum_all(sga + sgb3)
        bos = [bo0, bo1, bo2, bo3]
        sg3l = lax.dynamic_slice_in_dim(sg3, 2 * c, 2, 0)

        def dwe_body(s, t1a, t1b, t2a, t2b, ua, ub, sums, sg, fs, eg, out):
            avg, inv = stats(sums, fs)
            u = ua[...] + ub[...]
            outer = exact(u, sg[0:1], ((0,), (0,)))
            out[...] = (eg[0:1] * inv) * (
                t1a[...] + t1b[...] - (outer + (t2a[...] + t2b[...]) * sg[1:2]) * fs[0:1, 0:1]
            )

        def gatt_body(s, p, rc, ys, att, weh, g3, sums, sg, spl, sums2, fs, vec, wts, sfc, sq, sgb, wat, ga, gl, merged):
            m_acc, v_acc = 0.0, 0.0
            for k in range(nc):
                avg = sums[2 * k : 2 * k + 1] * fs[0:1, 0:1]
                inv = lax.rsqrt(sums[2 * k + 1 : 2 * k + 2] * fs[0:1, 0:1] - avg * avg + EPSILON)
                sc = g3[k : k + 1] * inv * fs[0:1, 0:1]
                kap = sg[2 * k + 1 : 2 * k + 2] * inv * sc
                w = weh[k]
                m_acc += mm((w.astype(F32) * kap).astype(BF16), w, ((1,), (1,)))
                vv = sg[2 * k : 2 * k + 1] * sc - avg * kap
                v_acc += exact(vv, w.astype(F32), ((1,), (1,)))
            mask = mask_of(s[NV], R, mid, edge)
            g = p[...] + rc[...] + ys[...] - mm(att[...].astype(BF16), m_acc.astype(BF16)) - v_acc
            g = jnp.where(mask, g, 0.0)
            ga[...] = g
            gw, a12 = [], []
            for r in range(2):
                norm, act, on, _ = second(spl, sums2, fs, vec, r, mask)
                gon = jnp.where(on, g, 0.0)
                a1, a2 = per_image(gon), per_image(gon * norm)
                zero = [jnp.zeros((8 - own, mid), F32)]
                a1, a2 = jnp.concatenate(a1 + zero, axis=0), jnp.concatenate(a2 + zero, axis=0)
                a12.append((a1, a2))
                gw.append(vec[r, 0:1] * a2 + vec[r, 1:2] * a1)
            mean = wts[0] * gw[0] + wts[1] * gw[1]
            gh = 0.0
            nb = mid // 128
            parts = []
            for r in range(2):
                z = wts[r] * (gw[r] - mean)
                for b in range(own):
                    for i in range(nb):
                        k = (b * 2 + r) * nb + i
                        gl[k : k + 1, :] = z[b : b + 1, i * 128 : (i + 1) * 128]
                gh = gh + exact(z, wat[r], ((1,), (1,)))
                for j in range(2):
                    parts.append(colsum(wts[r] * a12[r][j]))
            _, actf, _ = squeeze_norm(sq[...], sfc, fs, sgb)
            dzf = jnp.where(actf > 0, gh, 0.0)
            row = lax.broadcasted_iota(jnp.int32, (ni, inner), 0)
            z = jnp.zeros((ni, inner), F32)
            for b in range(own):
                z = jnp.where(row == s[G0] + b, dzf[b : b + 1], z)
            merged[0:ni] = z
            for k, pz in enumerate(parts):
                for i in range(nb):
                    merged[ni + k * nb + i : ni + k * nb + i + 1] = pz[:, i * 128 : (i + 1) * 128]

        nb = mid // 128
        ga, gl, merged = call(
            gatt_body,
            [ga0, grc, gys, att, weh, g3, s3, sg3, spl, s2, fsc, vec, wts, sfc, sq, sgb, wat],
            [((R, mid), F32), ((own * 2 * nb, 128), F32), ((ni + 4 * nb, inner), F32)],
            scalars=isc,
            flops=2 * R * mid * mid + 2 * nc * mid * mid * win,
        )
        merged = sum_all(merged)
        gl_rel = gather_all(lax.optimization_barrier((gl, merged))[0])

        osc = jnp.concatenate([isc, first_row.astype(jnp.int32)])
        ID0 = isc.shape[0]

        def all_body(s, c12r, vec, wsq, sfc, fs, sgb, c1_ref, c2_ref, pool_ref, norm_ref, hid_ref, scr):
            def place(j, _):
                for b in range(own):
                    scr[s[ID0 + j] + b] = c12r[j * own + b]
                return 0

            lax.fori_loop(0, nd * nc, place, 0)
            v = scr[...]
            pooled = 0.0
            for r in range(2):
                c1 = jnp.concatenate([v[:, r * nb + i, :] for i in range(nb)], axis=1)
                c2 = jnp.concatenate([v[:, (2 + r) * nb + i, :] for i in range(nb)], axis=1)
                c1_ref[r] = c1
                c2_ref[r] = c2
                pooled = pooled + vec[r, 0:1] * c2 + vec[r, 1:2] * c1
            pooled = pooled * (1.0 / area)
            pool_ref[...] = pooled
            norm, actf, _ = squeeze_norm(exact(pooled, wsq[...]), sfc, fs, sgb)
            norm_ref[...] = norm
            hid_ref[...] = jnp.maximum(actf, 0.0)

        c1_all, c2_all, pool_all, normf_all, hid_all = call(
            all_body,
            [c12_rel, vec, wsq, sfc, fsc, sgb],
            [
                ((2, ni, mid), F32),
                ((2, ni, mid), F32),
                ((ni, mid), F32),
                ((ni, inner), F32),
                ((ni, inner), F32),
            ],
            [pltpu.VMEM((ni, 4 * nb, 128), F32)],
            osc,
        )
        slot = jnp.arange(slots)
        amask = (slot[None] < image_counts[:, None]).astype(F32).reshape(ni, 1)
        amask = jnp.broadcast_to(amask, (ni, inner))

        def back_body(
            s, merged, c1a, c2a, normf, amask, sfc, fs, sgb, wsq, ga, spl, sums2, vec, wts, red, sums1, wh,
            dz1, sg1, b0, b1, b2, b3, gq_ref, sg2, gfc, zh, blk,
        ):
            dzf = merged[0:ni]
            norm_all = normf[...]
            s_f = colsum(dzf)
            g_f = colsum(dzf * norm_all)
            gfc[0:1] = g_f
            gfc[1:2] = s_f
            avg = sfc[0:1] * fs[1:2, 0:1]
            inv = lax.rsqrt(sfc[1:2] * fs[1:2, 0:1] - avg * avg + EPSILON)
            gq = sgb[0:1] * inv * (dzf - amask[...] * (s_f + norm_all * g_f) * fs[1:2, 0:1])
            gq_ref[...] = gq
            gp = exact(gq, wsq[...], ((1,), (1,))) * (1.0 / area)
            mask = mask_of(s[NV], R, mid, edge)
            imgs = lax.broadcasted_iota(jnp.int32, (R, mid), 0)
            grow = lax.broadcasted_iota(jnp.int32, (ni, mid), 0)
            gpo = [colsum(jnp.where(grow == s[G0] + b, gp, 0.0)) for b in range(own)]
            gprow = gpo[0]
            for b in range(1, own):
                gprow = jnp.where(imgs >= b * span, gpo[b], gprow)
            lane = lax.broadcasted_iota(jnp.int32, (R, 2 * lw), 1)
            gss = []
            acts = []
            for r in range(2):
                def piece(j):
                    k = (r * 2 + j) * nb
                    return jnp.concatenate([merged[ni + k + i : ni + k + i + 1] for i in range(nb)], axis=1)

                s2v = piece(0) + colsum(gp * c1a[r])
                g2v = piece(1) + colsum(gp * c2a[r])
                sg2[0, r : r + 1] = s2v
                sg2[1, r : r + 1] = g2v
                norm, act, on, inv2 = second(spl, sums2, fs, vec, r, mask)
                w = wts[r]
                wrow = w[0:1]
                for b in range(1, own):
                    wrow = jnp.where(imgs >= b * span, w[b : b + 1], wrow)
                dz = jnp.where(on, wrow * ga[...] + gprow, 0.0)
                gs = vec[r, 0:1] * inv2 * (dz - (s2v + norm * g2v) * fs[0:1, 0:1])
                gs = jnp.where(mask, gs, 0.0)
                gss.append(gs)
            for pair in range(nc // 2):
                cols = slice(pair * 2 * lw, (pair + 1) * 2 * lw)
                a, b = gss[0][:, cols], gss[1][:, cols]
                blk[2 * pair] = jnp.where(lane < lw, a, pltpu.roll(b, lw, 1))
                blk[2 * pair + 1] = jnp.where(lane < lw, pltpu.roll(a, lw, 1), b)
            for k, o in enumerate((b0, b1, b2, b3)):
                o[...] = blk[s[0] ^ k]
            avg1, inv1 = stats(sums1, fs)
            norm1 = (red[...] - avg1) * inv1
            on1 = (norm1 * vec[0, 3:4] + vec[1, 3:4] > 0) & mask
            for r in range(2):
                taps_in(gss[r], (zh,), own)
                acc = 0.0
                for t, (u, v) in enumerate(TAPS):
                    z = zh[2 - v, :, 2 - u : 2 - u + edge].reshape(R, mid)
                    acc += mm(z, wh[r, t * half : (t + 1) * half, :], ((1,), (1,)))
                cols = slice(r * half, (r + 1) * half)
                acc = jnp.where(on1[:, cols], acc, 0.0)
                dz1[:, cols] = acc
                sg1[0:1, cols] = colsum(acc)
                sg1[1:2, cols] = colsum(acc * norm1[:, cols])

        dz1, sg1, blk0, blk1, blk2, blk3, gq, sg2, gfc = call(
            back_body,
            [merged, c1_all, c2_all, normf_all, amask, sfc, fsc, sgb, wsq, ga, spl, s2, vec, wts, red, s1, wh],
            [((R, mid), F32), ((2, mid), F32)]
            + [((R, 2 * lw), F32)] * 4
            + [((ni, inner), F32), ((2, 2, mid), F32), ((2, inner), F32)],
            [pltpu.VMEM((3, own, PAD, PAD, mid), BF16), pltpu.VMEM((nc, R, 2 * lw), F32)],
            isc,
            flops=4 * R * nw * mid,
        )
        dz1_r = gather3(dz1)
        sg1 = sum_all(sg1)

        def final_grad(dz, red, sums, sg, fs, vec, mask):
            avg, inv = stats(sums, fs)
            norm = (red - avg) * inv
            g = vec[0, 3:4] * inv * (dz - (sg[0:1] + norm * sg[1:2]) * fs[0:1, 0:1])
            return jnp.where(mask, g, 0.0).astype(BF16)

        def dwr_body(s, d0, d1, d2, d3, r0, r1, r2, r3, x0, x1, x2, x3, sums, sg, fs, vec, out, go0, go1, go2, go3, scr):
            acc = 0.0
            for r, (dz, rd, x, go) in enumerate(
                ((d0, r0, x0, go0), (d1, r1, x1, go1), (d2, r2, x2, go2), (d3, r3, x3, go3))
            ):
                mask = mask_of(s[NV + r], R, win, edge)
                g = final_grad(dz[...], rd[...], sums, sg, fs, vec, mask)
                go[...] = g
                x = padded(x, scr, mask).astype(BF16)
                acc += mm(x, g, ((0,), (0,)))
            out[...] = acc

        dwr, gr0, gr1, gr2, gr3 = call(
            dwr_body,
            dz1_r + red_r + [features_in] * 4 + [s1, sg1, fsc, vec],
            [((win, mid), F32)] + [((R, mid), BF16)] * 4,
            [pltpu.VMEM((own * edge, PAD, win), F32)],
            isc,
            {8 + r: quarter_spec(r) for r in range(4)},
            flops=8 * R * win * mid,
        )
        grad_reduce_weight = big_sum_dp(dwr)

        def gin_body(s, g0, g1, g2, g3, bo0, bo1, bo2, bo3, go, w_ref, out_bo, out_gi, scr):
            w = w_ref[...].astype(BF16)
            for r, (g, bo) in enumerate(((g0, bo0), (g1, bo1), (g2, bo2), (g3, bo3))):
                z = mm(g[...], w, ((1,), (1,)))
                scr[...] = z.reshape(own * edge, PAD, win)
                z = scr[:, :edge, :].reshape(own, edge, edge, win)
                at = pl.ds((s[1] ^ r) * own, own)
                out_bo[at] = bo[...]
                out_gi[at] = z + jnp.where(bo[...] > 0, go[at], 0.0)

        block_out, grad_input = call(
            gin_body,
            [gr0, gr1, gr2, gr3] + bos + [grad_out, reduce_weight],
            [(features_in.shape, F32)] * 2,
            [pltpu.VMEM((own * edge, PAD, win), F32)],
            isc,
            flops=8 * R * win * mid,
        )

        blks = [blk0, swap(blk1, "chan", 1), swap(blk2, "chan", 2), swap(blk3, "chan", 3)]

        def dws_body(s, k0, k1, k2, k3, r0, r1, r2, r3, sums, fs, vec, out, zg, relu):
            avg, inv = stats(sums, fs)
            for k, (bk, rd, r) in enumerate(((k0, r0, 0), (k1, r2, 2), (k2, r1, 1), (k3, r3, 3))):
                mask = mask_of(s[NV + r], R, mid, edge)
                z = jnp.maximum((rd[...] - avg) * inv * vec[0, 3:4] + vec[1, 3:4], 0.0)
                relu[k * R : (k + 1) * R, :] = jnp.where(mask, z, 0.0).astype(BF16)
                taps_in(bk[...], (zg.at[:, k * own : (k + 1) * own],), own)
            rl = relu[...]
            lane = lax.broadcasted_iota(jnp.int32, (half, 2 * lw), 1)
            for t, (u, v) in enumerate(TAPS):
                z = zg[2 - v, :, 2 - u : 2 - u + edge].reshape(nc * R, 2 * lw)
                y = mm(rl, z, ((0,), (0,)))
                out[t * half : (t + 1) * half, :] = jnp.where(lane < lw, y[:half], y[half:])

        (dws,) = call(
            dws_body,
            blks + red_r + [s1, fsc, vec],
            [((nw, 2 * lw), F32)],
            [pltpu.VMEM((3, slots, PAD, PAD, 2 * lw), BF16), pltpu.VMEM((nc * R, mid), BF16)],
            isc,
            flops=2 * nc * R * mid * 9 * 2 * lw,
        )
        grad_split_weight = big_sum_dp(dws).reshape(split_weight.shape)

        (dwe,) = call(
            dwe_body,
            [t1a, t1b, t2a, t2b, ua, ub, s3l, sg3l, fsc, eg],
            [((mid, win), F32)],
            scalars=isc,
        )
        grad_expand_weight = big_sum_dp(dwe)

        def fc_body(s, glr, hid, pool, gq, waw, wab, wsw, scr):
            n = 2 * nb

            def place(j, _):
                for b in range(own):
                    scr[s[ID0 + j] + b] = glr[j * own + b]
                return 0

            lax.fori_loop(0, nd * nc, place, 0)
            v = scr[...]
            for r in range(2):
                z = jnp.concatenate([v[:, r * nb + i, :] for i in range(nb)], axis=1)
                wab[r : r + 1] = colsum(z)
                waw[r] = exact(hid[...], z, ((0,), (0,)))
            wsw[...] = exact(pool[...], gq[...], ((0,), (0,)))

        waw, wab, wsw = call(
            fc_body,
            [gl_rel.reshape(ni, 2 * nb, 128), hid_all, pool_all, gq],
            [((2, inner, mid), F32), ((2, mid), F32), ((mid, inner), F32)],
            [pltpu.VMEM((ni, 2 * nb, 128), F32)],
            osc,
        )

        def own_lanes(z, axis):
            return lax.dynamic_slice_in_dim(z, c * lw, lw, axis)

        return (
            block_out,
            grad_input,
            grad_reduce_weight,
            own_lanes(sg1[1], 0),
            own_lanes(sg1[0], 0),
            grad_split_weight,
            own_lanes(sg2[1], 1),
            own_lanes(sg2[0], 1),
            own_lanes(wsw, 0),
            gfc[0],
            gfc[1],
            own_lanes(waw, 2).transpose(1, 0, 2),
            own_lanes(wab, 1),
            grad_expand_weight,
            sg3l[1],
            sg3l[0],
        )

    return per_device


def solution(mesh):
    in_specs = (
        P("dp", None, None, "chan"),
        P(),
        P("chan", None),
        P("chan"),
        P("chan"),
        P(None, None, None, None, "chan"),
        P(None, "chan"),
        P(None, "chan"),
        P("chan", None),
        P(),
        P(),
        P(None, None, "chan"),
        P(None, "chan"),
        P(None, "chan"),
        P("chan"),
        P("chan"),
        P("dp", None, None, "chan"),
    )
    out_specs = (
        P("dp", None, None, "chan"),
        P("dp", None, None, "chan"),
        P("chan", None),
        P("chan"),
        P("chan"),
        P(None, None, None, None, "chan"),
        P(None, "chan"),
        P(None, "chan"),
        P("chan", None),
        P(),
        P(),
        P(None, None, "chan"),
        P(None, "chan"),
        P(None, "chan"),
        P("chan"),
        P("chan"),
    )
    return jax.shard_map(
        build(mesh), mesh=mesh, in_specs=in_specs, out_specs=out_specs, check_vma=False
    )
```

profile of v0, /device:TPU:0, one launch (start us, length us, event | category | flops | bytes accessed | tf_op | source)
XLA Modules:
  0.0 360.4 jit_solution(1824187493637696298)
XLA Ops:
  4.5 2.0 copy.56.refs_0_.refs_1_.refs_2_.refs_3_.x0.x1.x2.x3
  11.0 2.8 reshape.89
  14.2 2.1 concatenate.52.p0
  17.4 2.6 collective-permute-start.8
  20.3 16.0 %collective-permute-done.8.p1 = f32[1352,128]{1,0:T(8,128)S(1)} collective-permute-done((f32[1352,128]{1,0:T(8,128)S(1)}, f32[1352,128]{1,0:T(8,128)S(1)}, u32[]{:S(2)}, u32[]{:S(2)}) %collective-permute-start.8) | collective-permute-done | bytes 692256 | tf_op jit(solution)/shard_map/ppermute | solution.py:92
  39.7 10.8 %collective-permute-done.2.y = f32[448,256]{1,0:T(8,128)S(1)} collective-permute-done((f32[448,256]{1,0:T(8,128)S(1)}, f32[448,256]{1,0:T(8,128)S(1)}, u32[]{:S(2)}, u32[]{:S(2)}) %collective-permute-start.2) | collective-permute-done | bytes 458784 | tf_op jit(solution)/shard_map/ppermute | solution.py:92
  53.0 2.6 collective-permute-start.4
  66.0 2.8 shard_map.300
  68.9 2.8 shard_map.301
  73.0 2.6 collective-permute-start.12
  87.7 6.9 %collective-permute-done.22.p1 = f32[264,256]{1,0:T(8,128)S(1)} collective-permute-done((f32[264,256]{1,0:T(8,128)S(1)}, f32[264,256]{1,0:T(8,128)S(1)}, u32[]{:S(2)}, u32[]{:S(2)}) %collective-permute-start.22) | collective-permute-done | bytes 270368 | tf_op jit(solution)/shard_map/ppermute | solution.py:92
  97.4 2.6 collective-permute-start.17
  114.5 2.5 shard_map.305
  119.0 2.4 collective-permute-start.26
  121.4 3.2 copy.65.refs_4_.refs_5_.go
  131.9 2.1 collective-permute-start.29
  134.0 3.2 collective-permute-done.29
  138.7 3.6 %shard_map.306 = (f32[2,14,14,256]{3,2,1,0:T(8,128)S(1)}, f32[2,14,14,256]{3,2,1,0:T(8,128)S(1)}, f32[448,256]{1,0:T(8,128)S(1)}, f32[448,256]{1,0:T(8,128)S(1)}...) custom-call(s32[7]{0:T(128)S(1)} %stack.65.s, ...), custom_call_target="tpu_custom_call" | custom-call | flops 704643072 | bytes 9862144 | tf_op jit(solution)/shard_map/pallas_call | solution.py:53
  145.6 3.5 shard_map.307
  152.1 3.2 collective-permute-done.36
  159.3 2.2 collective-permute-done.38
  162.4 2.2 collective-permute-done.39
  168.1 2.3 collective-permute-start.101
  170.3 2.2 collective-permute-start.102
  174.0 2.1 collective-permute-start.103
  177.0 2.6 collective-permute-start.99
  189.7 3.8 %collective-permute-done.105 = f32[32,256]{1,0:T(8,128)S(1)} collective-permute-done((f32[32,256]{1,0:T(8,128)S(1)}, f32[32,256]{1,0:T(8,128)S(1)}, u32[]{:S(2)}, u32[]{:S(2)}) %collective-permute-start.105) | collective-permute-done | bytes 32800 | tf_op jit(solution)/shard_map/ppermute | solution.py:92
  194.0 3.3 collective-permute-start.107
  197.3 3.2 collective-permute-done.34.ys
  202.5 3.8 %shard_map.308 = (f32[448,256]{1,0:T(8,128)S(1)}, f32[8,128]{1,0:T(8,128)S(1)}, f32[72,128]{1,0:T(8,128)S(1)}) custom-call(s32[7]{0:T(128)S(1)} %stack.65.s, f32[448,256]{1,0:T(8,128)S(1)} %copy-done.26, f32[448,256]{1,0:T(8,128)S(1)} %collective-permute-done.30.rc, f32[448,256]{1,0:T(8,128)S(1)} %collective-permute-done.34.ys, ...), custom_call_target="tpu_custom_call" | custom-call | flops 192937984 | bytes 4108288 | tf_op jit(solution)/shard_map/pallas_call | solution.py:53
  210.6 4.3 %collective-permute-done.41 = f32[72,128]{1,0:T(8,128)S(1)} collective-permute-done((f32[72,128]{1,0:T(8,128)S(1)}, f32[72,128]{1,0:T(8,128)S(1)}, u32[]{:S(2)}, u32[]{:S(2)}) %collective-permute-start.41) | collective-permute-done | bytes 36896 | tf_op jit(solution)/shard_map/ppermute | solution.py:92
  214.9 2.5 collective-permute-start.110
  217.5 4.1 %collective-permute-done.42 = f32[72,128]{1,0:T(8,128)S(1)} collective-permute-done((f32[72,128]{1,0:T(8,128)S(1)}, f32[72,128]{1,0:T(8,128)S(1)}, u32[]{:S(2)}, u32[]{:S(2)}) %collective-permute-start.42) | collective-permute-done | bytes 36896 | tf_op jit(solution)/shard_map/ppermute | solution.py:92
  222.3 2.8 collective-permute-done.43
  226.3 2.3 collective-permute-done.44
  228.7 2.7 shard_map.310
  233.0 2.6 collective-permute-start.57
  237.0 2.0 collective-permute-start.58
  241.1 2.2 collective-permute-done.59
  245.1 2.6 collective-permute-done.94
  248.2 2.9 collective-permute-done.95
  256.5 4.1 %collective-permute-done.76.k2 = f32[448,128]{1,0:T(8,128)S(1)} collective-permute-done((f32[448,128]{1,0:T(8,128)S(1)}, f32[448,128]{1,0:T(8,128)S(1)}, u32[]{:S(2)}, u32[]{:S(2)}) %collective-permute-start.76) | collective-permute-done | bytes 229408 | tf_op jit(solution)/shard_map/ppermute | solution.py:92
  260.6 3.4 collective-permute-done.77.k3
  263.9 4.5 %shard_map.313 = f32[1152,128]{1,0:T(8,128)S(1)} custom-call(s32[7]{0:T(128)S(1)} %stack.65.s, f32[448,128]{1,0:T(8,128)S(1)} %get-tuple-element.134.k0, f32[448,128]{1,0:T(8,128)S(1)} %collective-permute-done.75.k1, f32[448,128]{1,0:T(8,128)S(1)} %collective-permute-done.76.k2, f32[448,128]{1,0:T(8,128)S(1)} %collective-permute-done.77.k3, ...), custom_call_target="tpu_custom_call" | custom-call | flops 1056964608 | bytes 3362816 | tf_op jit(solution)/shard_map/pallas_call | solution.py:53
  273.7 2.5 collective-permute-start.81
  276.8 2.2 collective-permute-start.83
  279.0 2.4 collective-permute-start.84
  283.2 2.8 collective-permute-done.81
  292.2 3.1 collective-permute-start.86
  295.5 3.0 collective-permute-start.88
  304.5 2.7 shard_map.311
  312.4 2.6 collective-permute-start.65
  316.9 2.2 collective-permute-start.67
  319.7 2.5 collective-permute-start.91
  324.7 2.1 collective-permute-done.91
  327.5 2.9 reshape_reshape.3
  330.4 3.1 copy.78
  339.7 2.4 copy.76
  342.0 2.4 copy.77
  344.4 2.7 collective-permute-start.70
  347.5 2.7 collective-permute-start.72
  350.2 2.1 collective-permute-start.73
  353.1 2.4 collective-permute-start.74
  356.0 3.7 %collective-permute-done.74 = f32[32,256]{1,0:T(8,128)S(1)} collective-permute-done((f32[32,256]{1,0:T(8,128)S(1)}, f32[32,256]{1,0:T(8,128)S(1)}, u32[]{:S(2)}, u32[]{:S(2)}) %collective-permute-start.74) | collective-permute-done | bytes 32800 | tf_op jit(solution)/shard_map/ppermute | solution.py:92
  (457 shorter events, 151.9 us)
Async XLA Ops:
  8.6 7.7 %collective-permute-start.1 = (f32[448,256]{1,0:T(8,128)}, f32[448,256]{1,0:T(8,128)}, u32[]{:S(2)}, u32[]{:S(2)}) collective-permute-start(f32[448,256]{1,0:T(8,128)} %get-tuple-element.88), channel_id=1, source_target_pairs={{0,1},{1,0},{2,3},{3,2},{4,5},{5,4},{6,7},{7,6},{8,9},{9,8},{10,11... | collective-permute-start | bytes 1376264 | tf_op jit(solution)/shard_map/ppermute | solution.py:92
  17.4 18.8 %collective-permute-start.8 = (f32[1352,128]{1,0:T(8,128)S(1)}, f32[1352,128]{1,0:T(8,128)S(1)}, u32[]{:S(2)}, u32[]{:S(2)}) collective-permute-start(f32[1352,128]{1,0:T(8,128)S(1)} %concatenate.52.p0), channel_id=1, source_target_pairs={{0,2},{1,3},{2,0},{3,1},{4,6},{5,7},{6,4},{7,5},{8,10},{9,11},{10,... | collective-permute-start | bytes 2076680 | tf_op jit(solution)/shard_map/ppermute | solution.py:92
  20.1 45.9 %collective-permute-start.9 = (f32[1352,128]{1,0:T(8,128)S(1)}, f32[1352,128]{1,0:T(8,128)}, u32[]{:S(2)}, u32[]{:S(2)}) collective-permute-start(f32[1352,128]{1,0:T(8,128)S(1)} %concatenate.52.p0), channel_id=1, source_target_pairs={{0,1},{1,0},{2,3},{3,2},{4,5},{5,4},{6,7},{7,6},{8,9},{9,8},{10,11... | collective-permute-start | bytes 2076680 | tf_op jit(solution)/shard_map/ppermute | solution.py:92
  36.2 29.8 %collective-permute-start.10 = (f32[1352,128]{1,0:T(8,128)S(1)}, f32[1352,128]{1,0:T(8,128)}, u32[]{:S(2)}, u32[]{:S(2)}) collective-permute-start(f32[1352,128]{1,0:T(8,128)S(1)} %collective-permute-done.8.p1), channel_id=1, source_target_pairs={{0,1},{1,0},{2,3},{3,2},{4,5},{5,4},{6,7},{7,6},{8,9},{9,8},{10,11... | collective-permute-start | bytes 2076680 | tf_op jit(solution)/shard_map/ppermute | solution.py:92
  38.0 12.5 %collective-permute-start.2 = (f32[448,256]{1,0:T(8,128)S(1)}, f32[448,256]{1,0:T(8,128)S(1)}, u32[]{:S(2)}, u32[]{:S(2)}) collective-permute-start(f32[448,256]{1,0:T(8,128)S(1)} %add.306), channel_id=1, source_target_pairs={{0,2},{1,3},{2,0},{3,1},{4,6},{5,7},{6,4},{7,5},{8,10},{9,11},{10,... | collective-permute-start | bytes 1376264 | tf_op jit(solution)/shard_map/ppermute | solution.py:92
  86.0 8.7 %collective-permute-start.22 = (f32[264,256]{1,0:T(8,128)S(1)}, f32[264,256]{1,0:T(8,128)S(1)}, u32[]{:S(2)}, u32[]{:S(2)}) collective-permute-start(f32[264,256]{1,0:T(8,128)S(1)} %maximum_maximum_fusion.p0), channel_id=1, source_target_pairs={{0,2},{1,3},{2,0},{3,1},{4,6},{5,7},{6,4},{7,5},{8,10},{9,11},{10,... | collective-permute-start | bytes 811016 | tf_op jit(solution)/shard_map/ppermute | solution.py:92
  87.7 26.1 %collective-permute-start.23 = (f32[264,256]{1,0:T(8,128)S(1)}, f32[264,256]{1,0:T(8,128)S(1)}, u32[]{:S(2)}, u32[]{:S(2)}) collective-permute-start(f32[264,256]{1,0:T(8,128)S(1)} %maximum_maximum_fusion.p0), channel_id=1, source_target_pairs={{0,1},{1,0},{2,3},{3,2},{4,5},{5,4},{6,7},{7,6},{8,9},{9,8},{10,11... | collective-permute-start | bytes 811016 | tf_op jit(solution)/shard_map/ppermute | solution.py:92
  94.7 19.1 %collective-permute-start.24 = (f32[264,256]{1,0:T(8,128)S(1)}, f32[264,256]{1,0:T(8,128)S(1)}, u32[]{:S(2)}, u32[]{:S(2)}) collective-permute-start(f32[264,256]{1,0:T(8,128)S(1)} %collective-permute-done.22.p1), channel_id=1, source_target_pairs={{0,1},{1,0},{2,3},{3,2},{4,5},{5,4},{6,7},{7,6},{8,9},{9,8},{10,11... | collective-permute-start | bytes 811016 | tf_op jit(solution)/shard_map/ppermute | solution.py:92
  112.2 13.0 %collective-permute-start.31 = (f32[448,256]{1,0:T(8,128)}, f32[448,256]{1,0:T(8,128)}, u32[]{:S(2)}, u32[]{:S(2)}) collective-permute-start(f32[448,256]{1,0:T(8,128)} %get-tuple-element.101.att.refs_1_), channel_id=1, source_target_pairs={{0,2},{1,3},{2,0},{3,1},{4,6},{5,7},{6,4},{7,5},{8,10},{9,11},{10,... | collective-permute-start | bytes 1376264 | tf_op jit(solution)/shard_map/ppermute | solution.py:92
  118.5 18.7 %collective-permute-start.21 = (f32[448,256]{1,0:T(8,128)}, f32[448,256]{1,0:T(8,128)}, u32[]{:S(2)}, u32[]{:S(2)}) collective-permute-start(f32[448,256]{1,0:T(8,128)} %get-tuple-element.101.att.refs_1_), channel_id=1, source_target_pairs={{0,1},{1,0},{2,3},{3,2},{4,5},{5,4},{6,7},{7,6},{8,9},{9,8},{10,11... | collective-permute-start | bytes 1376264 | tf_op jit(solution)/shard_map/ppermute | solution.py:92
  124.6 49.4 %collective-permute-start.53 = (f32[448,256]{1,0:T(8,128)}, f32[448,256]{1,0:T(8,128)}, u32[]{:S(2)}, u32[]{:S(2)}) collective-permute-start(f32[448,256]{1,0:T(8,128)} %copy-done.4), channel_id=1, source_target_pairs={{0,2},{1,3},{2,0},{3,1},{4,6},{5,7},{6,4},{7,5},{8,10},{9,11},{10,... | collective-permute-start | bytes 1376264 | tf_op jit(solution)/shard_map/ppermute | solution.py:92
  125.2 20.4 %collective-permute-start.32 = (f32[448,256]{1,0:T(8,128)}, f32[448,256]{1,0:T(8,128)S(1)}, u32[]{:S(2)}, u32[]{:S(2)}) collective-permute-start(f32[448,256]{1,0:T(8,128)} %collective-permute-done.31.refs_1_), channel_id=1, source_target_pairs={{0,1},{1,0},{2,3},{3,2},{4,5},{5,4},{6,7},{7,6},{8,9},{9,8},{10,11... | collective-permute-start | bytes 1376264 | tf_op jit(solution)/shard_map/ppermute | solution.py:92
  130.5 19.4 %collective-permute-start.46 = (f32[4,8,128]{2,1,0:T(8,128)S(1)}, f32[4,8,128]{2,1,0:T(8,128)S(1)}, u32[]{:S(2)}, u32[]{:S(2)}) collective-permute-start(f32[4,8,128]{2,1,0:T(8,128)S(1)} %pad_maximum_fusion.3), channel_id=1, source_target_pairs={{0,9},{1,8},{2,11},{3,10},{4,13},{5,12},{6,15},{7,14},{8,1},{9,0},... | collective-permute-start | bytes 49160 | tf_op jit(solution)/shard_map/ppermute | solution.py:92
  149.9 6.8 %collective-permute-start.47 = (f32[8,8,128]{2,1,0:T(8,128)S(1)}, f32[8,8,128]{2,1,0:T(8,128)S(1)}, u32[]{:S(2)}, u32[]{:S(2)}) collective-permute-start(f32[8,8,128]{2,1,0:T(8,128)S(1)} %pad_maximum_fusion.1), channel_id=1, source_target_pairs={{0,5},{1,4},{2,7},{3,6},{4,1},{5,0},{6,3},{7,2},{8,13},{9,12},{10,... | collective-permute-start | bytes 98312 | tf_op jit(solution)/shard_map/ppermute | solution.py:92
  161.8 8.5 %collective-permute-start.49 = (f32[32,8,128]{2,1,0:T(8,128)S(1)}, f32[32,8,128]{2,1,0:T(8,128)S(1)}, u32[]{:S(2)}, u32[]{:S(2)}) collective-permute-start(f32[32,8,128]{2,1,0:T(8,128)S(1)} %get-tuple-element.213), channel_id=1, source_target_pairs={{0,1},{1,0},{2,3},{3,2},{4,5},{5,4},{6,7},{7,6},{8,9},{9,8},{10,11... | collective-permute-start | bytes 393224 | tf_op jit(solution)/shard_map/ppermute | solution.py:92
  162.2 24.4 %collective-permute-start.33 = (f32[448,256]{1,0:T(8,128)}, f32[448,256]{1,0:T(8,128)}, u32[]{:S(2)}, u32[]{:S(2)}) collective-permute-start(f32[448,256]{1,0:T(8,128)} %get-tuple-element.108), channel_id=1, source_target_pairs={{0,1},{1,0},{2,3},{3,2},{4,5},{5,4},{6,7},{7,6},{8,9},{9,8},{10,11... | collective-permute-start | bytes 1376264 | tf_op jit(solution)/shard_map/ppermute | solution.py:92
  167.0 9.1 %collective-permute-start.100 = (f32[32,256]{1,0:T(8,128)}, f32[32,256]{1,0:T(8,128)}, u32[]{:S(2)}, u32[]{:S(2)}) collective-permute-start(f32[32,256]{1,0:T(8,128)} %get-tuple-element.203), channel_id=1, source_target_pairs={{0,16},{4,20},{8,24},{12,28},{16,0},{20,4},{24,8},{28,12},{1,17},{... | collective-permute-start | bytes 98312 | tf_op jit(solution)/shard_map/ppermute | solution.py:92
  168.1 9.0 %collective-permute-start.101 = (f32[32,256]{1,0:T(8,128)}, f32[32,256]{1,0:T(8,128)}, u32[]{:S(2)}, u32[]{:S(2)}) collective-permute-start(f32[32,256]{1,0:T(8,128)} %get-tuple-element.202), channel_id=1, source_target_pairs={{0,20},{4,16},{8,28},{12,24},{16,4},{20,0},{24,12},{28,8},{1,21},{... | collective-permute-start | bytes 98312 | tf_op jit(solution)/shard_map/ppermute | solution.py:92
  170.3 6.7 %collective-permute-start.102 = (f32[32,256]{1,0:T(8,128)}, f32[32,256]{1,0:T(8,128)}, u32[]{:S(2)}, u32[]{:S(2)}) collective-permute-start(f32[32,256]{1,0:T(8,128)} %get-tuple-element.201), channel_id=1, source_target_pairs={{0,24},{4,28},{8,16},{12,20},{16,8},{20,12},{24,0},{28,4},{1,25},{... | collective-permute-start | bytes 98312 | tf_op jit(solution)/shard_map/ppermute | solution.py:92
  174.0 10.2 %collective-permute-start.103 = (f32[32,256]{1,0:T(8,128)}, f32[32,256]{1,0:T(8,128)S(1)}, u32[]{:S(2)}, u32[]{:S(2)}) collective-permute-start(f32[32,256]{1,0:T(8,128)} %get-tuple-element.200), channel_id=1, source_target_pairs={{0,28},{4,24},{8,20},{12,16},{16,12},{20,8},{24,4},{28,0},{1,29},{... | collective-permute-start | bytes 98312 | tf_op jit(solution)/shard_map/ppermute | solution.py:92
  176.1 8.1 %collective-permute-start.97 = (f32[32,256]{1,0:T(8,128)}, f32[32,256]{1,0:T(8,128)S(1)}, u32[]{:S(2)}, u32[]{:S(2)}) collective-permute-start(f32[32,256]{1,0:T(8,128)} %get-tuple-element.199), channel_id=1, source_target_pairs={{0,4},{4,0},{8,12},{12,8},{16,20},{20,16},{24,28},{28,24},{1,5},{5... | collective-permute-start | bytes 98312 | tf_op jit(solution)/shard_map/ppermute | solution.py:92
  177.0 7.7 %collective-permute-start.98 = (f32[32,256]{1,0:T(8,128)}, f32[32,256]{1,0:T(8,128)S(1)}, u32[]{:S(2)}, u32[]{:S(2)}) collective-permute-start(f32[32,256]{1,0:T(8,128)} %get-tuple-element.205), channel_id=1, source_target_pairs={{0,8},{4,12},{8,0},{12,4},{16,24},{20,28},{24,16},{28,20},{1,9},{5... | collective-permute-start | bytes 98312 | tf_op jit(solution)/shard_map/ppermute | solution.py:92
  177.0 7.8 %collective-permute-start.99 = (f32[32,256]{1,0:T(8,128)}, f32[32,256]{1,0:T(8,128)S(1)}, u32[]{:S(2)}, u32[]{:S(2)}) collective-permute-start(f32[32,256]{1,0:T(8,128)} %get-tuple-element.204), channel_id=1, source_target_pairs={{0,12},{4,8},{8,4},{12,0},{16,28},{20,24},{24,20},{28,16},{1,13},{... | collective-permute-start | bytes 98312 | tf_op jit(solution)/shard_map/ppermute | solution.py:92
  184.2 72.3 %collective-permute-start.54 = (f32[448,256]{1,0:T(8,128)S(1)}, f32[448,256]{1,0:T(8,128)S(1)}, u32[]{:S(2)}, u32[]{:S(2)}) collective-permute-start(f32[448,256]{1,0:T(8,128)S(1)} %copy-done.6), channel_id=1, source_target_pairs={{0,1},{1,0},{2,3},{3,2},{4,5},{5,4},{6,7},{7,6},{8,9},{9,8},{10,11... | collective-permute-start | bytes 1376264 | tf_op jit(solution)/shard_map/ppermute | solution.py:92
  184.2 72.2 %collective-permute-start.55 = (f32[448,256]{1,0:T(8,128)}, f32[448,256]{1,0:T(8,128)S(1)}, u32[]{:S(2)}, u32[]{:S(2)}) collective-permute-start(f32[448,256]{1,0:T(8,128)} %collective-permute-done.53.r1), channel_id=1, source_target_pairs={{0,1},{1,0},{2,3},{3,2},{4,5},{5,4},{6,7},{7,6},{8,9},{9,8},{10,11... | collective-permute-start | bytes 1376264 | tf_op jit(solution)/shard_map/ppermute | solution.py:92
  184.7 9.3 %collective-permute-start.30 = (f32[448,256]{1,0:T(8,128)}, f32[448,256]{1,0:T(8,128)S(1)}, u32[]{:S(2)}, u32[]{:S(2)}) collective-permute-start(f32[448,256]{1,0:T(8,128)} %copy-done.53), channel_id=1, source_target_pairs={{0,1},{1,0},{2,3},{3,2},{4,5},{5,4},{6,7},{7,6},{8,9},{9,8},{10,11... | collective-permute-start | bytes 1376264 | tf_op jit(solution)/shard_map/ppermute | solution.py:92
  187.9 12.6 %collective-permute-start.34 = (f32[448,256]{1,0:T(8,128)S(1)}, f32[448,256]{1,0:T(8,128)S(1)}, u32[]{:S(2)}, u32[]{:S(2)}) collective-permute-start(f32[448,256]{1,0:T(8,128)S(1)} %add.328), channel_id=1, source_target_pairs={{0,2},{1,3},{2,0},{3,1},{4,6},{5,7},{6,4},{7,5},{8,10},{9,11},{10,... | collective-permute-start | bytes 1376264 | tf_op jit(solution)/shard_map/ppermute | solution.py:92
  193.6 12.7 %collective-permute-start.106 = (f32[32,256]{1,0:T(8,128)S(1)}, f32[32,256]{1,0:T(8,128)S(1)}, u32[]{:S(2)}, u32[]{:S(2)}) collective-permute-start(f32[32,256]{1,0:T(8,128)S(1)} %get-tuple-element.187), channel_id=1, source_target_pairs={{0,12},{4,8},{8,4},{12,0},{16,28},{20,24},{24,20},{28,16},{1,13},{... | collective-permute-start | bytes 98312 | tf_op jit(solution)/shard_map/ppermute | solution.py:92
  194.0 15.3 %collective-permute-start.107 = (f32[32,256]{1,0:T(8,128)S(1)}, f32[32,256]{1,0:T(8,128)S(1)}, u32[]{:S(2)}, u32[]{:S(2)}) collective-permute-start(f32[32,256]{1,0:T(8,128)S(1)} %get-tuple-element.187), channel_id=1, source_target_pairs={{0,16},{4,20},{8,24},{12,28},{16,0},{20,4},{24,8},{28,12},{1,17},{... | collective-permute-start | bytes 98312 | tf_op jit(solution)/shard_map/ppermute | solution.py:92
  200.5 16.9 %collective-permute-start.108 = (f32[32,256]{1,0:T(8,128)S(1)}, f32[32,256]{1,0:T(8,128)S(1)}, u32[]{:S(2)}, u32[]{:S(2)}) collective-permute-start(f32[32,256]{1,0:T(8,128)S(1)} %get-tuple-element.187), channel_id=1, source_target_pairs={{0,20},{4,16},{8,28},{12,24},{16,4},{20,0},{24,12},{28,8},{1,21},{... | collective-permute-start | bytes 98312 | tf_op jit(solution)/shard_map/ppermute | solution.py:92
  207.6 14.7 %collective-permute-start.109 = (f32[32,256]{1,0:T(8,128)S(1)}, f32[32,256]{1,0:T(8,128)S(1)}, u32[]{:S(2)}, u32[]{:S(2)}) collective-permute-start(f32[32,256]{1,0:T(8,128)S(1)} %get-tuple-element.187), channel_id=1, source_target_pairs={{0,24},{4,28},{8,16},{12,20},{16,8},{20,12},{24,0},{28,4},{1,25},{... | collective-permute-start | bytes 98312 | tf_op jit(solution)/shard_map/ppermute | solution.py:92
  214.9 11.4 %collective-permute-start.110 = (f32[32,256]{1,0:T(8,128)S(1)}, f32[32,256]{1,0:T(8,128)S(1)}, u32[]{:S(2)}, u32[]{:S(2)}) collective-permute-start(f32[32,256]{1,0:T(8,128)S(1)} %get-tuple-element.187), channel_id=1, source_target_pairs={{0,28},{4,24},{8,20},{12,16},{16,12},{20,8},{24,4},{28,0},{1,29},{... | collective-permute-start | bytes 98312 | tf_op jit(solution)/shard_map/ppermute | solution.py:92
  228.6 10.4 %collective-permute-start.92 = (f32[8,128]{1,0:T(8,128)S(1)}, f32[8,128]{1,0:T(8,128)S(1)}, u32[]{:S(2)}, u32[]{:S(2)}) collective-permute-start(f32[8,128]{1,0:T(8,128)S(1)} %get-tuple-element.140), channel_id=1, source_target_pairs={{0,17},{1,16},{2,19},{3,18},{4,21},{5,20},{6,23},{7,22},{8,25},{9,... | collective-permute-start | bytes 12296 | tf_op jit(solution)/shard_map/ppermute | solution.py:92
  231.5 25.0 %collective-permute-start.75 = (f32[448,128]{1,0:T(8,128)S(1)}, f32[448,128]{1,0:T(8,128)S(1)}, u32[]{:S(2)}, u32[]{:S(2)}) collective-permute-start(f32[448,128]{1,0:T(8,128)S(1)} %get-tuple-element.135), channel_id=1, source_target_pairs={{0,1},{1,0},{2,3},{3,2},{4,5},{5,4},{6,7},{7,6},{8,9},{9,8},{10,11... | collective-permute-start | bytes 688136 | tf_op jit(solution)/shard_map/ppermute | solution.py:92
  243.3 8.8 %collective-permute-start.60 = (f32[2,256]{1,0:T(2,128)S(1)}, f32[2,256]{1,0:T(2,128)S(1)}, u32[]{:S(2)}, u32[]{:S(2)}) collective-permute-start(f32[2,256]{1,0:T(2,128)S(1)} %add.349), channel_id=1, source_target_pairs={{0,3},{1,2},{2,1},{3,0},{4,7},{5,6},{6,5},{7,4},{8,11},{9,10},{10,... | collective-permute-start | bytes 6152 | tf_op jit(solution)/shard_map/ppermute | solution.py:92
  252.1 8.4 %collective-permute-start.76 = (f32[448,128]{1,0:T(8,128)S(1)}, f32[448,128]{1,0:T(8,128)S(1)}, u32[]{:S(2)}, u32[]{:S(2)}) collective-permute-start(f32[448,128]{1,0:T(8,128)S(1)} %get-tuple-element.136), channel_id=1, source_target_pairs={{0,2},{1,3},{2,0},{3,1},{4,6},{5,7},{6,4},{7,5},{8,10},{9,11},{10,... | collective-permute-start | bytes 688136 | tf_op jit(solution)/shard_map/ppermute | solution.py:92
  252.6 11.3 %collective-permute-start.77 = (f32[448,128]{1,0:T(8,128)S(1)}, f32[448,128]{1,0:T(8,128)S(1)}, u32[]{:S(2)}, u32[]{:S(2)}) collective-permute-start(f32[448,128]{1,0:T(8,128)S(1)} %get-tuple-element.137), channel_id=1, source_target_pairs={{0,3},{1,2},{2,1},{3,0},{4,7},{5,6},{6,5},{7,4},{8,11},{9,10},{10,... | collective-permute-start | bytes 688136 | tf_op jit(solution)/shard_map/ppermute | solution.py:92
  269.3 7.5 %collective-permute-start.78 = (f32[144,128]{1,0:T(8,128)}, f32[144,128]{1,0:T(8,128)S(1)}, u32[]{:S(2)}, u32[]{:S(2)}) collective-permute-start(f32[144,128]{1,0:T(8,128)} %get-tuple-element.192), channel_id=1, source_target_pairs={{0,4},{4,0},{8,12},{12,8},{16,20},{20,16},{24,28},{28,24},{1,5},{5... | collective-permute-start | bytes 221192 | tf_op jit(solution)/shard_map/ppermute | solution.py:92
  270.1 8.9 %collective-permute-start.79 = (f32[144,128]{1,0:T(8,128)}, f32[144,128]{1,0:T(8,128)S(1)}, u32[]{:S(2)}, u32[]{:S(2)}) collective-permute-start(f32[144,128]{1,0:T(8,128)} %get-tuple-element.198), channel_id=1, source_target_pairs={{0,8},{4,12},{8,0},{12,4},{16,24},{20,28},{24,16},{28,20},{1,9},{5... | collective-permute-start | bytes 221192 | tf_op jit(solution)/shard_map/ppermute | solution.py:92
  272.8 9.9 %collective-permute-start.80 = (f32[144,128]{1,0:T(8,128)}, f32[144,128]{1,0:T(8,128)S(1)}, u32[]{:S(2)}, u32[]{:S(2)}) collective-permute-start(f32[144,128]{1,0:T(8,128)} %get-tuple-element.197), channel_id=1, source_target_pairs={{0,12},{4,8},{8,4},{12,0},{16,28},{20,24},{24,20},{28,16},{1,13},{... | collective-permute-start | bytes 221192 | tf_op jit(solution)/shard_map/ppermute | solution.py:92
  273.7 12.4 %collective-permute-start.81 = (f32[144,128]{1,0:T(8,128)}, f32[144,128]{1,0:T(8,128)S(1)}, u32[]{:S(2)}, u32[]{:S(2)}) collective-permute-start(f32[144,128]{1,0:T(8,128)} %get-tuple-element.196), channel_id=1, source_target_pairs={{0,16},{4,20},{8,24},{12,28},{16,0},{20,4},{24,8},{28,12},{1,17},{... | collective-permute-start | bytes 221192 | tf_op jit(solution)/shard_map/ppermute | solution.py:92
  276.2 11.2 %collective-permute-start.82 = (f32[144,128]{1,0:T(8,128)}, f32[144,128]{1,0:T(8,128)S(1)}, u32[]{:S(2)}, u32[]{:S(2)}) collective-permute-start(f32[144,128]{1,0:T(8,128)} %get-tuple-element.195), channel_id=1, source_target_pairs={{0,20},{4,16},{8,28},{12,24},{16,4},{20,0},{24,12},{28,8},{1,21},{... | collective-permute-start | bytes 221192 | tf_op jit(solution)/shard_map/ppermute | solution.py:92
  276.8 10.6 %collective-permute-start.83 = (f32[144,128]{1,0:T(8,128)}, f32[144,128]{1,0:T(8,128)S(1)}, u32[]{:S(2)}, u32[]{:S(2)}) collective-permute-start(f32[144,128]{1,0:T(8,128)} %get-tuple-element.194), channel_id=1, source_target_pairs={{0,24},{4,28},{8,16},{12,20},{16,8},{20,12},{24,0},{28,4},{1,25},{... | collective-permute-start | bytes 221192 | tf_op jit(solution)/shard_map/ppermute | solution.py:92
  279.0 8.4 %collective-permute-start.84 = (f32[144,128]{1,0:T(8,128)}, f32[144,128]{1,0:T(8,128)S(1)}, u32[]{:S(2)}, u32[]{:S(2)}) collective-permute-start(f32[144,128]{1,0:T(8,128)} %get-tuple-element.193), channel_id=1, source_target_pairs={{0,28},{4,24},{8,20},{12,16},{16,12},{20,8},{24,4},{28,0},{1,29},{... | collective-permute-start | bytes 221192 | tf_op jit(solution)/shard_map/ppermute | solution.py:92
  282.7 18.0 %collective-permute-start.50 = (f32[448,256]{1,0:T(8,128)}, f32[448,256]{1,0:T(8,128)S(1)}, u32[]{:S(2)}, u32[]{:S(2)}) collective-permute-start(f32[448,256]{1,0:T(8,128)} %copy-done.31), channel_id=1, source_target_pairs={{0,2},{1,3},{2,0},{3,1},{4,6},{5,7},{6,4},{7,5},{8,10},{9,11},{10,... | collective-permute-start | bytes 1376264 | tf_op jit(solution)/shard_map/ppermute | solution.py:92
  286.1 18.3 %collective-permute-start.51 = (f32[448,256]{1,0:T(8,128)}, f32[448,256]{1,0:T(8,128)S(1)}, u32[]{:S(2)}, u32[]{:S(2)}) collective-permute-start(f32[448,256]{1,0:T(8,128)} %copy-done.31), channel_id=1, source_target_pairs={{0,1},{1,0},{2,3},{3,2},{4,5},{5,4},{6,7},{7,6},{8,9},{9,8},{10,11... | collective-permute-start | bytes 1376264 | tf_op jit(solution)/shard_map/ppermute | solution.py:92
  292.2 6.9 %collective-permute-start.86 = (f32[144,128]{1,0:T(8,128)S(1)}, f32[144,128]{1,0:T(8,128)S(1)}, u32[]{:S(2)}, u32[]{:S(2)}) collective-permute-start(f32[144,128]{1,0:T(8,128)S(1)} %get-tuple-element.189), channel_id=1, source_target_pairs={{0,8},{4,12},{8,0},{12,4},{16,24},{20,28},{24,16},{28,20},{1,9},{5... | collective-permute-start | bytes 221192 | tf_op jit(solution)/shard_map/ppermute | solution.py:92
  295.5 8.3 %collective-permute-start.88 = (f32[144,128]{1,0:T(8,128)S(1)}, f32[144,128]{1,0:T(8,128)S(1)}, u32[]{:S(2)}, u32[]{:S(2)}) collective-permute-start(f32[144,128]{1,0:T(8,128)S(1)} %get-tuple-element.189), channel_id=1, source_target_pairs={{0,16},{4,20},{8,24},{12,28},{16,0},{20,4},{24,8},{28,12},{1,17},{... | collective-permute-start | bytes 221192 | tf_op jit(solution)/shard_map/ppermute | solution.py:92
  299.1 9.8 %collective-permute-start.89 = (f32[144,128]{1,0:T(8,128)S(1)}, f32[144,128]{1,0:T(8,128)S(1)}, u32[]{:S(2)}, u32[]{:S(2)}) collective-permute-start(f32[144,128]{1,0:T(8,128)S(1)} %get-tuple-element.189), channel_id=1, source_target_pairs={{0,20},{4,16},{8,28},{12,24},{16,4},{20,0},{24,12},{28,8},{1,21},{... | collective-permute-start | bytes 221192 | tf_op jit(solution)/shard_map/ppermute | solution.py:92
  301.4 11.0 %collective-permute-start.90 = (f32[144,128]{1,0:T(8,128)S(1)}, f32[144,128]{1,0:T(8,128)S(1)}, u32[]{:S(2)}, u32[]{:S(2)}) collective-permute-start(f32[144,128]{1,0:T(8,128)S(1)} %get-tuple-element.189), channel_id=1, source_target_pairs={{0,24},{4,28},{8,16},{12,20},{16,8},{20,12},{24,0},{28,4},{1,25},{... | collective-permute-start | bytes 221192 | tf_op jit(solution)/shard_map/ppermute | solution.py:92
  307.2 7.8 %collective-permute-start.61 = (f32[32,256]{1,0:T(8,128)S(1)}, f32[32,256]{1,0:T(8,128)S(1)}, u32[]{:S(2)}, u32[]{:S(2)}) collective-permute-start(f32[32,256]{1,0:T(8,128)S(1)} %get-tuple-element.206), channel_id=1, source_target_pairs={{0,4},{4,0},{8,12},{12,8},{16,20},{20,16},{24,28},{28,24},{1,5},{5... | collective-permute-start | bytes 98312 | tf_op jit(solution)/shard_map/ppermute | solution.py:92
  308.5 8.4 %collective-permute-start.62 = (f32[32,256]{1,0:T(8,128)S(1)}, f32[32,256]{1,0:T(8,128)S(1)}, u32[]{:S(2)}, u32[]{:S(2)}) collective-permute-start(f32[32,256]{1,0:T(8,128)S(1)} %get-tuple-element.212), channel_id=1, source_target_pairs={{0,8},{4,12},{8,0},{12,4},{16,24},{20,28},{24,16},{28,20},{1,9},{5... | collective-permute-start | bytes 98312 | tf_op jit(solution)/shard_map/ppermute | solution.py:92
  309.5 10.2 %collective-permute-start.63 = (f32[32,256]{1,0:T(8,128)S(1)}, f32[32,256]{1,0:T(8,128)S(1)}, u32[]{:S(2)}, u32[]{:S(2)}) collective-permute-start(f32[32,256]{1,0:T(8,128)S(1)} %get-tuple-element.211), channel_id=1, source_target_pairs={{0,12},{4,8},{8,4},{12,0},{16,28},{20,24},{24,20},{28,16},{1,13},{... | collective-permute-start | bytes 98312 | tf_op jit(solution)/shard_map/ppermute | solution.py:92
  311.4 10.8 %collective-permute-start.64 = (f32[32,256]{1,0:T(8,128)S(1)}, f32[32,256]{1,0:T(8,128)S(1)}, u32[]{:S(2)}, u32[]{:S(2)}) collective-permute-start(f32[32,256]{1,0:T(8,128)S(1)} %get-tuple-element.210), channel_id=1, source_target_pairs={{0,16},{4,20},{8,24},{12,28},{16,0},{20,4},{24,8},{28,12},{1,17},{... | collective-permute-start | bytes 98312 | tf_op jit(solution)/shard_map/ppermute | solution.py:92
  312.4 9.8 %collective-permute-start.65 = (f32[32,256]{1,0:T(8,128)S(1)}, f32[32,256]{1,0:T(8,128)S(1)}, u32[]{:S(2)}, u32[]{:S(2)}) collective-permute-start(f32[32,256]{1,0:T(8,128)S(1)} %get-tuple-element.209), channel_id=1, source_target_pairs={{0,20},{4,16},{8,28},{12,24},{16,4},{20,0},{24,12},{28,8},{1,21},{... | collective-permute-start | bytes 98312 | tf_op jit(solution)/shard_map/ppermute | solution.py:92
  315.0 7.3 %collective-permute-start.66 = (f32[32,256]{1,0:T(8,128)S(1)}, f32[32,256]{1,0:T(8,128)S(1)}, u32[]{:S(2)}, u32[]{:S(2)}) collective-permute-start(f32[32,256]{1,0:T(8,128)S(1)} %get-tuple-element.208), channel_id=1, source_target_pairs={{0,24},{4,28},{8,16},{12,20},{16,8},{20,12},{24,0},{28,4},{1,25},{... | collective-permute-start | bytes 98312 | tf_op jit(solution)/shard_map/ppermute | solution.py:92
  316.9 6.9 %collective-permute-start.67 = (f32[32,256]{1,0:T(8,128)S(1)}, f32[32,256]{1,0:T(8,128)S(1)}, u32[]{:S(2)}, u32[]{:S(2)}) collective-permute-start(f32[32,256]{1,0:T(8,128)S(1)} %get-tuple-element.207), channel_id=1, source_target_pairs={{0,28},{4,24},{8,20},{12,16},{16,12},{20,8},{24,4},{28,0},{1,29},{... | collective-permute-start | bytes 98312 | tf_op jit(solution)/shard_map/ppermute | solution.py:92
  319.7 7.1 %collective-permute-start.91 = (f32[144,128]{1,0:T(8,128)S(1)}, f32[144,128]{1,0:T(8,128)S(1)}, u32[]{:S(2)}, u32[]{:S(2)}) collective-permute-start(f32[144,128]{1,0:T(8,128)S(1)} %get-tuple-element.189), channel_id=1, source_target_pairs={{0,28},{4,24},{8,20},{12,16},{16,12},{20,8},{24,4},{28,0},{1,29},{... | collective-permute-start | bytes 221192 | tf_op jit(solution)/shard_map/ppermute | solution.py:92
  323.9 26.3 %collective-permute-start.68 = (f32[32,256]{1,0:T(8,128)S(1)}, f32[32,256]{1,0:T(8,128)}, u32[]{:S(2)}, u32[]{:S(2)}) collective-permute-start(f32[32,256]{1,0:T(8,128)S(1)} %get-tuple-element.191), channel_id=1, source_target_pairs={{0,4},{4,0},{8,12},{12,8},{16,20},{20,16},{24,28},{28,24},{1,5},{5... | collective-permute-start | bytes 98312 | tf_op jit(solution)/shard_map/ppermute | solution.py:92
  344.4 8.7 %collective-permute-start.69 = (f32[32,256]{1,0:T(8,128)S(1)}, f32[32,256]{1,0:T(8,128)S(1)}, u32[]{:S(2)}, u32[]{:S(2)}) collective-permute-start(f32[32,256]{1,0:T(8,128)S(1)} %get-tuple-element.191), channel_id=1, source_target_pairs={{0,8},{4,12},{8,0},{12,4},{16,24},{20,28},{24,16},{28,20},{1,9},{5... | collective-permute-start | bytes 98312 | tf_op jit(solution)/shard_map/ppermute | solution.py:92
  344.4 11.1 %collective-permute-start.70 = (f32[32,256]{1,0:T(8,128)S(1)}, f32[32,256]{1,0:T(8,128)S(1)}, u32[]{:S(2)}, u32[]{:S(2)}) collective-permute-start(f32[32,256]{1,0:T(8,128)S(1)} %get-tuple-element.191), channel_id=1, source_target_pairs={{0,12},{4,8},{8,4},{12,0},{16,28},{20,24},{24,20},{28,16},{1,13},{... | collective-permute-start | bytes 98312 | tf_op jit(solution)/shard_map/ppermute | solution.py:92
  347.0 8.4 %collective-permute-start.71 = (f32[32,256]{1,0:T(8,128)S(1)}, f32[32,256]{1,0:T(8,128)S(1)}, u32[]{:S(2)}, u32[]{:S(2)}) collective-permute-start(f32[32,256]{1,0:T(8,128)S(1)} %get-tuple-element.191), channel_id=1, source_target_pairs={{0,16},{4,20},{8,24},{12,28},{16,0},{20,4},{24,8},{28,12},{1,17},{... | collective-permute-start | bytes 98312 | tf_op jit(solution)/shard_map/ppermute | solution.py:92
  347.5 8.0 %collective-permute-start.72 = (f32[32,256]{1,0:T(8,128)S(1)}, f32[32,256]{1,0:T(8,128)S(1)}, u32[]{:S(2)}, u32[]{:S(2)}) collective-permute-start(f32[32,256]{1,0:T(8,128)S(1)} %get-tuple-element.191), channel_id=1, source_target_pairs={{0,20},{4,16},{8,28},{12,24},{16,4},{20,0},{24,12},{28,8},{1,21},{... | collective-permute-start | bytes 98312 | tf_op jit(solution)/shard_map/ppermute | solution.py:92
  353.1 6.6 %collective-permute-start.74 = (f32[32,256]{1,0:T(8,128)S(1)}, f32[32,256]{1,0:T(8,128)S(1)}, u32[]{:S(2)}, u32[]{:S(2)}) collective-permute-start(f32[32,256]{1,0:T(8,128)S(1)} %get-tuple-element.191), channel_id=1, source_target_pairs={{0,28},{4,24},{8,20},{12,16},{16,12},{20,8},{24,4},{28,0},{1,29},{... | collective-permute-start | bytes 98312 | tf_op jit(solution)/shard_map/ppermute | solution.py:92
  (123 other events, 1165.3 us)
where the time goes:
time: 362 us; the launch traced here: 360 us
  starting transfers between devices  132 us (36%)
  waiting for transfers between devices  119 us (33%)
  local copies, waits for them, and re-layouts  56.2 us (16%)
  Pallas kernels  41.5 us (11%)
  other arithmetic  6.46 us (2%)
  between operations  5.06 us (1%)
    ppermute x111, starting transfers between devices, swap(): return lax.ppermute(x, axis, [(i, i ^ k) for i in range(n)])  132 us
    ppermute x111, waiting for transfers between devices, swap(): return lax.ppermute(x, axis, [(i, i ^ k) for i in range(n)])  119 us
    pallas_call x19, Pallas kernels, call(): pl.pallas_call(body, out_shape=out_shape, grid_spec=pltpu.PrefetchScalarG...  41.5 us
    unnamed x166, local copies, waits for them, and re-layouts  29.6 us
  transfers between devices with their start and end apart: 111, of which 48 were waited for; matrix products, arithmetic and copies ran while one was open for 12% of the time, Pallas kernels for 8%

commit v1 on v0

v1 whole, which is shorter than its diff:
```python
import functools

import jax
import jax.numpy as jnp
from jax import lax
from jax.experimental import pallas as pl
from jax.experimental.pallas import tpu as pltpu
from jax.sharding import PartitionSpec as P

EPSILON = 1e-05
F32, BF16 = jnp.float32, jnp.bfloat16
PAD = 16
VMEM_LIMIT = 32 * 1024 * 1024


def bits_of(n):
    out, k = [], 1
    while k < n:
        out.append(k)
        k *= 2
    return out


def split2(x):
    hi = x.astype(BF16)
    return hi, (x - hi.astype(F32)).astype(BF16)


def mm(a, b, dims=((1,), (0,))):
    return lax.dot_general(a, b, (dims, ((), ())), preferred_element_type=F32)


def split3(x):
    hi = x.astype(BF16)
    x = x - hi.astype(F32)
    mid = x.astype(BF16)
    return hi, mid, (x - mid.astype(F32)).astype(BF16)


def mm3(a, b, dims=((1,), (0,))):
    return mm(a[0], b[0], dims) + (mm(a[0], b[1], dims) + mm(a[1], b[0], dims))


def mm6(a, b, dims=((1,), (0,))):
    small = mm(a[0], b[2], dims) + mm(a[2], b[0], dims) + mm(a[1], b[1], dims)
    return mm(a[0], b[0], dims) + (mm(a[0], b[1], dims) + mm(a[1], b[0], dims) + small)


def exact(a, b, dims=((1,), (0,))):
    return lax.dot_general(
        a, b, (dims, ((), ())), precision=lax.Precision.HIGHEST, preferred_element_type=F32
    )


def call(body, counts, ins, outs, scratch=(), flops=0, far=(), far_out=()):
    far, far_out = sorted(far), sorted(far_out)
    moved = sum(a.size * a.dtype.itemsize for a in ins) + sum(
        int(jnp.dtype(d).itemsize) * functools.reduce(lambda x, y: x * y, s, 1) for s, d in outs
    )
    vmem, hbm = pl.BlockSpec(memory_space=pltpu.VMEM), pl.BlockSpec(memory_space=pltpu.HBM)
    own_scratch = len(scratch)
    held = [pltpu.VMEM(ins[k].shape, ins[k].dtype) for k in far] + [pltpu.VMEM(*outs[k]) for k in far_out]
    sems = [pltpu.SemaphoreType.DMA] * len(held)

    def kernel(s, *refs):
        n, m = len(ins), len(outs)
        refs_in, refs_out = list(refs[:n]), list(refs[n : n + m])
        rest = refs[n + m :]
        scr, bufs, sem = rest[:own_scratch], rest[own_scratch : own_scratch + len(held)], rest[own_scratch + len(held) :]
        copies = []
        for i, k in enumerate(far):
            copies.append(pltpu.make_async_copy(refs_in[k], bufs[i], sem[i]))
            copies[-1].start()
            refs_in[k] = bufs[i]
        homes = []
        for i, k in enumerate(far_out):
            i += len(far)
            homes.append(pltpu.make_async_copy(bufs[i], refs_out[k], sem[i]))
            refs_out[k] = bufs[i]
        for copy in copies:
            copy.wait()
        body(s, *refs_in, *refs_out, *scr)
        for copy in homes:
            copy.start()
        for copy in homes:
            copy.wait()

    ins = [pltpu.with_memory_space_constraint(a, pltpu.HBM) if k in far else a for k, a in enumerate(ins)]
    return pl.pallas_call(
        kernel,
        out_shape=[pltpu.HBM(s, d) if k in far_out else jax.ShapeDtypeStruct(s, d) for k, (s, d) in enumerate(outs)],
        in_specs=[pl.BlockSpec(memory_space=pltpu.SMEM)] + [hbm if k in far else vmem for k in range(len(ins))],
        out_specs=[hbm if k in far_out else vmem for k in range(len(outs))],
        scratch_shapes=list(scratch) + held + sems,
        compiler_params=pltpu.CompilerParams(vmem_limit_bytes=VMEM_LIMIT),
        cost_estimate=pl.CostEstimate(flops=flops, bytes_accessed=moved, transcendentals=0),
    )(counts, *ins)


def mask_of(nv, rows, cols, edge):
    r = lax.broadcasted_iota(jnp.int32, (rows, cols), 0)
    return ((r & (PAD - 1)) < edge) & (r < nv * (edge * PAD))


def colsum(x):
    return jnp.sum(x, axis=0, keepdims=True)


def build(mesh):
    nd, nc = mesh.shape["dp"], mesh.shape["chan"]
    both = ("dp", "chan")
    cbits, dbits = bits_of(nc), bits_of(nd)
    flat_bits = bits_of(nd * nc)
    pairs = [flat_bits[i : i + 2] for i in range(1, len(flat_bits), 2)]
    sum_groups = [[1]] + [[k | 1 for k in ([p[0], p[1], p[0] ^ p[1]] if len(p) == 2 else p)] for p in pairs[::-1]]

    def swap(x, axis, k):
        n = {"dp": nd, "chan": nc}[axis] if isinstance(axis, str) else nd * nc
        return lax.ppermute(x, axis, [(i, i ^ k) for i in range(n)])

    def sum_steps(x):
        out = [x]
        for g in sum_groups:
            x = out[-1]
            got = [swap(x, both, k) for k in g]
            x = x + got[0]
            out.append(x + (got[1] + got[2]) if len(g) == 3 else x)
        return out

    def sum_all(x):
        return sum_steps(x)[-1]

    def after(x, *deps):
        return lax.optimization_barrier((x,) + deps)[0]

    def pick(x, i):
        return lax.dynamic_index_in_dim(x, i, 0, False)

    groups = [dbits[:1]] + [dbits[i : i + 2] for i in range(1, len(dbits), 2)]

    def masks(g):
        out = [0]
        for k in g:
            out = out + [m ^ k for m in out]
        return out

    def place_in(g):
        n = 2 ** len(g)
        return (lax.axis_index("dp") // g[0]) % n, n

    def cut_chunks(scr, g, outs):
        at, n = place_in(g)
        rows = scr.shape[0] // n
        for m, o in enumerate(outs):
            o[...] = scr[pl.ds(pl.multiple_of((at ^ m) * rows, 8), rows), :]

    def chunk_outs(rows, g):
        n = 2 ** len(g)
        return [((rows // n, 128), F32)] * n

    def padded_rows(rows):
        return -(-rows // (8 * nd)) * 8 * nd

    def big_sum_dp(counts, chunks):
        for i, g in enumerate(groups):
            got = [chunks[0]] + [swap(z, "dp", m) for z, m in zip(chunks[1:], masks(g)[1:])]
            rows = got[0].shape[0]
            last = i == len(groups) - 1

            def add_body(s, *refs, n=len(got), last=last, i=i):
                v = refs[0][...]
                for z in refs[1:n]:
                    v = v + z[...]
                if last:
                    refs[n][...] = v
                else:
                    refs[-1][...] = v
                    cut_chunks(refs[-1], groups[i + 1], refs[n:-1])

            chunks = call(
                add_body,
                counts,
                got,
                [((rows, 128), F32)] if last else chunk_outs(rows, groups[i + 1]),
                [] if last else [pltpu.VMEM((rows, 128), F32)],
            )
        (x,) = chunks
        for g in groups[::-1]:
            got = [x] + [swap(x, "dp", m) for m in masks(g)[1:]]
            rows = x.shape[0]

            def join_body(s, *refs, g=g, rows=rows):
                at, _ = place_in(g)
                for m, z in enumerate(refs[:-1]):
                    refs[-1][pl.ds(pl.multiple_of((at ^ m) * rows, 8), rows), :] = z[...]

            (x,) = call(join_body, counts, got, [((rows * len(got), 128), F32)])
        return x

    def quarter_of(chan):
        q = chan * 0
        for k in cbits:
            q = q * 2 + (chan // k) % 2
        return q

    def per_device(
        features_in,
        image_counts,
        reduce_weight,
        reduce_gain,
        reduce_shift,
        split_weight,
        split_gain,
        split_shift,
        squeeze_weight,
        squeeze_gain,
        squeeze_shift,
        attend_weight,
        attend_bias,
        expand_weight,
        expand_gain,
        expand_shift,
        grad_out,
    ):
        slots, edge = features_in.shape[0], features_in.shape[1]
        area = edge * edge
        win = features_in.shape[3]
        mid = reduce_weight.shape[1]
        half = mid // 2
        lw = split_weight.shape[4]
        inner = squeeze_gain.shape[0]
        own = slots // nc
        span = edge * PAD
        R = own * span
        ni = nd * slots
        c = lax.axis_index("chan")

        def me():
            c = lax.axis_index("chan")
            return c, quarter_of(c)

        def valid(s, r):
            return jnp.clip(s[lax.axis_index("dp")] - (me()[1] ^ r) * own, 0, own)

        def recip(s, each):
            total = s[0]
            for i in range(1, nd):
                total = total + s[i]
            return (1.0 / (jnp.full((1, 128), total, jnp.int32).astype(F32) * each))[:, 0:1]

        TAPS = [(u, v) for u in range(3) for v in range(3)]

        def stats(sum_ref, s):
            n = recip(s, area)
            avg = sum_ref[0:1] * n
            inv = lax.rsqrt(sum_ref[1:2] * n - avg * avg + EPSILON)
            return avg, inv, n

        lb = win // 128

        def native(x):
            x = x.transpose(1, 2, 0, 3).reshape(area, slots, lb, 128)
            return x.transpose(0, 2, 1, 3).reshape(area * lb * slots, 128)

        def from_native(z):
            z = z.reshape(area, lb, slots, 128).transpose(0, 2, 1, 3)
            return z.reshape(edge, edge, slots, win).transpose(2, 0, 1, 3)

        def place_of(h, i, b, r):
            at = (h * edge * lb + i) * slots + (me()[1] ^ r) * own + b
            return pl.ds(at, edge, stride=lb * slots)

        def load_quarter(ref, scr, r, mask):
            for b in range(own):
                for h in range(edge):
                    for i in range(lb):
                        scr[b * edge + h, :edge, i * 128 : (i + 1) * 128] = ref[place_of(h, i, b, r), :]
            return jnp.where(mask, scr[...].reshape(R, win), 0.0)

        def store_quarter(ref, scr, r, z):
            scr[...] = z.reshape(own * edge, PAD, win)
            for b in range(own):
                for h in range(edge):
                    for i in range(lb):
                        ref[place_of(h, i, b, r), :] = scr[b * edge + h, :edge, i * 128 : (i + 1) * 128]

        feats, gouts = native(features_in), native(grad_out)
        quarter_scratch = pltpu.VMEM((own * edge, PAD, win), F32)

        wt = split_weight.transpose(0, 1, 3, 4, 2).reshape(-1, half)

        wt_c, wt_y = swap(wt, "chan", 1), swap(wt, "chan", 2)

        def pack(att_w, sq_w, rg, rs, sg, ss, ab, eg):
            return jnp.concatenate(
                [
                    att_w.transpose(1, 2, 0).reshape(2 * lw, inner),
                    sq_w,
                    sg.reshape(1, -1),
                    ss.reshape(1, -1),
                    ab.reshape(1, -1),
                    jnp.concatenate([rg, rs])[None],
                    eg.reshape(-1, 2 * lw),
                    jnp.zeros((8 - 4 - win // (2 * lw), 2 * lw), F32),
                ]
            )

        nw = 9 * half

        def reduce_body(rels, s, x_ref, w_ref, *refs):
            outs, scr = refs[:-1], refs[-1]
            w = split3(w_ref[...])
            for o, r in zip(outs, rels):
                x = load_quarter(x_ref, scr, r, mask_of(valid(s, r), R, win, edge))
                o[...] = mm6(split3(x), w)

        def reduce_call(rels):
            return call(
                functools.partial(reduce_body, rels),
                image_counts,
                [feats, reduce_weight],
                [((R, mid), F32)] * len(rels),
                [quarter_scratch],
                flops=12 * R * win * mid * len(rels),
                far=(0, 1),
            )

        p3, p1 = reduce_call((3, 1))
        p2, p0 = reduce_call((2, 0))
        y1 = p1 + swap(p3, "chan", 1)
        ys = swap(y1, "chan", 2)
        rc = swap(p2, "chan", 1)

        def gather3(x, gate=None):
            y = swap(x, "chan", 2)
            return [x, y, swap(x, "chan", 1), swap(y if gate is None else after(y, gate), "chan", 1)]

        small = lax.optimization_barrier(
            (
                y1,
                attend_weight,
                squeeze_weight,
                reduce_gain,
                reduce_shift,
                split_gain,
                split_shift,
                attend_bias,
                expand_gain,
            )
        )
        ps = pack(*small[1:])
        wt_r = [wt, wt_y, wt_c, swap(after(wt_y, y1), "chan", 1)]
        ps_all = gather3(ps)

        def pa_body(s, p0, p1, p2, p3, wat, vec, wsq, g3, scr):
            c, _ = me()
            scr[c] = p0[...]
            scr[c ^ 2] = p1[...]
            scr[c ^ 1] = p2[...]
            scr[c ^ 3] = p3[...]
            lo = 2 * lw + lw
            lane = lax.broadcasted_iota(jnp.int32, (8, 2 * lw), 1)
            for pair in range(nc // 2):
                a, b = scr[2 * pair, lo : lo + 8, :], scr[2 * pair + 1, lo : lo + 8, :]
                cols = slice(pair * 2 * lw, (pair + 1) * 2 * lw)
                vec[0, :, cols] = jnp.where(lane < lw, a, pltpu.roll(b, lw, 1))
                vec[1, :, cols] = jnp.where(lane < lw, pltpu.roll(a, lw, 1), b)
            g3[...] = jnp.zeros((8, win), F32)
            for k in range(nc):
                rows = slice(k * lw, (k + 1) * lw)
                for r in range(2):
                    wat[r, rows, :] = scr[k, r * lw : (r + 1) * lw, :]
                wsq[rows, :] = scr[k, 2 * lw : lo, :]
                for i in range(win // (2 * lw)):
                    g3[k : k + 1, i * 2 * lw : (i + 1) * 2 * lw] = scr[k, lo + 4 + i : lo + 5 + i, :]

        wat, vec, wsq, g3 = call(
            pa_body,
            image_counts,
            ps_all,
            [((2, mid, inner), F32), ((2, 8, mid), F32), ((mid, inner), F32), ((8, win), F32)],
            [pltpu.VMEM((nc,) + ps.shape, F32)],
        )

        CHAN_REL = (0, 2, 1, 3)

        def wt_body(s, v0, v1, v2, v3, w1, w2, w3, w1_home):
            for rel, ref in enumerate((v0, v1, v2, v3)):
                rows = pl.ds(pl.multiple_of((me()[0] ^ CHAN_REL[rel]) * lw, lw), lw)
                for t in range(9):
                    for r in range(2):
                        at = t * 2 * lw + r * lw
                        for o, z in zip((w1, w2, w3), split3(ref[at : at + lw, :])):
                            o[r, rows, t * half : (t + 1) * half] = z
            w1_home[...] = w1[...]

        w1, w2, w3, w1_home = call(
            wt_body, image_counts, wt_r, [((2, mid, nw), BF16)] * 4, far=(0,), far_out=(3,)
        )

        def red_body(s, a, b, y, red, sums):
            v = a[...] + b[...] + y[...]
            red[...] = v
            sums[0:1] = colsum(v)
            sums[1:2] = colsum(v * v)

        red, s1 = call(red_body, image_counts, [p0, rc, after(ys, vec, w1)], [((R, mid), F32), ((2, mid), F32)])
        s1_steps = sum_steps(s1)
        s1 = s1_steps[-1]

        def taps_in(z, scrs, n):
            w = z.shape[1]
            rows = n * span
            for v in range(3):
                zz = z if v == 1 else pltpu.roll(z, 1 if v == 0 else rows - 1, 0)
                parts = split3(zz) if len(scrs) == 3 else [zz.astype(BF16)]
                for scr, part in zip(scrs, parts):
                    scr[v, :, 0] = jnp.zeros((n, PAD, w), BF16)
                    scr[v, :, edge + 1] = jnp.zeros((n, PAD, w), BF16)
                    scr[v, :, 1 : edge + 1] = part.reshape(n, edge, PAD, w)

        def conv_body(s, red, sums, vec, w1, w2, w3, out, sums2, za, zb, zc):
            avg, inv, _ = stats(sums, s)
            mask = mask_of(valid(s, 0), R, mid, edge)
            z = jnp.maximum((red[...] - avg) * inv * vec[0, 3:4] + vec[1, 3:4], 0.0)
            z = jnp.where(mask, z, 0.0)
            taps_in(z, (za, zb, zc), own)
            for r in range(2):
                cols = slice(r * half, (r + 1) * half)
                lhs = [
                    jnp.concatenate([z[v, :, u : u + edge, :, cols].reshape(R, half) for u, v in TAPS], axis=1)
                    for z in (za, zb, zc)
                ]
                y = mm6(lhs, (w1[r], w2[r], w3[r]), ((1,), (1,)))
                out[:, r * mid : (r + 1) * mid] = y
                y = jnp.where(mask, y, 0.0)
                sums2[0:1, r * mid : (r + 1) * mid] = colsum(y)
                sums2[1:2, r * mid : (r + 1) * mid] = colsum(y * y)

        spl, s2 = call(
            conv_body,
            image_counts,
            [red, s1, vec, w1, w2, w3],
            [((R, 2 * mid), F32), ((2, 2 * mid), F32)],
            [pltpu.VMEM((3, own, PAD, PAD, mid), BF16)] * 3,
            flops=24 * R * nw * mid,
        )
        we_all = lax.all_gather(after(expand_weight, s1), "chan")
        s2_steps = sum_steps(s2)
        s2 = s2_steps[-1]

        def second(spl, sums, n, vec, r, mask):
            cols = slice(r * mid, (r + 1) * mid)
            avg = sums[0:1, cols] * n
            inv = lax.rsqrt(sums[1:2, cols] * n - avg * avg + EPSILON)
            norm = (spl[:, cols] - avg) * inv
            act = norm * vec[r, 0:1] + vec[r, 1:2]
            return norm, act, (act > 0) & mask, inv

        def per_image(z):
            return [colsum(z[b * span : (b + 1) * span]) for b in range(own)]

        nb = mid // 128
        BLOCK = max(64, 4 * nb * own)
        ND = nd * nc

        def pool_body(s, spl, sums, vec, wsq, c12, sq, sfc):
            mask = mask_of(valid(s, 0), R, mid, edge)
            n = recip(s, area)
            pooled = [0.0] * own
            c12[...] = jnp.zeros((BLOCK, 128), F32)
            for r in range(2):
                norm, act, on, _ = second(spl, sums, n, vec, r, mask)
                c1 = per_image(jnp.where(on, 1.0, 0.0))
                c2 = per_image(jnp.where(on, norm, 0.0))
                for b in range(own):
                    for i in range(nb):
                        sl = slice(i * 128, (i + 1) * 128)
                        for k, z in ((r * nb + i, c1), ((2 + r) * nb + i, c2)):
                            c12[k * own + b : k * own + b + 1, :] = z[b][:, sl]
                    pooled[b] = pooled[b] + vec[r, 0:1] * c2[b] + vec[r, 1:2] * c1[b]
            p = jnp.concatenate(pooled + [jnp.zeros((8 - own, mid), F32)], axis=0) * (1.0 / area)
            v = exact(p, wsq[...])
            sq[...] = v
            live = lax.broadcasted_iota(jnp.int32, (8, inner), 0) < valid(s, 0)
            v = jnp.where(live, v, 0.0)
            sfc[0:1] = colsum(v)
            sfc[1:2] = colsum(v * v)

        c12, sq, sfc = call(
            pool_body,
            image_counts,
            [spl, s2, vec, wsq],
            [((BLOCK, 128), F32), ((8, inner), F32), ((2, inner), F32)],
        )
        c12_g = lax.all_gather(c12, both, axis=0, tiled=True)
        sfc = sum_all(sfc)
        red_g = lax.all_gather(after(red, sfc), "chan")
        sgb = jnp.stack([squeeze_gain, squeeze_shift])

        def squeeze_norm(sq, sums, s, sgb):
            n = recip(s, 1)
            avg = sums[0:1] * n
            inv = lax.rsqrt(sums[1:2] * n - avg * avg + EPSILON)
            norm = (sq - avg) * inv
            return norm, norm * sgb[0:1] + sgb[1:2], inv

        def attend_body(s, spl, sums, vec, sfc, sq, sgb, wat, att, wts):
            mask = mask_of(valid(s, 0), R, mid, edge)
            n = recip(s, area)
            _, actf, _ = squeeze_norm(sq[...], sfc, s, sgb)
            hidden = jnp.maximum(actf, 0.0)
            lg = [exact(hidden, wat[r], ((1,), (1,))) + vec[r, 2:3] for r in range(2)]
            top = jnp.maximum(lg[0], lg[1])
            e = [jnp.exp(z - top) for z in lg]
            total = e[0] + e[1]
            acc = 0.0
            imgs = lax.broadcasted_iota(jnp.int32, (R, mid), 0)
            for r in range(2):
                w = e[r] / total
                wts[r] = w
                _, act, on, _ = second(spl, sums, n, vec, r, mask)
                wrow = w[0:1]
                for b in range(1, own):
                    wrow = jnp.where(imgs >= b * span, w[b : b + 1], wrow)
                acc = acc + jnp.where(on, act * wrow, 0.0)
            att[...] = acc

        att, wts = call(
            attend_body,
            image_counts,
            [spl, s2, vec, sfc, sq, sgb, wat],
            [((R, mid), F32), ((2, 8, mid), F32)],
        )

        def own_expand_body(s, att, w, sums):
            a = split2(att[...])
            for k in range(nc):
                y = mm3(a, split2(w[k]))
                sums[2 * k : 2 * k + 1] = colsum(y)
                sums[2 * k + 1 : 2 * k + 2] = colsum(y * y)

        (s3,) = call(
            own_expand_body, image_counts, [att, we_all], [((2 * nc, win), F32)], flops=6 * R * mid * win * nc, far=(1,)
        )
        s3_steps = sum_steps(s3)
        s3 = s3_steps[-1]
        att_r = gather3(att, s3_steps[-2])
        s3l = lax.dynamic_slice_in_dim(s3, 2 * c, 2, 0)
        eg = jnp.stack([expand_gain, expand_shift])

        def expand_body(rels, extra, s, *refs):
            n = len(rels)
            atts, (x_ref, g_ref, w_ref, sums, eg) = refs[:n], refs[n : n + 5]
            prev, refs = refs[n + 5 : n + 5 + extra], refs[n + 5 + extra :]
            bos, gas = refs[:n], refs[n : 2 * n]
            sg, t1, t2, u1, scr = refs[2 * n :]
            avg, inv, _ = stats(sums, s)
            w = split2(w_ref[...])
            sg_acc, t1_acc, t2_acc, u_acc = [0.0, 0.0], 0.0, 0.0, 0.0
            for k, r in enumerate(rels):
                mask = mask_of(valid(s, r), R, win, edge)
                a = atts[k][...]
                ap = split2(a)
                norm = (mm3(ap, w) - avg) * inv
                x = load_quarter(x_ref, scr, r, mask)
                pre = norm * eg[0:1] + eg[1:2] + x
                on = (pre > 0) & mask
                bos[k][...] = jnp.where(on, pre, 0.0)
                g = load_quarter(g_ref, scr, r, on)
                sg_acc[0] += colsum(g)
                sg_acc[1] += colsum(g * norm)
                gb = g.astype(BF16)
                nb = jnp.where(mask, norm, 0.0).astype(BF16)
                gas[k][...] = mm((g * (eg[0:1] * inv)).astype(BF16), w[0], ((1,), (1,)))
                t = mm(ap[0], jnp.concatenate([gb, nb], axis=1), ((0,), (0,)))
                t1_acc += t[:, :win]
                t2_acc += t[:, win:]
                u_acc += colsum(a)
            row = lax.broadcasted_iota(jnp.int32, (2 * nc, win), 0)
            c, _ = me()
            z = jnp.where(row == 2 * c, sg_acc[0], 0.0)
            sg[...] = jnp.where(row == 2 * c + 1, sg_acc[1], z)
            for o, z, p in zip((t1, t2, u1), (t1_acc, t2_acc, u_acc), prev[1:] or (None,) * 3):
                o[...] = z if p is None else z + p[...]
            if prev:
                sg[...] = sg[...] + prev[0][...]

        def expand_call(rels, prev):
            n = len(rels)
            return call(
                functools.partial(expand_body, rels, len(prev)),
                image_counts,
                [att_r[r] for r in rels] + [feats, gouts, expand_weight, s3l, eg] + prev,
                [((R, win), F32)] * n
                + [((R, mid), F32)] * n
                + [((2 * nc, win), F32), ((mid, win), F32), ((mid, win), F32), ((1, mid), F32)],
                [quarter_scratch],
                flops=12 * R * mid * win * n,
                far=(n, n + 1, n + 2),
                far_out=tuple(range(n)) + ((2 * n + 1, 2 * n + 2) if prev else ()),
            )

        bo3, bo1, ga3, ga1, *prev = expand_call((3, 1), [])
        bo2, bo0, ga2, ga0, sg3, t1, t2, u1 = expand_call((2, 0), list(prev))
        gy1 = ga1 + swap(ga3, "chan", 1)
        gys = swap(gy1, "chan", 2)
        grc = swap(ga2, "chan", 1)
        sg3 = sum_all(sg3)
        bos = [bo0, bo1, bo2, bo3]
        sg3l = lax.dynamic_slice_in_dim(sg3, 2 * c, 2, 0)

        def gatt_body(s, p, rc, ys, att, we, g3, sums, sg, spl, sums2, vec, wts, sfc, sq, sgb, wat, ga, l0, l1, l2, l3, merged, scr):
            m_acc, v_acc = 0.0, 0.0
            n = recip(s, area)
            for k in range(nc):
                avg = sums[2 * k : 2 * k + 1] * n
                inv = lax.rsqrt(sums[2 * k + 1 : 2 * k + 2] * n - avg * avg + EPSILON)
                sc = g3[k : k + 1] * inv * n
                kap = sg[2 * k + 1 : 2 * k + 2] * inv * sc
                w = we[k]
                wb = w.astype(BF16)
                m_acc += mm((w * kap).astype(BF16), wb, ((1,), (1,)))
                vv = sg[2 * k : 2 * k + 1] * sc - avg * kap
                row = lax.broadcasted_iota(jnp.int32, (16, win), 0)
                high = jnp.where(row == 0, vv, 0.0)
                low = jnp.where(row == 1, vv - vv.astype(BF16).astype(F32), 0.0)
                v_acc += colsum(mm((high + low).astype(BF16), wb, ((1,), (1,))))
            mask = mask_of(valid(s, 0), R, mid, edge)
            g = p[...] + rc[...] + ys[...] - mm(att[...].astype(BF16), m_acc.astype(BF16)) - v_acc
            g = jnp.where(mask, g, 0.0)
            ga[...] = g
            gw, a12 = [], []
            for r in range(2):
                norm, act, on, _ = second(spl, sums2, n, vec, r, mask)
                gon = jnp.where(on, g, 0.0)
                a1, a2 = per_image(gon), per_image(gon * norm)
                zero = [jnp.zeros((8 - own, mid), F32)]
                a1, a2 = jnp.concatenate(a1 + zero, axis=0), jnp.concatenate(a2 + zero, axis=0)
                a12.append((a1, a2))
                gw.append(vec[r, 0:1] * a2 + vec[r, 1:2] * a1)
            mean = wts[0] * gw[0] + wts[1] * gw[1]
            gh = 0.0
            parts, zs = [], []
            for r in range(2):
                z = wts[r] * (gw[r] - mean)
                zs.append(z)
                gh = gh + exact(z, wat[r])
                for j in range(2):
                    parts.append(colsum(wts[r] * a12[r][j]))
            parts += [colsum(z) for z in zs]
            _, actf, _ = squeeze_norm(sq[...], sfc, s, sgb)
            dzf = jnp.where(actf > 0, gh, 0.0)
            c, _ = me()
            row = lax.broadcasted_iota(jnp.int32, (ni, inner), 0)
            z = jnp.zeros((ni, inner), F32)
            for b in range(own):
                z = jnp.where(row == lax.axis_index("dp") * nc + c + b * ND, dzf[b : b + 1], z)
            merged[0:ni] = z
            lane = lax.broadcasted_iota(jnp.int32, (8, 2 * lw), 1)
            for pair in range(nc // 2):
                cols = slice(pair * 2 * lw, (pair + 1) * 2 * lw)
                a, b = zs[0][:, cols], zs[1][:, cols]
                scr[2 * pair] = jnp.where(lane < lw, a, pltpu.roll(b, lw, 1))
                scr[2 * pair + 1] = jnp.where(lane < lw, pltpu.roll(a, lw, 1), b)
            for k, o in enumerate((l0, l1, l2, l3)):
                o[...] = scr[c ^ k]
            merged[ni:] = jnp.zeros((6 * nb + 4, inner), F32)
            for k, pz in enumerate(parts):
                for i in range(nb):
                    merged[ni + k * nb + i : ni + k * nb + i + 1] = pz[:, i * 128 : (i + 1) * 128]

        ga, l0, l1, l2, l3, merged = call(
            gatt_body,
            image_counts,
            [ga0, grc, gys, att, we_all, g3, s3, sg3, spl, s2, vec, wts, sfc, sq, sgb, wat],
            [((R, mid), F32)] + [((8, 2 * lw), F32)] * 4 + [((ni + 6 * nb + 4, inner), F32)],
            [pltpu.VMEM((nc, 8, 2 * lw), F32)],
            flops=2 * R * mid * mid + 2 * nc * mid * mid * win,
            far=(4,),
            far_out=(0,),
        )

        def all_body(s, g, vec, wsq, sfc, sgb, c1_ref, c2_ref, pool_ref, norm_ref, hid_ref):
            def rows(k):
                return jnp.concatenate([g[pl.ds(k * own + b, ND, stride=BLOCK), :] for b in range(own)], axis=0)

            pooled = 0.0
            for r in range(2):
                c1 = jnp.concatenate([rows(r * nb + i) for i in range(nb)], axis=1)
                c2 = jnp.concatenate([rows((2 + r) * nb + i) for i in range(nb)], axis=1)
                c1_ref[r] = c1
                c2_ref[r] = c2
                pooled = pooled + vec[r, 0:1] * c2 + vec[r, 1:2] * c1
            pooled = pooled * (1.0 / area)
            pool_ref[...] = pooled
            norm, actf, _ = squeeze_norm(exact(pooled, wsq[...]), sfc, s, sgb)
            norm_ref[...] = norm
            hid_ref[...] = jnp.maximum(actf, 0.0)

        c1_all, c2_all, pool_all, normf_all, hid_all = call(
            all_body,
            image_counts,
            [c12_g, vec, wsq, sfc, sgb],
            [
                ((2, ni, mid), F32),
                ((2, ni, mid), F32),
                ((ni, mid), F32),
                ((ni, inner), F32),
                ((ni, inner), F32),
            ],
            far=(0,),
        )
        for k, g in enumerate(sum_groups):
            got = [swap(merged, both, m) for m in g]
            z = merged + got[0]
            merged = z + (got[1] + got[2]) if len(g) == 3 else z
            if k == 1:
                merged, c1_all = lax.optimization_barrier((merged, c1_all))

        def all_valid(s):
            row = lax.broadcasted_iota(jnp.int32, (ni, inner), 0)
            dev = row & (ND - 1)
            at, chan = dev >> (nc.bit_length() - 1), dev & (nc - 1)
            slot = (row >> (ND.bit_length() - 1)) + own * sum(
                ((chan >> i) & 1) * (nc >> (i + 1)) for i in range(len(cbits))
            )
            live = jnp.zeros((ni, inner), jnp.int32)
            for i in range(nd):
                live = jnp.where(at == i, s[i], live)
            return jnp.where(slot < live, 1.0, 0.0)

        def back_body(
            s, merged, c1a, c2a, normf, sfc, sgb, wsq, ga, spl, sums2, vec, wts, red, sums1, w1,
            dz1, sg1, b0, b1, b2, b3, gq_ref, sg2, gfc, wab, zh, blk,
        ):
            dzf = merged[0:ni]
            norm_all = normf[...]
            s_f = colsum(dzf)
            g_f = colsum(dzf * norm_all)
            gfc[0:1] = g_f
            gfc[1:2] = s_f
            for r in range(2):
                for i in range(nb):
                    k = ni + (4 + r) * nb + i
                    wab[r : r + 1, i * 128 : (i + 1) * 128] = merged[k : k + 1]
            nf, n = recip(s, 1), recip(s, area)
            _, _, inv = squeeze_norm(0.0, sfc, s, sgb)
            gq = sgb[0:1] * inv * (dzf - all_valid(s) * (s_f + norm_all * g_f) * nf)
            gq_ref[...] = gq
            gp = exact(gq, wsq[...], ((1,), (1,))) * (1.0 / area)
            mask = mask_of(valid(s, 0), R, mid, edge)
            imgs = lax.broadcasted_iota(jnp.int32, (R, mid), 0)
            grow = lax.broadcasted_iota(jnp.int32, (ni, mid), 0)
            c, _ = me()
            mine = lax.axis_index("dp") * nc + c
            gpo = [colsum(jnp.where(grow == mine + b * ND, gp, 0.0)) for b in range(own)]
            gprow = gpo[0]
            for b in range(1, own):
                gprow = jnp.where(imgs >= b * span, gpo[b], gprow)
            lane = lax.broadcasted_iota(jnp.int32, (R, 2 * lw), 1)
            gss = []
            acts = []
            for r in range(2):
                def piece(j):
                    k = (r * 2 + j) * nb
                    return jnp.concatenate([merged[ni + k + i : ni + k + i + 1] for i in range(nb)], axis=1)

                s2v = piece(0) + colsum(gp * c1a[r])
                g2v = piece(1) + colsum(gp * c2a[r])
                sg2[0, r : r + 1] = s2v
                sg2[1, r : r + 1] = g2v
                norm, act, on, inv2 = second(spl, sums2, n, vec, r, mask)
                w = wts[r]
                wrow = w[0:1]
                for b in range(1, own):
                    wrow = jnp.where(imgs >= b * span, w[b : b + 1], wrow)
                dz = jnp.where(on, wrow * ga[...] + gprow, 0.0)
                gs = vec[r, 0:1] * inv2 * (dz - (s2v + norm * g2v) * n)
                gs = jnp.where(mask, gs, 0.0)
                gss.append(gs)
            for pair in range(nc // 2):
                cols = slice(pair * 2 * lw, (pair + 1) * 2 * lw)
                a, b = gss[0][:, cols], gss[1][:, cols]
                blk[2 * pair] = jnp.where(lane < lw, a, pltpu.roll(b, lw, 1))
                blk[2 * pair + 1] = jnp.where(lane < lw, pltpu.roll(a, lw, 1), b)
            for k, o in enumerate((b0, b1, b2, b3)):
                o[...] = blk[c ^ k]
            avg1, inv1, _ = stats(sums1, s)
            norm1 = (red[...] - avg1) * inv1
            on1 = (norm1 * vec[0, 3:4] + vec[1, 3:4] > 0) & mask
            for r in range(2):
                taps_in(gss[r], (zh,), own)
                acc = 0.0
                for t, (u, v) in enumerate(TAPS):
                    z = zh[2 - v, :, 2 - u : 2 - u + edge].reshape(R, mid)
                    acc += mm(z, w1[r, :, t * half : (t + 1) * half])
                cols = slice(r * half, (r + 1) * half)
                acc = jnp.where(on1[:, cols], acc, 0.0)
                dz1[:, cols] = acc
                sg1[0:1, cols] = colsum(acc)
                sg1[1:2, cols] = colsum(acc * norm1[:, cols])

        dz1, sg1, blk0, blk1, blk2, blk3, gq, sg2, gfc, wab = call(
            back_body,
            image_counts,
            [merged, c1_all, c2_all, normf_all, sfc, sgb, wsq, ga, spl, s2, vec, wts, red, s1, w1_home],
            [((R, mid), F32), ((2, mid), F32)]
            + [((R, 2 * lw), F32)] * 4
            + [((ni, inner), F32), ((2, 2, mid), F32), ((2, inner), F32), ((2, mid), F32)],
            [pltpu.VMEM((3, own, PAD, PAD, mid), BF16), pltpu.VMEM((nc, R, 2 * lw), F32)],
            flops=4 * R * nw * mid,
            far=(7, 13),
            far_out=(2,),
        )
        blks = [blk0, swap(blk1, "chan", 1), swap(blk2, "chan", 2), swap(blk3, "chan", 3)]
        sg1_steps = sum_steps(sg1)
        sg1 = sg1_steps[-1]
        dz1_r = gather3(after(dz1, sg1_steps[1]), sg1)

        gl_r = [l0, swap(after(l1, sg1_steps[0]), "chan", 1), swap(after(l2, sg1_steps[0]), "chan", 2), swap(after(l3, sg1_steps[0]), "chan", 3)]

        def early_body(s, a0, a1, a2, a3, hid, t1, t2, u1, sums, sg, eg, out):
            acc = 0.0
            base = lax.axis_index("dp") * nc
            for k, a in enumerate((a0, a1, a2, a3)):
                z = a[...]
                row = lax.broadcasted_iota(jnp.int32, (8, inner), 0)
                h = jnp.zeros((8, inner), F32)
                for b in range(own):
                    h = jnp.where(row == b, hid[pl.ds(base + (me()[0] ^ k) + b * ND, 1), :], h)
                acc += exact(z, h, ((0,), (0,)))
            avg, inv, n = stats(sums, s)
            outer = exact(u1[...], sg[0:1], ((0,), (0,)))
            z = (eg[0:1] * inv) * (t1[...] - (outer + t2[...] * sg[1:2]) * n)
            for i in range(lb):
                out[i * mid : (i + 1) * mid] = z[:, i * 128 : (i + 1) * 128]
            at = lb * mid
            out[at : at + 2 * lw] = acc

        (early,) = call(
            early_body,
            image_counts,
            gl_r + [hid_all, t1, t2, u1, s3l, sg3l, eg],
            [((lb * mid + 2 * lw, inner), F32)],
            far=(5, 6),
        )

        n_early, n_total = lb * mid + 2 * lw, padded_rows(lb * mid + 2 * lw + win * mid // 128)
        mb = mid // 128

        def dwr_body(s, d0, d1, d2, d3, red_g, x_ref, sums, sg, vec, early, *refs):
            outs, (go0, go1, go2, go3, scr, sent) = refs[:-6], refs[-6:]
            avg, inv, n = stats(sums, s)
            acc = 0.0
            for r, (dz, go) in enumerate(((d0, go0), (d1, go1), (d2, go2), (d3, go3))):
                mask = mask_of(valid(s, r), R, win, edge)
                norm = (red_g[me()[0] ^ CHAN_REL[r]] - avg) * inv
                g = vec[0, 3:4] * inv * (dz[...] - (sg[0:1] + norm * sg[1:2]) * n)
                g = jnp.where(mask, g, 0.0).astype(BF16)
                go[...] = g
                acc += mm(load_quarter(x_ref, scr, r, mask).astype(BF16), g, ((0,), (0,)))
            sent[0:n_early] = early[...]
            for i in range(mb):
                sent[n_early + i * win : n_early + (i + 1) * win] = acc[:, i * 128 : (i + 1) * 128]
            cut_chunks(sent, groups[0], outs)

        *sent, gr0, gr1, gr2, gr3 = call(
            dwr_body,
            image_counts,
            dz1_r + [red_g, feats, s1, sg1, vec, early],
            chunk_outs(n_total, groups[0]) + [((R, mid), BF16)] * 4,
            [quarter_scratch, pltpu.VMEM((n_total, 128), F32)],
            flops=8 * R * win * mid,
            far=(4, 5),
        )
        summed = big_sum_dp(image_counts, sent)
        grad_expand_weight = summed[: lb * mid].reshape(lb, mid, 128).transpose(1, 0, 2).reshape(mid, win)
        watt = summed[lb * mid : n_early]
        dwr = summed[n_early : n_early + mb * win]
        grad_reduce_weight = dwr.reshape(mb, win, 128).transpose(1, 0, 2).reshape(win, mid)

        def gin_body(s, g0, g1, g2, g3, b0, b1, b2, b3, go, w_ref, out_bo, out_gi, scr):
            w = w_ref[...].astype(BF16)
            for r, (g, b) in enumerate(((g0, b0), (g1, b1), (g2, b2), (g3, b3))):
                bo = b[...]
                z = mm(g[...], w, ((1,), (1,))) + load_quarter(go, scr, r, bo > 0)
                store_quarter(out_gi, scr, r, z)
                store_quarter(out_bo, scr, r, bo)

        block_out, grad_input = call(
            gin_body,
            image_counts,
            [gr0, gr1, gr2, gr3] + bos + [gouts, reduce_weight],
            [(feats.shape, F32)] * 2,
            [quarter_scratch],
            flops=8 * R * win * mid,
            far=(4, 5, 6, 7, 8, 9),
            far_out=(0, 1),
        )
        block_out, grad_input = from_native(block_out), from_native(grad_input)

        n_dws = padded_rows(9 * 2 * lw)

        def dws_body(s, k0, k1, k2, k3, red_g, sums, vec, *refs):
            outs, (zg, relu, out) = refs[:-3], refs[-3:]
            avg, inv, _ = stats(sums, s)
            for k, bk in enumerate((k0, k1, k2, k3)):
                mask = mask_of(valid(s, CHAN_REL[k]), R, mid, edge)
                z = jnp.maximum((red_g[me()[0] ^ k] - avg) * inv * vec[0, 3:4] + vec[1, 3:4], 0.0)
                relu[k * R : (k + 1) * R, :] = jnp.where(mask, z, 0.0).astype(BF16)
                taps_in(bk[...], (zg.at[:, k * own : (k + 1) * own],), own)
            taps = [zg[2 - v, :, 2 - u : 2 - u + edge].reshape(nc * R, 2 * lw) for u, v in TAPS]
            y = mm(relu[...], jnp.concatenate(taps, axis=1), ((0,), (0,)))
            lane = lax.broadcasted_iota(jnp.int32, (half, 2 * lw), 1)
            for t in range(9):
                cols = slice(t * 2 * lw, (t + 1) * 2 * lw)
                out[t * 2 * lw : (t + 1) * 2 * lw, :] = jnp.where(lane < lw, y[:half, cols], y[half:, cols]).T
            cut_chunks(out, groups[0], outs)

        dws = call(
            dws_body,
            image_counts,
            blks + [red_g, s1, vec],
            chunk_outs(n_dws, groups[0]),
            [pltpu.VMEM((3, slots, PAD, PAD, 2 * lw), BF16), pltpu.VMEM((nc * R, mid), BF16), pltpu.VMEM((n_dws, 128), F32)],
            flops=2 * nc * R * mid * 9 * 2 * lw,
            far=(0, 4),
        )
        dws = big_sum_dp(image_counts, dws)[: 9 * 2 * lw]
        grad_split_weight = dws.reshape(3, 3, 2, lw, half).transpose(0, 1, 4, 2, 3)

        def sq_body(s, pool, gq, out):
            out[...] = exact(pool[...], gq[...], ((0,), (0,)))

        (wsw,) = call(sq_body, image_counts, [pool_all, gq], [((mid, inner), F32)])

        def own_lanes(z, axis):
            return lax.dynamic_slice_in_dim(z, c * lw, lw, axis)

        return (
            block_out,
            grad_input,
            grad_reduce_weight,
            own_lanes(sg1[1], 0),
            own_lanes(sg1[0], 0),
            grad_split_weight,
            own_lanes(sg2[1], 1),
            own_lanes(sg2[0], 1),
            own_lanes(wsw, 0),
            gfc[0],
            gfc[1],
            watt.reshape(2, lw, inner).transpose(2, 0, 1),
            own_lanes(wab, 1),
            grad_expand_weight,
            sg3l[1],
            sg3l[0],
        )

    return per_device


def solution(mesh):
    in_specs = (
        P("dp", None, None, "chan"),
        P(),
        P("chan", None),
        P("chan"),
        P("chan"),
        P(None, None, None, None, "chan"),
        P(None, "chan"),
        P(None, "chan"),
        P("chan", None),
        P(),
        P(),
        P(None, None, "chan"),
        P(None, "chan"),
        P(None, "chan"),
        P("chan"),
        P("chan"),
        P("dp", None, None, "chan"),
    )
    out_specs = (
        P("dp", None, None, "chan"),
        P("dp", None, None, "chan"),
        P("chan", None),
        P("chan"),
        P("chan"),
        P(None, None, None, None, "chan"),
        P(None, "chan"),
        P(None, "chan"),
        P("chan", None),
        P(),
        P(),
        P(None, None, "chan"),
        P(None, "chan"),
        P(None, "chan"),
        P("chan"),
        P("chan"),
    )
    return jax.shard_map(
        build(mesh), mesh=mesh, in_specs=in_specs, out_specs=out_specs, check_vma=False
    )
```

time: 362 us -> 268 us (0.74)
  starting transfers between devices: 132 us -> 84.3 us
  local copies, waits for them, and re-layouts: 56.2 us -> 14.3 us
  waiting for transfers between devices: 119 us -> 84.3 us
  Pallas kernels: 41.5 us -> 68.6 us
  between operations: 5.06 us -> 14.3 us
  other arithmetic: 6.46 us -> 1.12 us
    ppermute x111 -> x89, starting transfers between devices: 132 us -> 84 us  [swap(): return lax.ppermute(x, axis, [(i, i ^ k) for i in range(n)])]
    ppermute x111 -> x89, waiting for transfers between devices: 119 us -> 84.3 us  [swap(): return lax.ppermute(x, axis, [(i, i ^ k) for i in range(n)])]
    pallas_call x19 -> x27, Pallas kernels: 41.5 us -> 68.6 us  [call(): pl.pallas_call(kernel, out_shape=[pltpu.HBM(s, d) if k in far_out else ja...]
    unnamed x166 -> x50, local copies, waits for them, and re-layouts: 29.6 us -> 8.89 us
    dynamic_update_slice x21 -> x0, local copies, waits for them, and re-layouts: 5.31 us -> none  [big_sum_dp(): o = lax.dynamic_update_index_in_dim(o, parts[k], d ^ k, 0)]
    concatenate x7 -> x1, local copies, waits for them, and re-layouts: 3.88 us -> 0.03 us  [pack(): jnp.concatenate([att_w.transpose(1, 2, 0).reshape(2 * lw, inner), sq_w, s...]
    reshape x3 -> x4, local copies, waits for them, and re-layouts: 4.73 us -> 1.07 us  [the longest x1 0.83 us: per_device(): summed[:lb * mid].reshape(lb, mid, 128).transpose(1, 0, 2).reshape(mid, win)]
  transfers between devices with their start and end apart: 111 -> 92, of which waited for: 48 -> 48; matrix products, arithmetic and copies ran while one was open for 12% -> 2% of each run, Pallas kernels for 8% -> 25%
where the time goes in v1:
time: 268 us; the launch traced here: 267 us
  starting transfers between devices  84.3 us (31%)
  waiting for transfers between devices  84.3 us (31%)
  Pallas kernels  68.6 us (26%)
  local copies, waits for them, and re-layouts  14.3 us (5%)
  between operations  14.3 us (5%)
    ppermute x89, waiting for transfers between devices, swap(): return lax.ppermute(x, axis, [(i, i ^ k) for i in range(n)])  84.3 us
    ppermute x89, starting transfers between devices, swap(): return lax.ppermute(x, axis, [(i, i ^ k) for i in range(n)])  84 us
    pallas_call x27, Pallas kernels, call(): pl.pallas_call(kernel, out_shape=[pltpu.HBM(s, d) if k in far_out else ja...  68.6 us
    unnamed x50, local copies, waits for them, and re-layouts  8.89 us
  transfers between devices with their start and end apart: 92, of which 48 were waited for; matrix products, arithmetic and copies ran while one was open for 2% of the time, Pallas kernels for 25%

profile of v1, /device:TPU:0, one launch (start us, length us, event | category | flops | bytes accessed | tf_op | source)
XLA Modules:
  0.0 266.8 jit_solution(7593618127655198068)
XLA Ops:
  7.2 3.0 %collective-permute-start.6 = (f32[1152,128]{1,0:T(8,128)}, f32[1152,128]{1,0:T(8,128)S(1)}, u32[]{:S(2)}, u32[]{:S(2)}) collective-permute-start(f32[1152,128]{1,0:T(8,128)} %bitcast.12.refs_0_), channel_id=1, source_target_pairs={{0,2},{1,3},{2,0},{3,1},{4,6},{5,7},{6,4},{7,5},{8,10},{9,11},{10,... | collective-permute-start | bytes 1769480 | tf_op jit(solution)/shard_map/ppermute | solution.py:119
  10.9 3.2 %shard_map.289 = (f32[448,256]{1,0:T(8,128)S(1)}, f32[448,256]{1,0:T(8,128)S(1)}) custom-call(s32[8]{0:T(128)S(1)} %copy-done.1, f32[3136,128]{1,0:T(8,128)} %bitcast.75, f32[256,256]{1,0:T(8,128)} %refs_9_.1), custom_call_target="tpu_custom_call" | custom-call | flops 704643072 | bytes 2785280 | tf_op jit(solution)/shard_map/pallas_call | solution.py:89
  14.7 1.3 collective-permute-done.1
  17.0 6.8 %collective-permute-done.6.refs_1_ = f32[1152,128]{1,0:T(8,128)S(1)} collective-permute-done((f32[1152,128]{1,0:T(8,128)}, f32[1152,128]{1,0:T(8,128)S(1)}, u32[]{:S(2)}, u32[]{:S(2)}) %collective-permute-start.6) | collective-permute-done | bytes 589856 | tf_op jit(solution)/shard_map/ppermute | solution.py:119
  23.8 1.7 collective-permute-start.2
  25.5 4.0 %shard_map.288 = (f32[448,256]{1,0:T(8,128)}, f32[448,256]{1,0:T(8,128)S(1)}) custom-call(s32[8]{0:T(128)S(1)} %copy-done.1, f32[3136,128]{1,0:T(8,128)} %bitcast.76, f32[256,256]{1,0:T(8,128)} %refs_9_.1), custom_call_target="tpu_custom_call" | custom-call | flops 704643072 | bytes 2785280 | tf_op jit(solution)/shard_map/pallas_call | solution.py:89
  30.6 8.6 %collective-permute-done.3.refs_1_ = f32[200,128]{1,0:T(8,128)S(1)} collective-permute-done((f32[200,128]{1,0:T(8,128)S(1)}, f32[200,128]{1,0:T(8,128)S(1)}, u32[]{:S(2)}, u32[]{:S(2)}) %collective-permute-start.3) | collective-permute-done | bytes 102432 | tf_op jit(solution)/shard_map/ppermute | solution.py:119
  39.1 1.3 collective-permute-done.4.refs_2_
  42.4 3.4 %shard_map.291 = (bf16[2,256,1152]{2,1,0:T(8,128)(2,1)S(1)}, bf16[2,256,1152]{2,1,0:T(8,128)(2,1)S(1)}, bf16[2,256,1152]{2,1,0:T(8,128)(2,1)S(1)}, bf16[2,256,1152]{2,1,0:T(8,128)(2,1)}) custom-call(s32[8]{0:T(128)S(1)} %copy-done.2, f32[1152,128]{1,0:T(8,128)} %bitcast.12.refs_0_, f32[1152,128]{1,0:T(8,128)S(1)} %collective-permute-done.6.refs_1_, ...), custom_call_target="tpu_custom_call" | custom-call | bytes 7077888 | tf_op jit(solution)/shard_map/pallas_call | solution.py:89
  47.9 2.2 shard_map.292
  51.3 2.6 collective-permute-start.11
  53.9 1.3 collective-permute-start.12
  55.4 3.3 %collective-permute-done.12 = f32[2,256]{1,0:T(2,128)S(1)} collective-permute-done((f32[2,256]{1,0:T(2,128)S(1)}, f32[2,256]{1,0:T(2,128)S(1)}, u32[]{:S(2)}, u32[]{:S(2)}) %collective-permute-start.12) | collective-permute-done | bytes 2080 | tf_op jit(solution)/shard_map/ppermute | solution.py:119
  58.7 1.5 collective-permute-start.14
  61.9 2.2 collective-permute-done.15
  68.4 5.1 %shard_map.293 = (f32[448,512]{1,0:T(8,128)S(1)}, f32[2,512]{1,0:T(2,128)S(1)}) custom-call(s32[8]{0:T(128)S(1)} %copy-done.2, f32[448,256]{1,0:T(8,128)} %get-tuple-element.165.refs_0_.refs_12_, f32[2,256]{1,0:T(2,128)S(1)} %add_add_fusion.10.refs_1_.refs_13_.refs_6_.refs_5_, f32[2,8,256]{2,1,0:T(8,128)S(1)} %get-tuple-element.124.refs_2_.refs_10_.refs_1_.refs_8_.refs_6_, ...), custom_call_target="tpu_custom_call" | custom-call | flops 3170893824 | bytes 4937728 | tf_op jit(solution)/shard_map/pallas_call | solution.py:89
  76.6 1.3 collective-permute-start.17
  78.7 1.8 collective-permute-done.19
  80.4 1.5 collective-permute-start.21
  83.7 2.2 collective-permute-done.22
  85.9 1.7 shard_map.294
  89.8 1.9 collective-permute-start.26
  93.0 1.6 collective-permute-done.26
  95.4 1.3 collective-permute-start.29
  97.7 1.6 collective-permute-done.29
  102.2 2.7 %shard_map.296 = f32[8,256]{1,0:T(8,128)S(1)} custom-call(s32[8]{0:T(128)S(1)} %copy-done.2, f32[448,256]{1,0:T(8,128)S(1)} %get-tuple-element.138.refs_0_.refs_1_.refs_3_, f32[4,256,256]{2,1,0:T(8,128)} %bitcast.85), custom_call_target="tpu_custom_call" | custom-call | flops 704643072 | bytes 1515520 | tf_op jit(solution)/shard_map/pallas_call | solution.py:89
  107.2 1.7 collective-permute-start.34
  110.2 1.9 collective-permute-done.34
  112.0 2.4 collective-permute-done.38.refs_1_
  114.5 1.6 collective-permute-start.36
  118.0 2.2 collective-permute-done.37
  120.2 5.1 %shard_map.297 = (f32[448,256]{1,0:T(8,128)}, f32[448,256]{1,0:T(8,128)}, f32[448,256]{1,0:T(8,128)S(1)}, f32[448,256]{1,0:T(8,128)S(1)}, f32[8,256]{1,0:T(8,128...) custom-call(s32[8]{0:T(128)S(1)} %copy-done.2, ...), custom_call_target="tpu_custom_call" | custom-call | flops 704643072 | bytes 6763520 | tf_op jit(solution)/shard_map/pallas_call | solution.py:89
  125.8 5.3 %shard_map.298 = (f32[448,256]{1,0:T(8,128)}, f32[448,256]{1,0:T(8,128)}, f32[448,256]{1,0:T(8,128)S(1)}, f32[448,256]{1,0:T(8,128)S(1)}, f32[8,256]{1,0:T(8,128...) custom-call(s32[8]{0:T(128)S(1)} %copy-done.2, ...), custom_call_target="tpu_custom_call" | custom-call | flops 704643072 | bytes 7297024 | tf_op jit(solution)/shard_map/pallas_call | solution.py:89
  132.7 2.3 collective-permute-start.46
  140.0 1.5 collective-permute-start.47
  141.5 1.7 collective-permute-done.49
  143.2 4.9 %collective-permute-done.47 = f32[8,256]{1,0:T(8,128)S(1)} collective-permute-done((f32[8,256]{1,0:T(8,128)S(1)}, f32[8,256]{1,0:T(8,128)S(1)}, u32[]{:S(2)}, u32[]{:S(2)}) %collective-permute-start.47) | collective-permute-done | bytes 8224 | tf_op jit(solution)/shard_map/ppermute | solution.py:119
  148.7 3.6 %shard_map.299 = (f32[448,256]{1,0:T(8,128)}, f32[8,128]{1,0:T(8,128)S(1)}, f32[8,128]{1,0:T(8,128)S(1)}, f32[8,128]{1,0:T(8,128)S(1)}, f32[8,128]{1,0:T(8,128)S(1)}, /*index=5*/f32[80,128]{1,0:T(8,128)S(1)}) custom-call(s32[8]{0:T(128)S(1)} %copy-done.2, f32[448,256]{1,0:T(8,128)S(1)} %get-tuple-element.145.refs_0_, ...), custom_call_target="tpu_custom_call" | custom-call | flops 192937984 | bytes 4646912 | tf_op jit(solution)/shard_map/pallas_call | solution.py:89
  154.9 2.4 collective-permute-start.53
  157.3 2.2 shard_map.300
  165.0 1.7 collective-permute-done.56
  168.0 4.7 %shard_map.301 = (f32[448,256]{1,0:T(8,128)S(1)}, f32[2,256]{1,0:T(2,128)S(1)}, f32[448,128]{1,0:T(8,128)}, f32[448,128]{1,0:T(8,128)S(1)}, f32[448,128]{1,0:T(8...) custom-call(s32[8]{0:T(128)S(1)} %copy-done.2, ...), custom_call_target="tpu_custom_call" | custom-call | flops 528482304 | bytes 4940800 | tf_op jit(solution)/shard_map/pallas_call | solution.py:89
  174.6 1.3 collective-permute-start.58
  175.9 2.2 collective-permute-start.62
  181.7 1.3 collective-permute-start.65
  188.5 4.4 %collective-permute-done.79.refs_2_ = f32[448,128]{1,0:T(8,128)S(1)} collective-permute-done((f32[448,128]{1,0:T(8,128)S(1)}, f32[448,128]{1,0:T(8,128)S(1)}, u32[]{:S(2)}, u32[]{:S(2)}) %collective-permute-start.79) | collective-permute-done | bytes 229408 | tf_op jit(solution)/shard_map/ppermute | solution.py:119
  194.0 2.4 collective-permute-done.80.refs_3_
  197.1 1.5 collective-permute-start.69
  199.5 4.2 %shard_map.309 = (f32[576,128]{1,0:T(8,128)S(1)}, f32[576,128]{1,0:T(8,128)S(1)}) custom-call(s32[8]{0:T(128)S(1)} %copy-done.2, f32[448,128]{1,0:T(8,128)} %get-tuple-element.193.refs_0_, f32[448,128]{1,0:T(8,128)S(1)} %collective-permute-done.78.refs_1_, f32[448,128]{1,0:T(8,128)S(1)} %collective-permute-done.79.refs_2_, f32[448,128]{1,0:T(8,128)S(1)} %copy-done.13, ...), custom_call_target="tpu_custom_call" | custom-call | flops 1056964608 | bytes 3360768 | tf_op jit(solution)/shard_map/pallas_call | solution.py:89
  205.2 2.2 shard_map.302.refs_9_
  207.5 4.1 %shard_map.303 = (f32[576,128]{1,0:T(8,128)S(1)}, f32[576,128]{1,0:T(8,128)S(1)}, bf16[448,256]{1,0:T(8,128)(2,1)S(1)}, bf16[448,256]{1,0:T(8,128)(2,1)S(1)}, bf...) custom-call(s32[8]{0:T(128)S(1)} %copy-done.2, f32[448,256]{1,0:T(8,128)S(1)} %get-tuple-element.163.refs_0_, ...), custom_call_target="tpu_custom_call" | custom-call | flops 234881024 | bytes 7131136 | tf_op jit(solution)/shard_map/pallas_call | solution.py:89
  211.6 1.5 collective-permute-start.70
  214.7 1.7 collective-permute-start.83
  216.4 2.3 collective-permute-start.84
  219.3 3.7 %collective-permute-done.83.refs_2_ = f32[144,128]{1,0:T(8,128)S(1)} collective-permute-done((f32[144,128]{1,0:T(8,128)S(1)}, f32[144,128]{1,0:T(8,128)S(1)}, u32[]{:S(2)}, u32[]{:S(2)}) %collective-permute-start.83) | collective-permute-done | bytes 73760 | tf_op jit(solution)/shard_map/ppermute | solution.py:119
  223.6 1.4 collective-permute-start.85
  226.4 1.7 collective-permute-start.72
  228.1 2.0 collective-permute-start.73
  231.0 1.9 collective-permute-start.87
  232.8 5.8 %collective-permute-done.72.refs_2_ = f32[144,128]{1,0:T(8,128)S(1)} collective-permute-done((f32[144,128]{1,0:T(8,128)S(1)}, f32[144,128]{1,0:T(8,128)S(1)}, u32[]{:S(2)}, u32[]{:S(2)}) %collective-permute-start.72) | collective-permute-done | bytes 73760 | tf_op jit(solution)/shard_map/ppermute | solution.py:119
  239.2 2.2 collective-permute-start.74
  242.0 1.9 collective-permute-start.76
  250.3 6.5 %shard_map.304 = (f32[3136,128]{1,0:T(8,128)}, f32[3136,128]{1,0:T(8,128)}) custom-call(s32[8]{0:T(128)S(1)} %copy-done.2, bf16[448,256]{1,0:T(8,128)(2,1)S(1)} %get-tuple-element.177.refs_0_, bf16[448,256]{1,0:T(8,128)(2,1)S(1)} %get-tuple-element.178.refs_1_, bf16[448,256]{1,0:T(8,128)(2,1)S(1)} %get-tuple-element.179.refs_2_, ...), custom_call_target="tpu_custom_call" | custom-call | flops 234881024 | bytes 7831552 | tf_op jit(solution)/shard_map/pallas_call | solution.py:89
  256.8 1.4 shard_map.313
  (244 shorter events, 80.5 us)
Async XLA Ops:
  7.2 95.1 %all-gather.8.cloned.1.call-start = ((), (), s32[]{:S(2)}) async-start(), calls=%async_computation.1 | async-start | bytes 1310720 | tf_op jit(solution)/shard_map/all_gather | solution.py:448
  7.2 16.6 %collective-permute-start.6 = (f32[1152,128]{1,0:T(8,128)}, f32[1152,128]{1,0:T(8,128)S(1)}, u32[]{:S(2)}, u32[]{:S(2)}) collective-permute-start(f32[1152,128]{1,0:T(8,128)} %bitcast.12.refs_0_), channel_id=1, source_target_pairs={{0,2},{1,3},{2,0},{3,1},{4,6},{5,7},{6,4},{7,5},{8,10},{9,11},{10,... | collective-permute-start | bytes 1769480 | tf_op jit(solution)/shard_map/ppermute | solution.py:119
  14.2 28.2 %collective-permute-start.7 = (f32[1152,128]{1,0:T(8,128)}, f32[1152,128]{1,0:T(8,128)S(1)}, u32[]{:S(2)}, u32[]{:S(2)}) collective-permute-start(f32[1152,128]{1,0:T(8,128)} %bitcast.12.refs_0_), channel_id=1, source_target_pairs={{0,1},{1,0},{2,3},{3,2},{4,5},{5,4},{6,7},{7,6},{8,9},{9,8},{10,11... | collective-permute-start | bytes 1769480 | tf_op jit(solution)/shard_map/ppermute | solution.py:119
  23.8 18.6 %collective-permute-start.8 = (f32[1152,128]{1,0:T(8,128)S(1)}, f32[1152,128]{1,0:T(8,128)S(1)}, u32[]{:S(2)}, u32[]{:S(2)}) collective-permute-start(f32[1152,128]{1,0:T(8,128)S(1)} %collective-permute-done.6.refs_1_), channel_id=1, source_target_pairs={{0,1},{1,0},{2,3},{3,2},{4,5},{5,4},{6,7},{7,6},{8,9},{9,8},{10,11... | collective-permute-start | bytes 1769480 | tf_op jit(solution)/shard_map/ppermute | solution.py:119
  23.8 24.1 %collective-permute-start.2 = (f32[448,256]{1,0:T(8,128)}, f32[448,256]{1,0:T(8,128)S(1)}, u32[]{:S(2)}, u32[]{:S(2)}) collective-permute-start(f32[448,256]{1,0:T(8,128)} %add.165), channel_id=1, source_target_pairs={{0,2},{1,3},{2,0},{3,1},{4,6},{5,7},{6,4},{7,5},{8,10},{9,11},{10,... | collective-permute-start | bytes 1376264 | tf_op jit(solution)/shard_map/ppermute | solution.py:119
  29.6 18.3 %collective-permute-start = (f32[448,256]{1,0:T(8,128)}, f32[448,256]{1,0:T(8,128)}, u32[]{:S(2)}, u32[]{:S(2)}) collective-permute-start(f32[448,256]{1,0:T(8,128)} %get-tuple-element.113), channel_id=1, source_target_pairs={{0,1},{1,0},{2,3},{3,2},{4,5},{5,4},{6,7},{7,6},{8,9},{9,8},{10,11... | collective-permute-start | bytes 1376264 | tf_op jit(solution)/shard_map/ppermute | solution.py:119
  30.2 8.9 %collective-permute-start.3 = (f32[200,128]{1,0:T(8,128)S(1)}, f32[200,128]{1,0:T(8,128)S(1)}, u32[]{:S(2)}, u32[]{:S(2)}) collective-permute-start(f32[200,128]{1,0:T(8,128)S(1)} %concatenate.7.refs_0_), channel_id=1, source_target_pairs={{0,2},{1,3},{2,0},{3,1},{4,6},{5,7},{6,4},{7,5},{8,10},{9,11},{10,... | collective-permute-start | bytes 307208 | tf_op jit(solution)/shard_map/ppermute | solution.py:119
  51.3 4.1 %collective-permute-start.11 = (f32[2,256]{1,0:T(2,128)S(1)}, f32[2,256]{1,0:T(2,128)S(1)}, u32[]{:S(2)}, u32[]{:S(2)}) collective-permute-start(f32[2,256]{1,0:T(2,128)S(1)} %add.166), channel_id=1, source_target_pairs={{0,17},{1,16},{2,19},{3,18},{4,21},{5,20},{6,23},{7,22},{8,25},{9,... | collective-permute-start | bytes 6152 | tf_op jit(solution)/shard_map/ppermute | solution.py:119
  53.9 4.8 %collective-permute-start.12 = (f32[2,256]{1,0:T(2,128)S(1)}, f32[2,256]{1,0:T(2,128)S(1)}, u32[]{:S(2)}, u32[]{:S(2)}) collective-permute-start(f32[2,256]{1,0:T(2,128)S(1)} %add.166), channel_id=1, source_target_pairs={{0,25},{1,24},{2,27},{3,26},{4,29},{5,28},{6,31},{7,30},{8,17},{9,... | collective-permute-start | bytes 6152 | tf_op jit(solution)/shard_map/ppermute | solution.py:119
  60.2 3.9 %collective-permute-start.15 = (f32[2,256]{1,0:T(2,128)S(1)}, f32[2,256]{1,0:T(2,128)S(1)}, u32[]{:S(2)}, u32[]{:S(2)}) collective-permute-start(f32[2,256]{1,0:T(2,128)S(1)} %add_add_fusion.11), channel_id=1, source_target_pairs={{0,7},{1,6},{2,5},{3,4},{4,3},{5,2},{6,1},{7,0},{8,15},{9,14},{10,... | collective-permute-start | bytes 6152 | tf_op jit(solution)/shard_map/ppermute | solution.py:119
  64.5 92.8 %all-gather.6.cloned.1.call-start = ((), (), s32[]{:S(2)}) async-start(), calls=%async_computation | async-start | bytes 1081344 | tf_op jit(solution)/shard_map/all_gather | solution.py:496
  74.7 3.9 %collective-permute-start.18 = (f32[2,512]{1,0:T(2,128)S(1)}, f32[2,512]{1,0:T(2,128)S(1)}, u32[]{:S(2)}, u32[]{:S(2)}) collective-permute-start(f32[2,512]{1,0:T(2,128)S(1)} %add.173), channel_id=1, source_target_pairs={{0,17},{1,16},{2,19},{3,18},{4,21},{5,20},{6,23},{7,22},{8,25},{9,... | collective-permute-start | bytes 12296 | tf_op jit(solution)/shard_map/ppermute | solution.py:119
  75.6 4.8 %collective-permute-start.19 = (f32[2,512]{1,0:T(2,128)S(1)}, f32[2,512]{1,0:T(2,128)S(1)}, u32[]{:S(2)}, u32[]{:S(2)}) collective-permute-start(f32[2,512]{1,0:T(2,128)S(1)} %add.173), channel_id=1, source_target_pairs={{0,25},{1,24},{2,27},{3,26},{4,29},{5,28},{6,31},{7,30},{8,17},{9,... | collective-permute-start | bytes 12296 | tf_op jit(solution)/shard_map/ppermute | solution.py:119
  81.9 3.9 %collective-permute-start.22 = (f32[2,512]{1,0:T(2,128)S(1)}, f32[2,512]{1,0:T(2,128)S(1)}, u32[]{:S(2)}, u32[]{:S(2)}) collective-permute-start(f32[2,512]{1,0:T(2,128)S(1)} %add_add_fusion.7), channel_id=1, source_target_pairs={{0,7},{1,6},{2,5},{3,4},{4,3},{5,2},{6,1},{7,0},{8,15},{9,14},{10,... | collective-permute-start | bytes 12296 | tf_op jit(solution)/shard_map/ppermute | solution.py:119
  87.6 110.9 %all-gather.10.cloned.1.call-start = ((), (), s32[]{:S(2)}) async-start(), calls=%async_computation.2 | async-start | bytes 2293760 | tf_op jit(solution)/shard_map/all_gather | solution.py:498
  89.1 3.9 %collective-permute-start.25 = (f32[2,128]{1,0:T(2,128)S(1)}, f32[2,128]{1,0:T(2,128)S(1)}, u32[]{:S(2)}, u32[]{:S(2)}) collective-permute-start(f32[2,128]{1,0:T(2,128)S(1)} %add.180), channel_id=1, source_target_pairs={{0,17},{1,16},{2,19},{3,18},{4,21},{5,20},{6,23},{7,22},{8,25},{9,... | collective-permute-start | bytes 3080 | tf_op jit(solution)/shard_map/ppermute | solution.py:119
  89.8 4.8 %collective-permute-start.26 = (f32[2,128]{1,0:T(2,128)S(1)}, f32[2,128]{1,0:T(2,128)S(1)}, u32[]{:S(2)}, u32[]{:S(2)}) collective-permute-start(f32[2,128]{1,0:T(2,128)S(1)} %add.180), channel_id=1, source_target_pairs={{0,25},{1,24},{2,27},{3,26},{4,29},{5,28},{6,31},{7,30},{8,17},{9,... | collective-permute-start | bytes 3080 | tf_op jit(solution)/shard_map/ppermute | solution.py:119
  95.4 3.9 %collective-permute-start.29 = (f32[2,128]{1,0:T(2,128)S(1)}, f32[2,128]{1,0:T(2,128)S(1)}, u32[]{:S(2)}, u32[]{:S(2)}) collective-permute-start(f32[2,128]{1,0:T(2,128)S(1)} %add_add_fusion.13), channel_id=1, source_target_pairs={{0,7},{1,6},{2,5},{3,4},{4,3},{5,2},{6,1},{7,0},{8,15},{9,14},{10,... | collective-permute-start | bytes 3080 | tf_op jit(solution)/shard_map/ppermute | solution.py:119
  101.0 13.4 %collective-permute-start.38 = (f32[448,256]{1,0:T(8,128)S(1)}, f32[448,256]{1,0:T(8,128)S(1)}, u32[]{:S(2)}, u32[]{:S(2)}) collective-permute-start(f32[448,256]{1,0:T(8,128)S(1)} %get-tuple-element.138.refs_0_.refs_1_.refs_3_), channel_id=1, source_target_pairs={{0,2},{1,3},{2,0},{3,1},{4,6},{5,7},{6,4},{7,5},{8,10},{9,11},{10,... | collective-permute-start | bytes 1376264 | tf_op jit(solution)/shard_map/ppermute | solution.py:119
  106.2 4.0 %collective-permute-start.33 = (f32[8,256]{1,0:T(8,128)S(1)}, f32[8,256]{1,0:T(8,128)S(1)}, u32[]{:S(2)}, u32[]{:S(2)}) collective-permute-start(f32[8,256]{1,0:T(8,128)S(1)} %add.187), channel_id=1, source_target_pairs={{0,17},{1,16},{2,19},{3,18},{4,21},{5,20},{6,23},{7,22},{8,25},{9,... | collective-permute-start | bytes 24584 | tf_op jit(solution)/shard_map/ppermute | solution.py:119
  107.2 4.9 %collective-permute-start.34 = (f32[8,256]{1,0:T(8,128)S(1)}, f32[8,256]{1,0:T(8,128)S(1)}, u32[]{:S(2)}, u32[]{:S(2)}) collective-permute-start(f32[8,256]{1,0:T(8,128)S(1)} %add.187), channel_id=1, source_target_pairs={{0,25},{1,24},{2,27},{3,26},{4,29},{5,28},{6,31},{7,30},{8,17},{9,... | collective-permute-start | bytes 24584 | tf_op jit(solution)/shard_map/ppermute | solution.py:119
  114.4 5.8 %collective-permute-start.39 = (f32[448,256]{1,0:T(8,128)S(1)}, f32[448,256]{1,0:T(8,128)S(1)}, u32[]{:S(2)}, u32[]{:S(2)}) collective-permute-start(f32[448,256]{1,0:T(8,128)S(1)} %collective-permute-done.38.refs_1_), channel_id=1, source_target_pairs={{0,1},{1,0},{2,3},{3,2},{4,5},{5,4},{6,7},{7,6},{8,9},{9,8},{10,11... | collective-permute-start | bytes 1376264 | tf_op jit(solution)/shard_map/ppermute | solution.py:119
  116.1 4.1 %collective-permute-start.37 = (f32[8,256]{1,0:T(8,128)S(1)}, f32[8,256]{1,0:T(8,128)S(1)}, u32[]{:S(2)}, u32[]{:S(2)}) collective-permute-start(f32[8,256]{1,0:T(8,128)S(1)} %add_add_fusion.5), channel_id=1, source_target_pairs={{0,7},{1,6},{2,5},{3,4},{4,3},{5,2},{6,1},{7,0},{8,15},{9,14},{10,... | collective-permute-start | bytes 24584 | tf_op jit(solution)/shard_map/ppermute | solution.py:119
  117.9 8.0 %collective-permute-start.30 = (f32[448,256]{1,0:T(8,128)S(1)}, f32[448,256]{1,0:T(8,128)S(1)}, u32[]{:S(2)}, u32[]{:S(2)}) collective-permute-start(f32[448,256]{1,0:T(8,128)S(1)} %get-tuple-element.138.refs_0_.refs_1_.refs_3_), channel_id=1, source_target_pairs={{0,1},{1,0},{2,3},{3,2},{4,5},{5,4},{6,7},{7,6},{8,9},{9,8},{10,11... | collective-permute-start | bytes 1376264 | tf_op jit(solution)/shard_map/ppermute | solution.py:119
  125.4 10.4 %collective-permute-start.41 = (f32[448,256]{1,0:T(8,128)S(1)}, f32[448,256]{1,0:T(8,128)S(1)}, u32[]{:S(2)}, u32[]{:S(2)}) collective-permute-start(f32[448,256]{1,0:T(8,128)S(1)} %get-tuple-element.148), channel_id=1, source_target_pairs={{0,1},{1,0},{2,3},{3,2},{4,5},{5,4},{6,7},{7,6},{8,9},{9,8},{10,11... | collective-permute-start | bytes 1376264 | tf_op jit(solution)/shard_map/ppermute | solution.py:119
  132.4 4.4 %collective-permute-start.45 = (f32[8,256]{1,0:T(8,128)S(1)}, f32[8,256]{1,0:T(8,128)S(1)}, u32[]{:S(2)}, u32[]{:S(2)}) collective-permute-start(f32[8,256]{1,0:T(8,128)S(1)} %add.196), channel_id=1, source_target_pairs={{0,17},{1,16},{2,19},{3,18},{4,21},{5,20},{6,23},{7,22},{8,25},{9,... | collective-permute-start | bytes 24584 | tf_op jit(solution)/shard_map/ppermute | solution.py:119
  132.7 4.9 %collective-permute-start.46 = (f32[8,256]{1,0:T(8,128)S(1)}, f32[8,256]{1,0:T(8,128)S(1)}, u32[]{:S(2)}, u32[]{:S(2)}) collective-permute-start(f32[8,256]{1,0:T(8,128)S(1)} %add.196), channel_id=1, source_target_pairs={{0,25},{1,24},{2,27},{3,26},{4,29},{5,28},{6,31},{7,30},{8,17},{9,... | collective-permute-start | bytes 24584 | tf_op jit(solution)/shard_map/ppermute | solution.py:119
  135.4 12.7 %collective-permute-start.40 = (f32[448,256]{1,0:T(8,128)S(1)}, f32[448,256]{1,0:T(8,128)S(1)}, u32[]{:S(2)}, u32[]{:S(2)}) collective-permute-start(f32[448,256]{1,0:T(8,128)S(1)} %get-tuple-element.146), channel_id=1, source_target_pairs={{0,1},{1,0},{2,3},{3,2},{4,5},{5,4},{6,7},{7,6},{8,9},{9,8},{10,11... | collective-permute-start | bytes 1376264 | tf_op jit(solution)/shard_map/ppermute | solution.py:119
  135.8 12.9 %collective-permute-start.42 = (f32[448,256]{1,0:T(8,128)S(1)}, f32[448,256]{1,0:T(8,128)S(1)}, u32[]{:S(2)}, u32[]{:S(2)}) collective-permute-start(f32[448,256]{1,0:T(8,128)S(1)} %add.195), channel_id=1, source_target_pairs={{0,2},{1,3},{2,0},{3,1},{4,6},{5,7},{6,4},{7,5},{8,10},{9,11},{10,... | collective-permute-start | bytes 1376264 | tf_op jit(solution)/shard_map/ppermute | solution.py:119
  139.0 4.2 %collective-permute-start.49 = (f32[8,256]{1,0:T(8,128)S(1)}, f32[8,256]{1,0:T(8,128)S(1)}, u32[]{:S(2)}, u32[]{:S(2)}) collective-permute-start(f32[8,256]{1,0:T(8,128)S(1)} %add_add_fusion.3), channel_id=1, source_target_pairs={{0,7},{1,6},{2,5},{3,4},{4,3},{5,2},{6,1},{7,0},{8,15},{9,14},{10,... | collective-permute-start | bytes 24584 | tf_op jit(solution)/shard_map/ppermute | solution.py:119
  140.0 8.1 %collective-permute-start.47 = (f32[8,256]{1,0:T(8,128)S(1)}, f32[8,256]{1,0:T(8,128)S(1)}, u32[]{:S(2)}, u32[]{:S(2)}) collective-permute-start(f32[8,256]{1,0:T(8,128)S(1)} %add_add_fusion.3), channel_id=1, source_target_pairs={{0,3},{1,2},{2,1},{3,0},{4,7},{5,6},{6,5},{7,4},{8,11},{9,10},{10,... | collective-permute-start | bytes 24584 | tf_op jit(solution)/shard_map/ppermute | solution.py:119
  153.7 5.8 %collective-permute-start.52 = (f32[80,128]{1,0:T(8,128)S(1)}, f32[80,128]{1,0:T(8,128)S(1)}, u32[]{:S(2)}, u32[]{:S(2)}) collective-permute-start(f32[80,128]{1,0:T(8,128)S(1)} %add.203), channel_id=1, source_target_pairs={{0,17},{1,16},{2,19},{3,18},{4,21},{5,20},{6,23},{7,22},{8,25},{9,... | collective-permute-start | bytes 122888 | tf_op jit(solution)/shard_map/ppermute | solution.py:119
  154.9 5.3 %collective-permute-start.53 = (f32[80,128]{1,0:T(8,128)S(1)}, f32[80,128]{1,0:T(8,128)S(1)}, u32[]{:S(2)}, u32[]{:S(2)}) collective-permute-start(f32[80,128]{1,0:T(8,128)S(1)} %add.203), channel_id=1, source_target_pairs={{0,25},{1,24},{2,27},{3,26},{4,29},{5,28},{6,31},{7,30},{8,17},{9,... | collective-permute-start | bytes 122888 | tf_op jit(solution)/shard_map/ppermute | solution.py:119
  157.3 4.1 %collective-permute-start.51 = (f32[80,128]{1,0:T(8,128)S(1)}, f32[80,128]{1,0:T(8,128)S(1)}, u32[]{:S(2)}, u32[]{:S(2)}) collective-permute-start(f32[80,128]{1,0:T(8,128)S(1)} %add.203), channel_id=1, source_target_pairs={{0,9},{1,8},{2,11},{3,10},{4,13},{5,12},{6,15},{7,14},{8,1},{9,0},... | collective-permute-start | bytes 122888 | tf_op jit(solution)/shard_map/ppermute | solution.py:119
  162.3 4.3 %collective-permute-start.56 = (f32[80,128]{1,0:T(8,128)S(1)}, f32[80,128]{1,0:T(8,128)S(1)}, u32[]{:S(2)}, u32[]{:S(2)}) collective-permute-start(f32[80,128]{1,0:T(8,128)S(1)} %add_add_fusion.1), channel_id=1, source_target_pairs={{0,7},{1,6},{2,5},{3,4},{4,3},{5,2},{6,1},{7,0},{8,15},{9,14},{10,... | collective-permute-start | bytes 122888 | tf_op jit(solution)/shard_map/ppermute | solution.py:119
  163.6 4.4 %collective-permute-start.54 = (f32[80,128]{1,0:T(8,128)S(1)}, f32[80,128]{1,0:T(8,128)S(1)}, u32[]{:S(2)}, u32[]{:S(2)}) collective-permute-start(f32[80,128]{1,0:T(8,128)S(1)} %add_add_fusion.1), channel_id=1, source_target_pairs={{0,3},{1,2},{2,1},{3,0},{4,7},{5,6},{6,5},{7,4},{8,11},{9,10},{10,... | collective-permute-start | bytes 122888 | tf_op jit(solution)/shard_map/ppermute | solution.py:119
  174.6 12.8 %collective-permute-start.58 = (f32[448,256]{1,0:T(8,128)S(1)}, f32[448,256]{1,0:T(8,128)S(1)}, u32[]{:S(2)}, u32[]{:S(2)}) collective-permute-start(f32[448,256]{1,0:T(8,128)S(1)} %get-tuple-element.163.refs_0_), channel_id=1, source_target_pairs={{0,2},{1,3},{2,0},{3,1},{4,6},{5,7},{6,4},{7,5},{8,10},{9,11},{10,... | collective-permute-start | bytes 1376264 | tf_op jit(solution)/shard_map/ppermute | solution.py:119
  175.9 3.9 %collective-permute-start.61 = (f32[2,256]{1,0:T(2,128)S(1)}, f32[2,256]{1,0:T(2,128)S(1)}, u32[]{:S(2)}, u32[]{:S(2)}) collective-permute-start(f32[2,256]{1,0:T(2,128)S(1)} %add.210), channel_id=1, source_target_pairs={{0,17},{1,16},{2,19},{3,18},{4,21},{5,20},{6,23},{7,22},{8,25},{9,... | collective-permute-start | bytes 6152 | tf_op jit(solution)/shard_map/ppermute | solution.py:119
  175.9 4.8 %collective-permute-start.62 = (f32[2,256]{1,0:T(2,128)S(1)}, f32[2,256]{1,0:T(2,128)S(1)}, u32[]{:S(2)}, u32[]{:S(2)}) collective-permute-start(f32[2,256]{1,0:T(2,128)S(1)} %add.210), channel_id=1, source_target_pairs={{0,25},{1,24},{2,27},{3,26},{4,29},{5,28},{6,31},{7,30},{8,17},{9,... | collective-permute-start | bytes 6152 | tf_op jit(solution)/shard_map/ppermute | solution.py:119
  181.7 4.0 %collective-permute-start.65 = (f32[2,256]{1,0:T(2,128)S(1)}, f32[2,256]{1,0:T(2,128)S(1)}, u32[]{:S(2)}, u32[]{:S(2)}) collective-permute-start(f32[2,256]{1,0:T(2,128)S(1)} %add_add_fusion.9), channel_id=1, source_target_pairs={{0,7},{1,6},{2,5},{3,4},{4,3},{5,2},{6,1},{7,0},{8,15},{9,14},{10,... | collective-permute-start | bytes 6152 | tf_op jit(solution)/shard_map/ppermute | solution.py:119
  184.1 3.9 %collective-permute-start.78 = (f32[448,128]{1,0:T(8,128)}, f32[448,128]{1,0:T(8,128)S(1)}, u32[]{:S(2)}, u32[]{:S(2)}) collective-permute-start(f32[448,128]{1,0:T(8,128)} %copy-done.11), channel_id=1, source_target_pairs={{0,1},{1,0},{2,3},{3,2},{4,5},{5,4},{6,7},{7,6},{8,9},{9,8},{10,11... | collective-permute-start | bytes 688136 | tf_op jit(solution)/shard_map/ppermute | solution.py:119
  184.5 8.4 %collective-permute-start.79 = (f32[448,128]{1,0:T(8,128)S(1)}, f32[448,128]{1,0:T(8,128)S(1)}, u32[]{:S(2)}, u32[]{:S(2)}) collective-permute-start(f32[448,128]{1,0:T(8,128)S(1)} %get-tuple-element.195), channel_id=1, source_target_pairs={{0,2},{1,3},{2,0},{3,1},{4,6},{5,7},{6,4},{7,5},{8,10},{9,11},{10,... | collective-permute-start | bytes 688136 | tf_op jit(solution)/shard_map/ppermute | solution.py:119
  185.7 10.6 %collective-permute-start.80 = (f32[448,128]{1,0:T(8,128)S(1)}, f32[448,128]{1,0:T(8,128)S(1)}, u32[]{:S(2)}, u32[]{:S(2)}) collective-permute-start(f32[448,128]{1,0:T(8,128)S(1)} %get-tuple-element.196), channel_id=1, source_target_pairs={{0,3},{1,2},{2,1},{3,0},{4,7},{5,6},{6,5},{7,4},{8,11},{9,10},{10,... | collective-permute-start | bytes 688136 | tf_op jit(solution)/shard_map/ppermute | solution.py:119
  186.7 20.8 %collective-permute-start.59 = (f32[448,256]{1,0:T(8,128)S(1)}, f32[448,256]{1,0:T(8,128)S(1)}, u32[]{:S(2)}, u32[]{:S(2)}) collective-permute-start(f32[448,256]{1,0:T(8,128)S(1)} %get-tuple-element.163.refs_0_), channel_id=1, source_target_pairs={{0,1},{1,0},{2,3},{3,2},{4,5},{5,4},{6,7},{7,6},{8,9},{9,8},{10,11... | collective-permute-start | bytes 1376264 | tf_op jit(solution)/shard_map/ppermute | solution.py:119
  187.4 20.1 %collective-permute-start.66 = (f32[448,256]{1,0:T(8,128)S(1)}, f32[448,256]{1,0:T(8,128)S(1)}, u32[]{:S(2)}, u32[]{:S(2)}) collective-permute-start(f32[448,256]{1,0:T(8,128)S(1)} %collective-permute-done.58.refs_1_), channel_id=1, source_target_pairs={{0,1},{1,0},{2,3},{3,2},{4,5},{5,4},{6,7},{7,6},{8,9},{9,8},{10,11... | collective-permute-start | bytes 1376264 | tf_op jit(solution)/shard_map/ppermute | solution.py:119
  188.1 15.6 %collective-permute-start.67 = (f32[8,128]{1,0:T(8,128)S(1)}, f32[8,128]{1,0:T(8,128)S(1)}, u32[]{:S(2)}, u32[]{:S(2)}) collective-permute-start(f32[8,128]{1,0:T(8,128)S(1)} %get-tuple-element.168), channel_id=1, source_target_pairs={{0,1},{1,0},{2,3},{3,2},{4,5},{5,4},{6,7},{7,6},{8,9},{9,8},{10,11... | collective-permute-start | bytes 12296 | tf_op jit(solution)/shard_map/ppermute | solution.py:119
  192.9 12.3 %collective-permute-start.68 = (f32[8,128]{1,0:T(8,128)S(1)}, f32[8,128]{1,0:T(8,128)S(1)}, u32[]{:S(2)}, u32[]{:S(2)}) collective-permute-start(f32[8,128]{1,0:T(8,128)S(1)} %get-tuple-element.170), channel_id=1, source_target_pairs={{0,2},{1,3},{2,0},{3,1},{4,6},{5,7},{6,4},{7,5},{8,10},{9,11},{10,... | collective-permute-start | bytes 12296 | tf_op jit(solution)/shard_map/ppermute | solution.py:119
  197.1 8.2 %collective-permute-start.69 = (f32[8,128]{1,0:T(8,128)S(1)}, f32[8,128]{1,0:T(8,128)S(1)}, u32[]{:S(2)}, u32[]{:S(2)}) collective-permute-start(f32[8,128]{1,0:T(8,128)S(1)} %get-tuple-element.172), channel_id=1, source_target_pairs={{0,3},{1,2},{2,1},{3,0},{4,7},{5,6},{6,5},{7,4},{8,11},{9,10},{10,... | collective-permute-start | bytes 12296 | tf_op jit(solution)/shard_map/ppermute | solution.py:119
  203.7 10.0 %collective-permute-start.81 = (f32[576,128]{1,0:T(8,128)S(1)}, f32[576,128]{1,0:T(8,128)S(1)}, u32[]{:S(2)}, u32[]{:S(2)}) collective-permute-start(f32[576,128]{1,0:T(8,128)S(1)} %get-tuple-element.198), channel_id=1, source_target_pairs={{0,4},{4,0},{8,12},{12,8},{16,20},{20,16},{24,28},{28,24},{1,5},{5... | collective-permute-start | bytes 884744 | tf_op jit(solution)/shard_map/ppermute | solution.py:119
  211.6 13.4 %collective-permute-start.70 = (f32[576,128]{1,0:T(8,128)S(1)}, f32[576,128]{1,0:T(8,128)S(1)}, u32[]{:S(2)}, u32[]{:S(2)}) collective-permute-start(f32[576,128]{1,0:T(8,128)S(1)} %get-tuple-element.188), channel_id=1, source_target_pairs={{0,4},{4,0},{8,12},{12,8},{16,20},{20,16},{24,28},{28,24},{1,5},{5... | collective-permute-start | bytes 884744 | tf_op jit(solution)/shard_map/ppermute | solution.py:119
  214.3 5.1 %collective-permute-start.82 = (f32[144,128]{1,0:T(8,128)S(1)}, f32[144,128]{1,0:T(8,128)S(1)}, u32[]{:S(2)}, u32[]{:S(2)}) collective-permute-start(f32[144,128]{1,0:T(8,128)S(1)} %get-tuple-element.200), channel_id=1, source_target_pairs={{0,8},{4,12},{8,0},{12,4},{16,24},{20,28},{24,16},{28,20},{1,9},{5... | collective-permute-start | bytes 221192 | tf_op jit(solution)/shard_map/ppermute | solution.py:119
  214.7 8.3 %collective-permute-start.83 = (f32[144,128]{1,0:T(8,128)S(1)}, f32[144,128]{1,0:T(8,128)S(1)}, u32[]{:S(2)}, u32[]{:S(2)}) collective-permute-start(f32[144,128]{1,0:T(8,128)S(1)} %get-tuple-element.201), channel_id=1, source_target_pairs={{0,16},{4,20},{8,24},{12,28},{16,0},{20,4},{24,8},{28,12},{1,17},{... | collective-permute-start | bytes 221192 | tf_op jit(solution)/shard_map/ppermute | solution.py:119
  216.4 6.6 %collective-permute-start.84 = (f32[144,128]{1,0:T(8,128)S(1)}, f32[144,128]{1,0:T(8,128)S(1)}, u32[]{:S(2)}, u32[]{:S(2)}) collective-permute-start(f32[144,128]{1,0:T(8,128)S(1)} %get-tuple-element.202), channel_id=1, source_target_pairs={{0,24},{4,28},{8,16},{12,20},{16,8},{20,12},{24,0},{28,4},{1,25},{... | collective-permute-start | bytes 221192 | tf_op jit(solution)/shard_map/ppermute | solution.py:119
  223.6 18.4 %collective-permute-start.85 = (f32[144,128]{1,0:T(8,128)S(1)}, f32[144,128]{1,0:T(8,128)S(1)}, u32[]{:S(2)}, u32[]{:S(2)}) collective-permute-start(f32[144,128]{1,0:T(8,128)S(1)} %shard_map.311.refs_0_), channel_id=1, source_target_pairs={{0,8},{4,12},{8,0},{12,4},{16,24},{20,28},{24,16},{28,20},{1,9},{5... | collective-permute-start | bytes 221192 | tf_op jit(solution)/shard_map/ppermute | solution.py:119
  225.6 5.4 %collective-permute-start.71 = (f32[144,128]{1,0:T(8,128)S(1)}, f32[144,128]{1,0:T(8,128)S(1)}, u32[]{:S(2)}, u32[]{:S(2)}) collective-permute-start(f32[144,128]{1,0:T(8,128)S(1)} %get-tuple-element.190), channel_id=1, source_target_pairs={{0,8},{4,12},{8,0},{12,4},{16,24},{20,28},{24,16},{28,20},{1,9},{5... | collective-permute-start | bytes 221192 | tf_op jit(solution)/shard_map/ppermute | solution.py:119
  226.4 12.3 %collective-permute-start.72 = (f32[144,128]{1,0:T(8,128)S(1)}, f32[144,128]{1,0:T(8,128)S(1)}, u32[]{:S(2)}, u32[]{:S(2)}) collective-permute-start(f32[144,128]{1,0:T(8,128)S(1)} %get-tuple-element.191), channel_id=1, source_target_pairs={{0,16},{4,20},{8,24},{12,28},{16,0},{20,4},{24,8},{28,12},{1,17},{... | collective-permute-start | bytes 221192 | tf_op jit(solution)/shard_map/ppermute | solution.py:119
  228.1 10.6 %collective-permute-start.73 = (f32[144,128]{1,0:T(8,128)S(1)}, f32[144,128]{1,0:T(8,128)S(1)}, u32[]{:S(2)}, u32[]{:S(2)}) collective-permute-start(f32[144,128]{1,0:T(8,128)S(1)} %get-tuple-element.192), channel_id=1, source_target_pairs={{0,24},{4,28},{8,16},{12,20},{16,8},{20,12},{24,0},{28,4},{1,25},{... | collective-permute-start | bytes 221192 | tf_op jit(solution)/shard_map/ppermute | solution.py:119
  230.7 13.8 %collective-permute-start.86 = (f32[144,128]{1,0:T(8,128)S(1)}, f32[144,128]{1,0:T(8,128)S(1)}, u32[]{:S(2)}, u32[]{:S(2)}) collective-permute-start(f32[144,128]{1,0:T(8,128)S(1)} %shard_map.311.refs_0_), channel_id=1, source_target_pairs={{0,16},{4,20},{8,24},{12,28},{16,0},{20,4},{24,8},{28,12},{1,17},{... | collective-permute-start | bytes 221192 | tf_op jit(solution)/shard_map/ppermute | solution.py:119
  231.0 13.5 %collective-permute-start.87 = (f32[144,128]{1,0:T(8,128)S(1)}, f32[144,128]{1,0:T(8,128)S(1)}, u32[]{:S(2)}, u32[]{:S(2)}) collective-permute-start(f32[144,128]{1,0:T(8,128)S(1)} %shard_map.311.refs_0_), channel_id=1, source_target_pairs={{0,24},{4,28},{8,16},{12,20},{16,8},{20,12},{24,0},{28,4},{1,25},{... | collective-permute-start | bytes 221192 | tf_op jit(solution)/shard_map/ppermute | solution.py:119
  239.2 6.8 %collective-permute-start.74 = (f32[144,128]{1,0:T(8,128)S(1)}, f32[144,128]{1,0:T(8,128)S(1)}, u32[]{:S(2)}, u32[]{:S(2)}) collective-permute-start(f32[144,128]{1,0:T(8,128)S(1)} %shard_map.306.refs_0_), channel_id=1, source_target_pairs={{0,8},{4,12},{8,0},{12,4},{16,24},{20,28},{24,16},{28,20},{1,9},{5... | collective-permute-start | bytes 221192 | tf_op jit(solution)/shard_map/ppermute | solution.py:119
  241.4 5.9 %collective-permute-start.75 = (f32[144,128]{1,0:T(8,128)S(1)}, f32[144,128]{1,0:T(8,128)S(1)}, u32[]{:S(2)}, u32[]{:S(2)}) collective-permute-start(f32[144,128]{1,0:T(8,128)S(1)} %shard_map.306.refs_0_), channel_id=1, source_target_pairs={{0,16},{4,20},{8,24},{12,28},{16,0},{20,4},{24,8},{28,12},{1,17},{... | collective-permute-start | bytes 221192 | tf_op jit(solution)/shard_map/ppermute | solution.py:119
  242.0 6.3 %collective-permute-start.76 = (f32[144,128]{1,0:T(8,128)S(1)}, f32[144,128]{1,0:T(8,128)S(1)}, u32[]{:S(2)}, u32[]{:S(2)}) collective-permute-start(f32[144,128]{1,0:T(8,128)S(1)} %shard_map.306.refs_0_), channel_id=1, source_target_pairs={{0,24},{4,28},{8,16},{12,20},{16,8},{20,12},{24,0},{28,4},{1,25},{... | collective-permute-start | bytes 221192 | tf_op jit(solution)/shard_map/ppermute | solution.py:119
  245.1 11.7 %collective-permute-start.88 = (f32[576,128]{1,0:T(8,128)S(1)}, f32[576,128]{1,0:T(8,128)S(1)}, u32[]{:S(2)}, u32[]{:S(2)}) collective-permute-start(f32[576,128]{1,0:T(8,128)S(1)} %shard_map.312.refs_0_), channel_id=1, source_target_pairs={{0,4},{4,0},{8,12},{12,8},{16,20},{20,16},{24,28},{28,24},{1,5},{5... | collective-permute-start | bytes 884744 | tf_op jit(solution)/shard_map/ppermute | solution.py:119
  248.8 9.3 %collective-permute-start.77 = (f32[576,128]{1,0:T(8,128)S(1)}, f32[576,128]{1,0:T(8,128)S(1)}, u32[]{:S(2)}, u32[]{:S(2)}) collective-permute-start(f32[576,128]{1,0:T(8,128)S(1)} %shard_map.307.refs_0_), channel_id=1, source_target_pairs={{0,4},{4,0},{8,12},{12,8},{16,20},{20,16},{24,28},{28,24},{1,5},{5... | collective-permute-start | bytes 884744 | tf_op jit(solution)/shard_map/ppermute | solution.py:119
  (53 other events, 357.8 us)
Sparse Core Ops, SparseCore 0:
  64.6 15.2 all-gather.7
  87.8 52.7 all-gather.5
  142.7 19.9 all-gather.9

commit v2 on v1

--- a/solution.py
+++ b/solution.py
@@ -52,14 +52,19 @@
     )
 
 
-def call(body, counts, ins, outs, scratch=(), flops=0, far=(), far_out=()):
-    far, far_out = sorted(far), sorted(far_out)
+def call(body, counts, ins, outs, scratch=(), flops=0, far=(), far_out=(), lazy=False):
+    cuts = far if isinstance(far, dict) else {k: None for k in far}
+    far, far_out = sorted(cuts), sorted(far_out)
     moved = sum(a.size * a.dtype.itemsize for a in ins) + sum(
         int(jnp.dtype(d).itemsize) * functools.reduce(lambda x, y: x * y, s, 1) for s, d in outs
     )
     vmem, hbm = pl.BlockSpec(memory_space=pltpu.VMEM), pl.BlockSpec(memory_space=pltpu.HBM)
     own_scratch = len(scratch)
-    held = [pltpu.VMEM(ins[k].shape, ins[k].dtype) for k in far] + [pltpu.VMEM(*outs[k]) for k in far_out]
+    def shape_of(k):
+        shape, part = ins[k].shape, cuts[k]
+        return shape if part is None else shape[:1] + (part.stop - part.start,) + shape[2:]
+
+    held = [pltpu.VMEM(shape_of(k), ins[k].dtype) for k in far] + [pltpu.VMEM(*outs[k]) for k in far_out]
     sems = [pltpu.SemaphoreType.DMA] * len(held)
 
     def kernel(s, *refs):
@@ -69,7 +74,9 @@
         scr, bufs, sem = rest[:own_scratch], rest[own_scratch : own_scratch + len(held)], rest[own_scratch + len(held) :]
         copies = []
         for i, k in enumerate(far):
-            copies.append(pltpu.make_async_copy(refs_in[k], bufs[i], sem[i]))
+            part = cuts[k]
+            src = refs_in[k] if part is None else refs_in[k].at[:, part.start : part.stop, :]
+            copies.append(pltpu.make_async_copy(src, bufs[i], sem[i]))
             copies[-1].start()
             refs_in[k] = bufs[i]
         homes = []
@@ -77,9 +84,12 @@
             i += len(far)
             homes.append(pltpu.make_async_copy(bufs[i], refs_out[k], sem[i]))
             refs_out[k] = bufs[i]
-        for copy in copies:
-            copy.wait()
-        body(s, *refs_in, *refs_out, *scr)
+        if lazy:
+            body(s, *refs_in, *refs_out, *scr, arrive=lambda k: copies[far.index(k)].wait())
+        else:
+            for copy in copies:
+                copy.wait()
+            body(s, *refs_in, *refs_out, *scr)
         for copy in homes:
             copy.start()
         for copy in homes:
@@ -118,10 +128,15 @@
         n = {"dp": nd, "chan": nc}[axis] if isinstance(axis, str) else nd * nc
         return lax.ppermute(x, axis, [(i, i ^ k) for i in range(n)])
 
-    def sum_steps(x):
+    def after(x, *deps):
+        return lax.optimization_barrier((x,) + deps)[0]
+
+    def sum_steps(x, before_last=()):
         out = [x]
-        for g in sum_groups:
+        for i, g in enumerate(sum_groups):
             x = out[-1]
+            if before_last and i == len(sum_groups) - 1:
+                x = after(x, *before_last)
             got = [swap(x, both, k) for k in g]
             x = x + got[0]
             out.append(x + (got[1] + got[2]) if len(g) == 3 else x)
@@ -129,9 +144,6 @@
 
     def sum_all(x):
         return sum_steps(x)[-1]
-
-    def after(x, *deps):
-        return lax.optimization_barrier((x,) + deps)[0]
 
     def pick(x, i):
         return lax.dynamic_index_in_dim(x, i, 0, False)
@@ -161,9 +173,18 @@
     def padded_rows(rows):
         return -(-rows // (8 * nd)) * 8 * nd
 
-    def big_sum_dp(counts, chunks):
+    def sum_dp(counts, chunks, write, outs, before=()):
+        stages = []
+
+        def exchanged(first, rest, g):
+            got = [first] + [swap(z, "dp", m) for z, m in zip(rest, masks(g)[1:])]
+            k = len(stages)
+            if k < len(before) and before[k]:
+                got[0] = after(got[0], *before[k])
+            return got
+
         for i, g in enumerate(groups):
-            got = [chunks[0]] + [swap(z, "dp", m) for z, m in zip(chunks[1:], masks(g)[1:])]
+            got = exchanged(chunks[0], chunks[1:], g)
             rows = got[0].shape[0]
             last = i == len(groups) - 1
 
@@ -184,18 +205,25 @@
                 [((rows, 128), F32)] if last else chunk_outs(rows, groups[i + 1]),
                 [] if last else [pltpu.VMEM((rows, 128), F32)],
             )
+            stages.append(chunks[0])
         (x,) = chunks
         for g in groups[::-1]:
-            got = [x] + [swap(x, "dp", m) for m in masks(g)[1:]]
+            got = exchanged(x, [x] * (2 ** len(g) - 1), g)
             rows = x.shape[0]
-
-            def join_body(s, *refs, g=g, rows=rows):
+            last = g is groups[0]
+
+            def join_body(s, *refs, n=len(got), g=g, rows=rows, last=last):
                 at, _ = place_in(g)
-                for m, z in enumerate(refs[:-1]):
+                for m, z in enumerate(refs[:n]):
                     refs[-1][pl.ds(pl.multiple_of((at ^ m) * rows, 8), rows), :] = z[...]
-
-            (x,) = call(join_body, counts, got, [((rows * len(got), 128), F32)])
-        return x
+                if last:
+                    write(refs[-1], *refs[n:-1])
+
+            whole = ((rows * len(got), 128), F32)
+            if last:
+                return call(join_body, counts, got, outs, [pltpu.VMEM(*whole)])
+            (x,) = call(join_body, counts, got, [whole])
+            stages.append(x)
 
     def quarter_of(chan):
         q = chan * 0
@@ -284,18 +312,21 @@
                     for i in range(lb):
                         ref[place_of(h, i, b, r), :] = scr[b * edge + h, :edge, i * 128 : (i + 1) * 128]
 
+        def mine_of(ref):
+            c, out = me()[0], ref[0:2]
+            for k in range(1, nc):
+                out = jnp.where(c == k, ref[2 * k : 2 * k + 2], out)
+            return out
+
         feats, gouts = native(features_in), native(grad_out)
         quarter_scratch = pltpu.VMEM((own * edge, PAD, win), F32)
 
         wt = split_weight.transpose(0, 1, 3, 4, 2).reshape(-1, half)
 
-        wt_c, wt_y = swap(wt, "chan", 1), swap(wt, "chan", 2)
-
-        def pack(att_w, sq_w, rg, rs, sg, ss, ab, eg):
+
+        def pack(rg, rs, sg, ss, ab, eg):
             return jnp.concatenate(
                 [
-                    att_w.transpose(1, 2, 0).reshape(2 * lw, inner),
-                    sq_w,
                     sg.reshape(1, -1),
                     ss.reshape(1, -1),
                     ab.reshape(1, -1),
@@ -308,25 +339,27 @@
         nw = 9 * half
 
         def reduce_body(rels, s, x_ref, w_ref, *refs):
-            outs, scr = refs[:-1], refs[-1]
+            n, scr = len(rels), refs[-1]
             w = split3(w_ref[...])
-            for o, r in zip(outs, rels):
-                x = load_quarter(x_ref, scr, r, mask_of(valid(s, r), R, win, edge))
-                o[...] = mm6(split3(x), w)
-
-        def reduce_call(rels):
+            for k, r in enumerate(rels):
+                x = split3(load_quarter(x_ref, scr, r, mask_of(valid(s, r), R, win, edge)))
+                refs[n + k][...] = x[0]
+                refs[k][...] = mm6(x, w)
+
+        def reduce_call(rels, feats=feats):
             return call(
                 functools.partial(reduce_body, rels),
                 image_counts,
                 [feats, reduce_weight],
-                [((R, mid), F32)] * len(rels),
+                [((R, mid), F32)] * len(rels) + [((R, win), BF16)] * len(rels),
                 [quarter_scratch],
                 flops=12 * R * win * mid * len(rels),
                 far=(0, 1),
+                far_out=(len(rels), len(rels) + 1),
             )
 
-        p3, p1 = reduce_call((3, 1))
-        p2, p0 = reduce_call((2, 0))
+        p3, p1, x3, x1 = reduce_call((3, 1))
+        p2, p0, x2, x0 = reduce_call((2, 0))
         y1 = p1 + swap(p3, "chan", 1)
         ys = swap(y1, "chan", 2)
         rc = swap(p2, "chan", 1)
@@ -336,116 +369,117 @@
             return [x, y, swap(x, "chan", 1), swap(y if gate is None else after(y, gate), "chan", 1)]
 
         small = lax.optimization_barrier(
-            (
-                y1,
-                attend_weight,
-                squeeze_weight,
-                reduce_gain,
-                reduce_shift,
-                split_gain,
-                split_shift,
-                attend_bias,
-                expand_gain,
-            )
+            (y1, reduce_gain, reduce_shift, split_gain, split_shift, attend_bias, expand_gain)
         )
         ps = pack(*small[1:])
-        wt_r = [wt, wt_y, wt_c, swap(after(wt_y, y1), "chan", 1)]
-        ps_all = gather3(ps)
-
-        def pa_body(s, p0, p1, p2, p3, wat, vec, wsq, g3, scr):
-            c, _ = me()
-            scr[c] = p0[...]
-            scr[c ^ 2] = p1[...]
-            scr[c ^ 1] = p2[...]
-            scr[c ^ 3] = p3[...]
-            lo = 2 * lw + lw
+
+        wt_y = swap(after(wt, ys), "chan", 2)
+        wt_r = [wt, wt_y, swap(wt, "chan", 1), swap(wt_y, "chan", 1)]
+
+        small = lax.optimization_barrier((y1, expand_weight, attend_weight, squeeze_weight))
+        pw = jnp.concatenate(
+            [small[1][:, i * 128 : (i + 1) * 128] for i in range(lb)]
+            + [small[2].transpose(1, 2, 0).reshape(2 * lw, inner), small[3]]
+        )
+        CHAN_REL = (0, 2, 1, 3)
+
+        nl = mid // 128
+
+        def red_body(s, a, b, y, ps, red, sums):
+            v = a[...] + b[...] + y[...]
+            red[...] = v
+            sums[...] = jnp.zeros((8 + 8 * nc, 128), F32)
+            for k, z in enumerate((colsum(v), colsum(v * v))):
+                for i in range(nl):
+                    sums[k * nl + i : k * nl + i + 1, :] = z[:, i * 128 : (i + 1) * 128]
+            sums[pl.ds(pl.multiple_of(8 + 8 * me()[0], 8), 8), :] = ps[...]
+
+        red, s1 = call(red_body, image_counts, [p0, rc, ys, ps], [((R, mid), F32), ((8 + 8 * nc, 128), F32)])
+        s1_steps = sum_steps(s1, (wt_y,))
+
+        def vec_body(s, sums, s1, vec, g3):
+            for k in range(2):
+                for i in range(nl):
+                    s1[k : k + 1, i * 128 : (i + 1) * 128] = sums[k * nl + i : k * nl + i + 1, :]
+            own_of = [sums[8 + 8 * k : 16 + 8 * k, :] * (1.0 / nd) for k in range(nc)]
             lane = lax.broadcasted_iota(jnp.int32, (8, 2 * lw), 1)
             for pair in range(nc // 2):
-                a, b = scr[2 * pair, lo : lo + 8, :], scr[2 * pair + 1, lo : lo + 8, :]
+                a, b = own_of[2 * pair], own_of[2 * pair + 1]
                 cols = slice(pair * 2 * lw, (pair + 1) * 2 * lw)
                 vec[0, :, cols] = jnp.where(lane < lw, a, pltpu.roll(b, lw, 1))
                 vec[1, :, cols] = jnp.where(lane < lw, pltpu.roll(a, lw, 1), b)
             g3[...] = jnp.zeros((8, win), F32)
             for k in range(nc):
-                rows = slice(k * lw, (k + 1) * lw)
-                for r in range(2):
-                    wat[r, rows, :] = scr[k, r * lw : (r + 1) * lw, :]
-                wsq[rows, :] = scr[k, 2 * lw : lo, :]
                 for i in range(win // (2 * lw)):
-                    g3[k : k + 1, i * 2 * lw : (i + 1) * 2 * lw] = scr[k, lo + 4 + i : lo + 5 + i, :]
-
-        wat, vec, wsq, g3 = call(
-            pa_body,
-            image_counts,
-            ps_all,
-            [((2, mid, inner), F32), ((2, 8, mid), F32), ((mid, inner), F32), ((8, win), F32)],
-            [pltpu.VMEM((nc,) + ps.shape, F32)],
-        )
-
-        CHAN_REL = (0, 2, 1, 3)
-
-        def wt_body(s, v0, v1, v2, v3, w1, w2, w3, w1_home):
-            for rel, ref in enumerate((v0, v1, v2, v3)):
-                rows = pl.ds(pl.multiple_of((me()[0] ^ CHAN_REL[rel]) * lw, lw), lw)
-                for t in range(9):
-                    for r in range(2):
-                        at = t * 2 * lw + r * lw
-                        for o, z in zip((w1, w2, w3), split3(ref[at : at + lw, :])):
-                            o[r, rows, t * half : (t + 1) * half] = z
-            w1_home[...] = w1[...]
-
-        w1, w2, w3, w1_home = call(
-            wt_body, image_counts, wt_r, [((2, mid, nw), BF16)] * 4, far=(0,), far_out=(3,)
-        )
-
-        def red_body(s, a, b, y, red, sums):
-            v = a[...] + b[...] + y[...]
-            red[...] = v
-            sums[0:1] = colsum(v)
-            sums[1:2] = colsum(v * v)
-
-        red, s1 = call(red_body, image_counts, [p0, rc, after(ys, vec, w1)], [((R, mid), F32), ((2, mid), F32)])
-        s1_steps = sum_steps(s1)
-        s1 = s1_steps[-1]
+                    g3[k : k + 1, i * 2 * lw : (i + 1) * 2 * lw] = own_of[k][4 + i : 5 + i, :]
+
+        s1, vec, g3 = call(
+            vec_body, image_counts, [s1_steps[-1]], [((2, mid), F32), ((2, 8, mid), F32), ((8, win), F32)]
+        )
+
+        pw_all = lax.all_gather(after(pw, s1_steps[-2], wt_y), "chan")
+        WE = slice(0, lb * mid)
+        WAT = slice(lb * mid, lb * mid + 2 * lw)
+        WSQ = slice(lb * mid + 2 * lw, lb * mid + 3 * lw)
+
+        def we_of(ref, k):
+            return jnp.concatenate([ref[k, i * mid : (i + 1) * mid, :] for i in range(lb)], axis=1)
+
+        def wat_of(ref, r):
+            return jnp.concatenate([ref[k, r * lw : (r + 1) * lw, :] for k in range(nc)], axis=0)
+
+        def wsq_of(ref):
+            return ref[...].reshape(mid, inner)
 
         def taps_in(z, scrs, n):
             w = z.shape[1]
             rows = n * span
             for v in range(3):
                 zz = z if v == 1 else pltpu.roll(z, 1 if v == 0 else rows - 1, 0)
-                parts = split3(zz) if len(scrs) == 3 else [zz.astype(BF16)]
+                parts = split2(zz) if len(scrs) == 2 else [zz.astype(BF16)]
                 for scr, part in zip(scrs, parts):
                     scr[v, :, 0] = jnp.zeros((n, PAD, w), BF16)
                     scr[v, :, edge + 1] = jnp.zeros((n, PAD, w), BF16)
                     scr[v, :, 1 : edge + 1] = part.reshape(n, edge, PAD, w)
 
-        def conv_body(s, red, sums, vec, w1, w2, w3, out, sums2, za, zb, zc):
+        def conv_body(s, red, sums, vec, v0, v1, v2, v3, out, sums2, w1, za, zb, w2, arrive):
             avg, inv, _ = stats(sums, s)
             mask = mask_of(valid(s, 0), R, mid, edge)
             z = jnp.maximum((red[...] - avg) * inv * vec[0, 3:4] + vec[1, 3:4], 0.0)
             z = jnp.where(mask, z, 0.0)
-            taps_in(z, (za, zb, zc), own)
+            taps_in(z, (za, zb), own)
+            for rel, ref in enumerate((v0, v1, v2, v3)):
+                arrive(3 + rel)
+                rows = pl.ds(pl.multiple_of((me()[0] ^ CHAN_REL[rel]) * lw, lw), lw)
+                for t in range(9):
+                    for r in range(2):
+                        at = t * 2 * lw + r * lw
+                        for o, z in zip((w1, w2), split2(ref[at : at + lw, :])):
+                            o[r, rows, t * half : (t + 1) * half] = z
             for r in range(2):
                 cols = slice(r * half, (r + 1) * half)
                 lhs = [
                     jnp.concatenate([z[v, :, u : u + edge, :, cols].reshape(R, half) for u, v in TAPS], axis=1)
-                    for z in (za, zb, zc)
+                    for z in (za, zb)
                 ]
-                y = mm6(lhs, (w1[r], w2[r], w3[r]), ((1,), (1,)))
+                y = mm3(lhs, (w1[r], w2[r]), ((1,), (1,)))
                 out[:, r * mid : (r + 1) * mid] = y
                 y = jnp.where(mask, y, 0.0)
                 sums2[0:1, r * mid : (r + 1) * mid] = colsum(y)
                 sums2[1:2, r * mid : (r + 1) * mid] = colsum(y * y)
 
-        spl, s2 = call(
+        spl, s2, w1 = call(
             conv_body,
             image_counts,
-            [red, s1, vec, w1, w2, w3],
-            [((R, 2 * mid), F32), ((2, 2 * mid), F32)],
-            [pltpu.VMEM((3, own, PAD, PAD, mid), BF16)] * 3,
-            flops=24 * R * nw * mid,
-        )
-        we_all = lax.all_gather(after(expand_weight, s1), "chan")
+            [red, s1, vec] + wt_r,
+            [((R, 2 * mid), F32), ((2, 2 * mid), F32), ((2, mid, nw), BF16)],
+            [pltpu.VMEM((3, own, PAD, PAD, mid), BF16)] * 2 + [pltpu.VMEM((2, mid, nw), BF16)],
+            flops=12 * R * nw * mid,
+            far=(3, 4, 5, 6),
+            far_out=(2,),
+            lazy=True,
+        )
+
         s2_steps = sum_steps(s2)
         s2 = s2_steps[-1]
 
@@ -464,7 +498,7 @@
         BLOCK = max(64, 4 * nb * own)
         ND = nd * nc
 
-        def pool_body(s, spl, sums, vec, wsq, c12, sq, sfc):
+        def pool_body(s, spl, sums, vec, wsq, c12, sq, sfc, arrive):
             mask = mask_of(valid(s, 0), R, mid, edge)
             n = recip(s, area)
             pooled = [0.0] * own
@@ -480,7 +514,8 @@
                             c12[k * own + b : k * own + b + 1, :] = z[b][:, sl]
                     pooled[b] = pooled[b] + vec[r, 0:1] * c2[b] + vec[r, 1:2] * c1[b]
             p = jnp.concatenate(pooled + [jnp.zeros((8 - own, mid), F32)], axis=0) * (1.0 / area)
-            v = exact(p, wsq[...])
+            arrive(3)
+            v = exact(p, wsq_of(wsq))
             sq[...] = v
             live = lax.broadcasted_iota(jnp.int32, (8, inner), 0) < valid(s, 0)
             v = jnp.where(live, v, 0.0)
@@ -490,8 +525,10 @@
         c12, sq, sfc = call(
             pool_body,
             image_counts,
-            [spl, s2, vec, wsq],
+            [spl, s2, vec, pw_all],
             [((BLOCK, 128), F32), ((8, inner), F32), ((2, inner), F32)],
+            far={3: WSQ},
+            lazy=True,
         )
         c12_g = lax.all_gather(c12, both, axis=0, tiled=True)
         sfc = sum_all(sfc)
@@ -505,12 +542,14 @@
             norm = (sq - avg) * inv
             return norm, norm * sgb[0:1] + sgb[1:2], inv
 
-        def attend_body(s, spl, sums, vec, sfc, sq, sgb, wat, att, wts):
+        def attend_body(s, spl, sums, vec, sfc, sq, sgb, wat, att, wts, arrive):
             mask = mask_of(valid(s, 0), R, mid, edge)
             n = recip(s, area)
             _, actf, _ = squeeze_norm(sq[...], sfc, s, sgb)
             hidden = jnp.maximum(actf, 0.0)
-            lg = [exact(hidden, wat[r], ((1,), (1,))) + vec[r, 2:3] for r in range(2)]
+            halves = [second(spl, sums, n, vec, r, mask) for r in range(2)]
+            arrive(6)
+            lg = [exact(hidden, wat_of(wat, r), ((1,), (1,))) + vec[r, 2:3] for r in range(2)]
             top = jnp.maximum(lg[0], lg[1])
             e = [jnp.exp(z - top) for z in lg]
             total = e[0] + e[1]
@@ -519,7 +558,7 @@
             for r in range(2):
                 w = e[r] / total
                 wts[r] = w
-                _, act, on, _ = second(spl, sums, n, vec, r, mask)
+                _, act, on, _ = halves[r]
                 wrow = w[0:1]
                 for b in range(1, own):
                     wrow = jnp.where(imgs >= b * span, w[b : b + 1], wrow)
@@ -529,33 +568,36 @@
         att, wts = call(
             attend_body,
             image_counts,
-            [spl, s2, vec, sfc, sq, sgb, wat],
+            [spl, s2, vec, sfc, sq, sgb, pw_all],
             [((R, mid), F32), ((2, 8, mid), F32)],
-        )
-
-        def own_expand_body(s, att, w, sums):
+            far={6: WAT},
+            lazy=True,
+        )
+
+        def own_expand_body(s, att, we, sums):
             a = split2(att[...])
             for k in range(nc):
-                y = mm3(a, split2(w[k]))
+                y = mm3(a, split2(we_of(we, k)))
                 sums[2 * k : 2 * k + 1] = colsum(y)
                 sums[2 * k + 1 : 2 * k + 2] = colsum(y * y)
 
         (s3,) = call(
-            own_expand_body, image_counts, [att, we_all], [((2 * nc, win), F32)], flops=6 * R * mid * win * nc, far=(1,)
-        )
-        s3_steps = sum_steps(s3)
+            own_expand_body, image_counts, [att, pw_all], [((2 * nc, win), F32)], flops=6 * R * mid * win * nc, far={1: WE}
+        )
+        att_y = swap(att, "chan", 2)
+        s3_steps = sum_steps(s3, (att_y,))
         s3 = s3_steps[-1]
-        att_r = gather3(att, s3_steps[-2])
-        s3l = lax.dynamic_slice_in_dim(s3, 2 * c, 2, 0)
+        att_r = [att, att_y, swap(att, "chan", 1), swap(after(att_y, s3_steps[-2]), "chan", 1)]
         eg = jnp.stack([expand_gain, expand_shift])
 
-        def expand_body(rels, extra, s, *refs):
+        def expand_body(rels, extra, s, *refs, arrive):
             n = len(rels)
             atts, (x_ref, g_ref, w_ref, sums, eg) = refs[:n], refs[n : n + 5]
             prev, refs = refs[n + 5 : n + 5 + extra], refs[n + 5 + extra :]
             bos, gas = refs[:n], refs[n : 2 * n]
             sg, t1, t2, u1, scr = refs[2 * n :]
-            avg, inv, _ = stats(sums, s)
+            avg, inv, _ = stats(mine_of(sums), s)
+            arrive(n + 2)
             w = split2(w_ref[...])
             sg_acc, t1_acc, t2_acc, u_acc = [0.0, 0.0], 0.0, 0.0, 0.0
             for k, r in enumerate(rels):
@@ -563,10 +605,14 @@
                 a = atts[k][...]
                 ap = split2(a)
                 norm = (mm3(ap, w) - avg) * inv
+                if k == 0:
+                    arrive(n)
                 x = load_quarter(x_ref, scr, r, mask)
                 pre = norm * eg[0:1] + eg[1:2] + x
                 on = (pre > 0) & mask
                 bos[k][...] = jnp.where(on, pre, 0.0)
+                if k == 0:
+                    arrive(n + 1)
                 g = load_quarter(g_ref, scr, r, on)
                 sg_acc[0] += colsum(g)
                 sg_acc[1] += colsum(g * norm)
@@ -591,7 +637,7 @@
             return call(
                 functools.partial(expand_body, rels, len(prev)),
                 image_counts,
-                [att_r[r] for r in rels] + [feats, gouts, expand_weight, s3l, eg] + prev,
+                [att_r[r] for r in rels] + [feats, gouts, expand_weight, s3, eg] + prev,
                 [((R, win), F32)] * n
                 + [((R, mid), F32)] * n
                 + [((2 * nc, win), F32), ((mid, win), F32), ((mid, win), F32), ((1, mid), F32)],
@@ -599,16 +645,16 @@
                 flops=12 * R * mid * win * n,
                 far=(n, n + 1, n + 2),
                 far_out=tuple(range(n)) + ((2 * n + 1, 2 * n + 2) if prev else ()),
+                lazy=True,
             )
 
         bo3, bo1, ga3, ga1, *prev = expand_call((3, 1), [])
-        bo2, bo0, ga2, ga0, sg3, t1, t2, u1 = expand_call((2, 0), list(prev))
         gy1 = ga1 + swap(ga3, "chan", 1)
+        bo2, bo0, ga2, ga0, sg3, t1, t2, u1 = expand_call((2, 0), [after(prev[0], gy1)] + list(prev[1:]))
         gys = swap(gy1, "chan", 2)
         grc = swap(ga2, "chan", 1)
-        sg3 = sum_all(sg3)
+        sg3 = sum_steps(sg3, (gys,))[-1]
         bos = [bo0, bo1, bo2, bo3]
-        sg3l = lax.dynamic_slice_in_dim(sg3, 2 * c, 2, 0)
 
         def gatt_body(s, p, rc, ys, att, we, g3, sums, sg, spl, sums2, vec, wts, sfc, sq, sgb, wat, ga, l0, l1, l2, l3, merged, scr):
             m_acc, v_acc = 0.0, 0.0
@@ -618,7 +664,7 @@
                 inv = lax.rsqrt(sums[2 * k + 1 : 2 * k + 2] * n - avg * avg + EPSILON)
                 sc = g3[k : k + 1] * inv * n
                 kap = sg[2 * k + 1 : 2 * k + 2] * inv * sc
-                w = we[k]
+                w = we_of(we, k)
                 wb = w.astype(BF16)
                 m_acc += mm((w * kap).astype(BF16), wb, ((1,), (1,)))
                 vv = sg[2 * k : 2 * k + 1] * sc - avg * kap
@@ -645,7 +691,7 @@
             for r in range(2):
                 z = wts[r] * (gw[r] - mean)
                 zs.append(z)
-                gh = gh + exact(z, wat[r])
+                gh = gh + exact(z, wat_of(wat, r))
                 for j in range(2):
                     parts.append(colsum(wts[r] * a12[r][j]))
             parts += [colsum(z) for z in zs]
@@ -673,17 +719,21 @@
         ga, l0, l1, l2, l3, merged = call(
             gatt_body,
             image_counts,
-            [ga0, grc, gys, att, we_all, g3, s3, sg3, spl, s2, vec, wts, sfc, sq, sgb, wat],
+            [ga0, grc, gys, att, pw_all, g3, s3, sg3, spl, s2, vec, wts, sfc, sq, sgb, pw_all],
             [((R, mid), F32)] + [((8, 2 * lw), F32)] * 4 + [((ni + 6 * nb + 4, inner), F32)],
             [pltpu.VMEM((nc, 8, 2 * lw), F32)],
             flops=2 * R * mid * mid + 2 * nc * mid * mid * win,
-            far=(4,),
+            far={4: WE, 15: WAT},
             far_out=(0,),
         )
 
+        used = 4 * nb * own
+
         def all_body(s, g, vec, wsq, sfc, sgb, c1_ref, c2_ref, pool_ref, norm_ref, hid_ref):
+            g = g.reshape(ND * used, 128)
+
             def rows(k):
-                return jnp.concatenate([g[pl.ds(k * own + b, ND, stride=BLOCK), :] for b in range(own)], axis=0)
+                return jnp.concatenate([g[pl.ds(k * own + b, ND, stride=used), :] for b in range(own)], axis=0)
 
             pooled = 0.0
             for r in range(2):
@@ -694,14 +744,14 @@
                 pooled = pooled + vec[r, 0:1] * c2 + vec[r, 1:2] * c1
             pooled = pooled * (1.0 / area)
             pool_ref[...] = pooled
-            norm, actf, _ = squeeze_norm(exact(pooled, wsq[...]), sfc, s, sgb)
+            norm, actf, _ = squeeze_norm(exact(pooled, wsq_of(wsq)), sfc, s, sgb)
             norm_ref[...] = norm
             hid_ref[...] = jnp.maximum(actf, 0.0)
 
         c1_all, c2_all, pool_all, normf_all, hid_all = call(
             all_body,
             image_counts,
-            [c12_g, vec, wsq, sfc, sgb],
+            [c12_g.reshape(ND, BLOCK, 128), vec, pw_all, sfc, sgb],
             [
                 ((2, ni, mid), F32),
                 ((2, ni, mid), F32),
@@ -709,7 +759,7 @@
                 ((ni, inner), F32),
                 ((ni, inner), F32),
             ],
-            far=(0,),
+            far={0: slice(0, used), 2: WSQ},
         )
         for k, g in enumerate(sum_groups):
             got = [swap(merged, both, m) for m in g]
@@ -731,8 +781,8 @@
             return jnp.where(slot < live, 1.0, 0.0)
 
         def back_body(
-            s, merged, c1a, c2a, normf, sfc, sgb, wsq, ga, spl, sums2, vec, wts, red, sums1, w1,
-            dz1, sg1, b0, b1, b2, b3, gq_ref, sg2, gfc, wab, zh, blk,
+            s, merged, c1a, c2a, normf, sfc, sgb, wsq, ga, spl, sums2, vec, wts, l0, l1, l2, l3,
+            gs_ref, b0, b1, b2, b3, gq_ref, sg2, gfc, wab, blk, arrive,
         ):
             dzf = merged[0:ni]
             norm_all = normf[...]
@@ -748,7 +798,8 @@
             _, _, inv = squeeze_norm(0.0, sfc, s, sgb)
             gq = sgb[0:1] * inv * (dzf - all_valid(s) * (s_f + norm_all * g_f) * nf)
             gq_ref[...] = gq
-            gp = exact(gq, wsq[...], ((1,), (1,))) * (1.0 / area)
+            arrive(6)
+            gp = exact(gq, wsq_of(wsq), ((1,), (1,))) * (1.0 / area)
             mask = mask_of(valid(s, 0), R, mid, edge)
             imgs = lax.broadcasted_iota(jnp.int32, (R, mid), 0)
             grow = lax.broadcasted_iota(jnp.int32, (ni, mid), 0)
@@ -775,6 +826,8 @@
                 wrow = w[0:1]
                 for b in range(1, own):
                     wrow = jnp.where(imgs >= b * span, w[b : b + 1], wrow)
+                if r == 0:
+                    arrive(7)
                 dz = jnp.where(on, wrow * ga[...] + gprow, 0.0)
                 gs = vec[r, 0:1] * inv2 * (dz - (s2v + norm * g2v) * n)
                 gs = jnp.where(mask, gs, 0.0)
@@ -784,13 +837,21 @@
                 a, b = gss[0][:, cols], gss[1][:, cols]
                 blk[2 * pair] = jnp.where(lane < lw, a, pltpu.roll(b, lw, 1))
                 blk[2 * pair + 1] = jnp.where(lane < lw, pltpu.roll(a, lw, 1), b)
-            for k, o in enumerate((b0, b1, b2, b3)):
-                o[...] = blk[c ^ k]
+            for k, (o, z) in enumerate(((b0, l0), (b1, l1), (b2, l2), (b3, l3))):
+                o[0:R] = blk[c ^ k]
+                o[R : R + 8] = z[...]
+            for r in range(2):
+                gs_ref[:, r * mid : (r + 1) * mid] = gss[r]
+
+        def conv_back_body(s, gs, red, sums1, vec, w1, dz1, sg1, zh, arrive):
+            mask = mask_of(valid(s, 0), R, mid, edge)
             avg1, inv1, _ = stats(sums1, s)
             norm1 = (red[...] - avg1) * inv1
             on1 = (norm1 * vec[0, 3:4] + vec[1, 3:4] > 0) & mask
             for r in range(2):
-                taps_in(gss[r], (zh,), own)
+                taps_in(gs[:, r * mid : (r + 1) * mid], (zh,), own)
+                if r == 0:
+                    arrive(4)
                 acc = 0.0
                 for t, (u, v) in enumerate(TAPS):
                     z = zh[2 - v, :, 2 - u : 2 - u + edge].reshape(R, mid)
@@ -801,115 +862,84 @@
                 sg1[0:1, cols] = colsum(acc)
                 sg1[1:2, cols] = colsum(acc * norm1[:, cols])
 
-        dz1, sg1, blk0, blk1, blk2, blk3, gq, sg2, gfc, wab = call(
+        gs, blk0, blk1, blk2, blk3, gq, sg2, gfc, wab = call(
             back_body,
             image_counts,
-            [merged, c1_all, c2_all, normf_all, sfc, sgb, wsq, ga, spl, s2, vec, wts, red, s1, w1_home],
-            [((R, mid), F32), ((2, mid), F32)]
-            + [((R, 2 * lw), F32)] * 4
+            [merged, c1_all, c2_all, normf_all, sfc, sgb, pw_all, ga, spl, s2, vec, wts, l0, l1, l2, l3],
+            [((R, 2 * mid), F32)]
+            + [((R + 8, 2 * lw), F32)] * 4
             + [((ni, inner), F32), ((2, 2, mid), F32), ((2, inner), F32), ((2, mid), F32)],
-            [pltpu.VMEM((3, own, PAD, PAD, mid), BF16), pltpu.VMEM((nc, R, 2 * lw), F32)],
+            [pltpu.VMEM((nc, R, 2 * lw), F32)],
+            far={6: WSQ, 7: None},
+            lazy=True,
+        )
+        dz1, sg1 = call(
+            conv_back_body,
+            image_counts,
+            [gs, red, s1, vec, w1],
+            [((R, mid), F32), ((2, mid), F32)],
+            [pltpu.VMEM((3, own, PAD, PAD, mid), BF16)],
             flops=4 * R * nw * mid,
-            far=(7, 13),
-            far_out=(2,),
+            far=(4,),
+            lazy=True,
         )
         blks = [blk0, swap(blk1, "chan", 1), swap(blk2, "chan", 2), swap(blk3, "chan", 3)]
-        sg1_steps = sum_steps(sg1)
-        sg1 = sg1_steps[-1]
-        dz1_r = gather3(after(dz1, sg1_steps[1]), sg1)
-
-        gl_r = [l0, swap(after(l1, sg1_steps[0]), "chan", 1), swap(after(l2, sg1_steps[0]), "chan", 2), swap(after(l3, sg1_steps[0]), "chan", 3)]
-
-        def early_body(s, a0, a1, a2, a3, hid, t1, t2, u1, sums, sg, eg, out):
+
+        def prep_body(s, red_g, sums, vec, relu, norm):
+            avg, inv, _ = stats(sums, s)
+            for k in range(nc):
+                mask = mask_of(valid(s, CHAN_REL[k]), R, mid, edge)
+                v = (red_g[me()[0] ^ k] - avg) * inv
+                rows = slice(k * R, (k + 1) * R)
+                norm[rows, :] = v.astype(BF16)
+                z = jnp.maximum(v * vec[0, 3:4] + vec[1, 3:4], 0.0)
+                relu[rows, :] = jnp.where(mask, z, 0.0).astype(BF16)
+
+        relu_all, norm_all = call(
+            prep_body, image_counts, [after(red_g, gs), s1, vec], [((nc * R, mid), BF16)] * 2, far=(0,)
+        )
+
+        def masked_body(s, b0, b1, b2, b3, go, m0, m1, m2, m3, out_bo, scr):
+            for r, (b, o) in enumerate(((b0, m0), (b1, m1), (b2, m2), (b3, m3))):
+                bo = b[...]
+                o[...] = load_quarter(go, scr, r, bo > 0)
+                store_quarter(out_bo, scr, r, bo)
+
+        *masked, block_out = call(
+            masked_body,
+            image_counts,
+            [after(bos[0], gs)] + bos[1:] + [gouts],
+            [((R, win), F32)] * 4 + [(feats.shape, F32)],
+            [quarter_scratch],
+            far=(0, 1, 2, 3, 4),
+            far_out=(0, 1, 2, 3, 4),
+        )
+
+        dz1_y = swap(after(dz1, relu_all, masked[0]), "chan", 2)
+
+        n_w = 9 * 2 * lw
+        n_dws = padded_rows(n_w + lb * mid + 2 * lw)
+
+        def dws_body(s, k0, k1, k2, k3, relu, hid, t1, t2, u1, sums3, sg, eg, *refs):
+            outs, (sg_out, zg, out) = refs[:-3], refs[-3:]
             acc = 0.0
             base = lax.axis_index("dp") * nc
-            for k, a in enumerate((a0, a1, a2, a3)):
-                z = a[...]
+            for k, a in enumerate((k0, k1, k2, k3)):
                 row = lax.broadcasted_iota(jnp.int32, (8, inner), 0)
                 h = jnp.zeros((8, inner), F32)
                 for b in range(own):
                     h = jnp.where(row == b, hid[pl.ds(base + (me()[0] ^ k) + b * ND, 1), :], h)
-                acc += exact(z, h, ((0,), (0,)))
-            avg, inv, n = stats(sums, s)
+                acc += exact(a[R : R + 8, :], h, ((0,), (0,)))
+            out[n_w + lb * mid : n_w + lb * mid + 2 * lw] = acc
+            _, inv, n = stats(mine_of(sums3), s)
+            sg = mine_of(sg)
+            sg_out[...] = sg
             outer = exact(u1[...], sg[0:1], ((0,), (0,)))
             z = (eg[0:1] * inv) * (t1[...] - (outer + t2[...] * sg[1:2]) * n)
             for i in range(lb):
-                out[i * mid : (i + 1) * mid] = z[:, i * 128 : (i + 1) * 128]
-            at = lb * mid
-            out[at : at + 2 * lw] = acc
-
-        (early,) = call(
-            early_body,
-            image_counts,
-            gl_r + [hid_all, t1, t2, u1, s3l, sg3l, eg],
-            [((lb * mid + 2 * lw, inner), F32)],
-            far=(5, 6),
-        )
-
-        n_early, n_total = lb * mid + 2 * lw, padded_rows(lb * mid + 2 * lw + win * mid // 128)
-        mb = mid // 128
-
-        def dwr_body(s, d0, d1, d2, d3, red_g, x_ref, sums, sg, vec, early, *refs):
-            outs, (go0, go1, go2, go3, scr, sent) = refs[:-6], refs[-6:]
-            avg, inv, n = stats(sums, s)
-            acc = 0.0
-            for r, (dz, go) in enumerate(((d0, go0), (d1, go1), (d2, go2), (d3, go3))):
-                mask = mask_of(valid(s, r), R, win, edge)
-                norm = (red_g[me()[0] ^ CHAN_REL[r]] - avg) * inv
-                g = vec[0, 3:4] * inv * (dz[...] - (sg[0:1] + norm * sg[1:2]) * n)
-                g = jnp.where(mask, g, 0.0).astype(BF16)
-                go[...] = g
-                acc += mm(load_quarter(x_ref, scr, r, mask).astype(BF16), g, ((0,), (0,)))
-            sent[0:n_early] = early[...]
-            for i in range(mb):
-                sent[n_early + i * win : n_early + (i + 1) * win] = acc[:, i * 128 : (i + 1) * 128]
-            cut_chunks(sent, groups[0], outs)
-
-        *sent, gr0, gr1, gr2, gr3 = call(
-            dwr_body,
-            image_counts,
-            dz1_r + [red_g, feats, s1, sg1, vec, early],
-            chunk_outs(n_total, groups[0]) + [((R, mid), BF16)] * 4,
-            [quarter_scratch, pltpu.VMEM((n_total, 128), F32)],
-            flops=8 * R * win * mid,
-            far=(4, 5),
-        )
-        summed = big_sum_dp(image_counts, sent)
-        grad_expand_weight = summed[: lb * mid].reshape(lb, mid, 128).transpose(1, 0, 2).reshape(mid, win)
-        watt = summed[lb * mid : n_early]
-        dwr = summed[n_early : n_early + mb * win]
-        grad_reduce_weight = dwr.reshape(mb, win, 128).transpose(1, 0, 2).reshape(win, mid)
-
-        def gin_body(s, g0, g1, g2, g3, b0, b1, b2, b3, go, w_ref, out_bo, out_gi, scr):
-            w = w_ref[...].astype(BF16)
-            for r, (g, b) in enumerate(((g0, b0), (g1, b1), (g2, b2), (g3, b3))):
-                bo = b[...]
-                z = mm(g[...], w, ((1,), (1,))) + load_quarter(go, scr, r, bo > 0)
-                store_quarter(out_gi, scr, r, z)
-                store_quarter(out_bo, scr, r, bo)
-
-        block_out, grad_input = call(
-            gin_body,
-            image_counts,
-            [gr0, gr1, gr2, gr3] + bos + [gouts, reduce_weight],
-            [(feats.shape, F32)] * 2,
-            [quarter_scratch],
-            flops=8 * R * win * mid,
-            far=(4, 5, 6, 7, 8, 9),
-            far_out=(0, 1),
-        )
-        block_out, grad_input = from_native(block_out), from_native(grad_input)
-
-        n_dws = padded_rows(9 * 2 * lw)
-
-        def dws_body(s, k0, k1, k2, k3, red_g, sums, vec, *refs):
-            outs, (zg, relu, out) = refs[:-3], refs[-3:]
-            avg, inv, _ = stats(sums, s)
+                out[n_w + i * mid : n_w + (i + 1) * mid] = z[:, i * 128 : (i + 1) * 128]
             for k, bk in enumerate((k0, k1, k2, k3)):
-                mask = mask_of(valid(s, CHAN_REL[k]), R, mid, edge)
-                z = jnp.maximum((red_g[me()[0] ^ k] - avg) * inv * vec[0, 3:4] + vec[1, 3:4], 0.0)
-                relu[k * R : (k + 1) * R, :] = jnp.where(mask, z, 0.0).astype(BF16)
-                taps_in(bk[...], (zg.at[:, k * own : (k + 1) * own],), own)
+                taps_in(bk[0:R, :], (zg.at[:, k * own : (k + 1) * own],), own)
             taps = [zg[2 - v, :, 2 - u : 2 - u + edge].reshape(nc * R, 2 * lw) for u, v in TAPS]
             y = mm(relu[...], jnp.concatenate(taps, axis=1), ((0,), (0,)))
             lane = lax.broadcasted_iota(jnp.int32, (half, 2 * lw), 1)
@@ -918,17 +948,83 @@
                 out[t * 2 * lw : (t + 1) * 2 * lw, :] = jnp.where(lane < lw, y[:half, cols], y[half:, cols]).T
             cut_chunks(out, groups[0], outs)
 
-        dws = call(
+        *dws, sg3l = call(
             dws_body,
             image_counts,
-            blks + [red_g, s1, vec],
-            chunk_outs(n_dws, groups[0]),
-            [pltpu.VMEM((3, slots, PAD, PAD, 2 * lw), BF16), pltpu.VMEM((nc * R, mid), BF16), pltpu.VMEM((n_dws, 128), F32)],
+            blks + [relu_all, after(hid_all, masked[0]), t1, t2, u1, s3, sg3, eg],
+            chunk_outs(n_dws, groups[0]) + [((2, win), F32)],
+            [pltpu.VMEM((3, slots, PAD, PAD, 2 * lw), BF16), pltpu.VMEM((n_dws, 128), F32)],
             flops=2 * nc * R * mid * 9 * 2 * lw,
-            far=(0, 4),
-        )
-        dws = big_sum_dp(image_counts, dws)[: 9 * 2 * lw]
+            far=(0, 6, 7),
+        )
+        sg1_steps = sum_steps(after(sg1, dws[1]))
+        sg1 = sg1_steps[-1]
+        dz1_r = [dz1, dz1_y, swap(dz1, "chan", 1), swap(dz1_y, "chan", 1)]
+
+        mb = mid // 128
+        n_dwr = padded_rows(mb * win)
+
+        def dwr_body(s, d0, d1, d2, d3, norms, x0, x1, x2, x3, sums, sg, vec, *refs):
+            outs, (go0, go1, go2, go3, sent) = refs[:-5], refs[-5:]
+            _, inv, n = stats(sums, s)
+            acc = 0.0
+            for r, (dz, go, x) in enumerate(((d0, go0, x0), (d1, go1, x1), (d2, go2, x2), (d3, go3, x3))):
+                mask = mask_of(valid(s, r), R, win, edge)
+                k = CHAN_REL[r]
+                norm = norms[k * R : (k + 1) * R, :].astype(F32)
+                g = vec[0, 3:4] * inv * (dz[...] - (sg[0:1] + norm * sg[1:2]) * n)
+                g = jnp.where(mask, g, 0.0).astype(BF16)
+                go[...] = g
+                acc += mm(x[...], g, ((0,), (0,)))
+            for i in range(mb):
+                sent[i * win : (i + 1) * win] = acc[:, i * 128 : (i + 1) * 128]
+            cut_chunks(sent, groups[0], outs)
+
+        *sent, gr0, gr1, gr2, gr3 = call(
+            dwr_body,
+            image_counts,
+            dz1_r + [norm_all, x0, x1, x2, x3, s1, sg1, vec],
+            chunk_outs(n_dwr, groups[0]) + [((R, mid), BF16)] * 4,
+            [pltpu.VMEM((n_dwr, 128), F32)],
+            flops=8 * R * win * mid,
+            far=(5, 6, 7, 8),
+        )
+        def gin_body(s, g0, g1, g2, g3, m0, m1, m2, m3, w_ref, out_gi, scr):
+            w = w_ref[...].astype(BF16)
+            for r, (g, m) in enumerate(((g0, m0), (g1, m1), (g2, m2), (g3, m3))):
+                store_quarter(out_gi, scr, r, mm(g[...], w, ((1,), (1,))) + m[...])
+
+        (grad_input,) = call(
+            gin_body,
+            image_counts,
+            [gr0, gr1, gr2, gr3] + masked + [reduce_weight],
+            [(feats.shape, F32)],
+            [quarter_scratch],
+            flops=8 * R * win * mid,
+            far=(4, 5, 6, 7, 8),
+            far_out=(0,),
+        )
+
+        def write_dwr(whole, out):
+            for i in range(mb):
+                out[:, i * 128 : (i + 1) * 128] = whole[i * win : (i + 1) * win, :]
+
+        (grad_reduce_weight,) = sum_dp(image_counts, sent, write_dwr, [((win, mid), F32)])
+        def write_dws(whole, o_ws, o_we, o_at):
+            o_ws[...] = whole[:n_w, :]
+            for i in range(lb):
+                o_we[:, i * 128 : (i + 1) * 128] = whole[n_w + i * mid : n_w + (i + 1) * mid, :]
+            o_at[...] = whole[n_w + lb * mid : n_w + lb * mid + 2 * lw, :]
+
+        dws, grad_expand_weight, watt = sum_dp(
+            image_counts,
+            dws,
+            write_dws,
+            [((n_w, 128), F32), ((mid, win), F32), ((2 * lw, 128), F32)],
+            [(), (grad_input,)],
+        )
         grad_split_weight = dws.reshape(3, 3, 2, lw, half).transpose(0, 1, 4, 2, 3)
+        block_out, grad_input = from_native(block_out), from_native(grad_input)
 
         def sq_body(s, pool, gq, out):
             out[...] = exact(pool[...], gq[...], ((0,), (0,)))

time: 268 us -> 245 us (0.914)
  waiting for transfers between devices: 84.3 us -> 74 us
  local copies, waits for them, and re-layouts: 14.3 us -> 5.59 us
  starting transfers between devices: 84.3 us -> 79.8 us
    ppermute x89 -> x83, waiting for transfers between devices: 84.3 us -> 73.9 us  [swap(): return lax.ppermute(x, axis, [(i, i ^ k) for i in range(n)])]
    unnamed x50 -> x36, local copies, waits for them, and re-layouts: 8.89 us -> 1.74 us
    ppermute x89 -> x83, starting transfers between devices: 84 us -> 79.5 us  [swap(): return lax.ppermute(x, axis, [(i, i ^ k) for i in range(n)])]
    pallas_call x27 -> x28, Pallas kernels: 68.6 us -> 69 us  [call(): pl.pallas_call(kernel, out_shape=[pltpu.HBM(s, d) if k in far_out else ja...]
  transfers between devices with their start and end apart: 92 -> 86, of which waited for: 48 -> 49; matrix products, arithmetic and copies ran while one was open for 2% -> 2% of each run, Pallas kernels for 25% -> 25%
where the time goes in v2:
time: 245 us; the launch traced here: 244 us
  starting transfers between devices  79.8 us (33%)
  waiting for transfers between devices  74 us (30%)
  Pallas kernels  69 us (28%)
  between operations  14.3 us (6%)
  local copies, waits for them, and re-layouts  5.59 us (2%)
    ppermute x83, starting transfers between devices, swap(): return lax.ppermute(x, axis, [(i, i ^ k) for i in range(n)])  79.5 us
    ppermute x83, waiting for transfers between devices, swap(): return lax.ppermute(x, axis, [(i, i ^ k) for i in range(n)])  73.9 us
    pallas_call x28, Pallas kernels, call(): pl.pallas_call(kernel, out_shape=[pltpu.HBM(s, d) if k in far_out else ja...  69 us
  transfers between devices with their start and end apart: 86, of which 49 were waited for; matrix products, arithmetic and copies ran while one was open for 2% of the time, Pallas kernels for 25%

profile of v2, /device:TPU:0, one launch (start us, length us, event | category | flops | bytes accessed | tf_op | source)
XLA Modules:
  0.0 243.8 jit_solution(2192192822075612214)
XLA Ops:
  7.9 3.3 %shard_map.289 = (f32[448,256]{1,0:T(8,128)S(1)}, f32[448,256]{1,0:T(8,128)S(1)}, bf16[448,256]{1,0:T(8,128)(2,1)}, bf16[448,256]{1,0:T(8,128)(2,1)}) custom-call(s32[8]{0:T(128)S(1)} %copy-done, f32[3136,128]{1,0:T(8,128)} %bitcast.74, f32[256,256]{1,0:T(8,128)} %refs_8_.1), custom_call_target="tpu_custom_call" | custom-call | flops 704643072 | bytes 3244032 | tf_op jit(solution)/shard_map/pallas_call | solution.py:99
  11.7 1.4 collective-permute-done.1
  13.3 3.0 %collective-permute-start.2 = (f32[448,256]{1,0:T(8,128)S(1)}, f32[448,256]{1,0:T(8,128)S(1)}, u32[]{:S(2)}, u32[]{:S(2)}) collective-permute-start(f32[448,256]{1,0:T(8,128)S(1)} %add.161), channel_id=1, source_target_pairs={{0,2},{1,3},{2,0},{3,1},{4,6},{5,7},{6,4},{7,5},{8,10},{9,11},{10,... | collective-permute-start | bytes 1376264 | tf_op jit(solution)/shard_map/ppermute | solution.py:129
  16.3 3.3 %shard_map.288 = (f32[448,256]{1,0:T(8,128)S(1)}, f32[448,256]{1,0:T(8,128)S(1)}, bf16[448,256]{1,0:T(8,128)(2,1)}, bf16[448,256]{1,0:T(8,128)(2,1)}) custom-call(s32[8]{0:T(128)S(1)} %copy-done, f32[3136,128]{1,0:T(8,128)} %bitcast.75, f32[256,256]{1,0:T(8,128)} %refs_8_.1), custom_call_target="tpu_custom_call" | custom-call | flops 704643072 | bytes 3244032 | tf_op jit(solution)/shard_map/pallas_call | solution.py:99
  19.7 7.4 %collective-permute-done.2.refs_2_ = f32[448,256]{1,0:T(8,128)S(1)} collective-permute-done((f32[448,256]{1,0:T(8,128)S(1)}, f32[448,256]{1,0:T(8,128)S(1)}, u32[]{:S(2)}, u32[]{:S(2)}) %collective-permute-start.2) | collective-permute-done | bytes 458784 | tf_op jit(solution)/shard_map/ppermute | solution.py:129
  27.1 1.7 collective-permute-start.7
  29.2 1.4 shard_map.290
  31.8 2.4 collective-permute-start.5
  34.2 1.3 collective-permute-start.6
  36.5 2.8 %collective-permute-done.6 = f32[40,128]{1,0:T(8,128)S(1)} collective-permute-done((f32[40,128]{1,0:T(8,128)S(1)}, f32[40,128]{1,0:T(8,128)S(1)}, u32[]{:S(2)}, u32[]{:S(2)}) %collective-permute-start.6) | collective-permute-done | bytes 20512 | tf_op jit(solution)/shard_map/ppermute | solution.py:129
  39.3 2.8 %collective-permute-done.7.refs_4_ = f32[1152,128]{1,0:T(8,128)} collective-permute-done((f32[1152,128]{1,0:T(8,128)S(1)}, f32[1152,128]{1,0:T(8,128)}, u32[]{:S(2)}, u32[]{:S(2)}) %collective-permute-start.7) | collective-permute-done | bytes 589856 | tf_op jit(solution)/shard_map/ppermute | solution.py:129
  43.8 1.5 collective-permute-start.10
  45.9 2.0 collective-permute-done.10
  50.6 4.8 %shard_map.292 = (f32[448,512]{1,0:T(8,128)S(1)}, f32[2,512]{1,0:T(2,128)S(1)}, bf16[2,256,1152]{2,1,0:T(8,128)(2,1)}) custom-call(s32[8]{0:T(128)S(1)} %copy-done.1, f32[448,256]{1,0:T(8,128)} %get-tuple-element.188.refs_0_.refs_1_, f32[2,256]{1,0:T(2,128)S(1)} %get-tuple-element.141.refs_1_.refs_2_.refs_9_, ...), custom_call_target="tpu_custom_call" | custom-call | flops 1585446912 | bytes 4937728 | tf_op jit(solution)/shard_map/pallas_call | solution.py:99
  56.6 2.4 collective-permute-start.15
  60.6 3.3 %collective-permute-done.16 = f32[2,512]{1,0:T(2,128)S(1)} collective-permute-done((f32[2,512]{1,0:T(2,128)S(1)}, f32[2,512]{1,0:T(2,128)S(1)}, u32[]{:S(2)}, u32[]{:S(2)}) %collective-permute-start.16) | collective-permute-done | bytes 4128 | tf_op jit(solution)/shard_map/ppermute | solution.py:129
  67.1 1.8 collective-permute-done.19
  68.9 2.1 shard_map.293
  76.4 1.8 collective-permute-done.23
  79.5 1.3 collective-permute-start.26
  81.3 2.1 collective-permute-done.26
  83.8 2.0 shard_map.294
  86.6 2.7 %shard_map.295 = f32[8,256]{1,0:T(8,128)S(1)} custom-call(s32[8]{0:T(128)S(1)} %copy-done.1, f32[448,256]{1,0:T(8,128)S(1)} %get-tuple-element.151.refs_0_.refs_1_.refs_3_, f32[4,704,128]{2,1,0:T(8,128)} %bitcast.66), custom_call_target="tpu_custom_call" | custom-call | flops 704643072 | bytes 1908736 | tf_op jit(solution)/shard_map/pallas_call | solution.py:99
  91.4 1.7 collective-permute-start.31
  94.5 1.7 collective-permute-done.31
  96.3 2.9 %collective-permute-done.32.refs_1_ = f32[448,256]{1,0:T(8,128)S(1)} collective-permute-done((f32[448,256]{1,0:T(8,128)S(1)}, f32[448,256]{1,0:T(8,128)S(1)}, u32[]{:S(2)}, u32[]{:S(2)}) %collective-permute-start.32) | collective-permute-done | bytes 458784 | tf_op jit(solution)/shard_map/ppermute | solution.py:129
  102.5 1.7 collective-permute-done.35
  104.4 5.4 %shard_map.296 = (f32[448,256]{1,0:T(8,128)}, f32[448,256]{1,0:T(8,128)}, f32[448,256]{1,0:T(8,128)S(1)}, f32[448,256]{1,0:T(8,128)S(1)}, f32[8,256]{1,0:T(8,128...) custom-call(s32[8]{0:T(128)S(1)} %copy-done.1, ...), custom_call_target="tpu_custom_call" | custom-call | flops 704643072 | bytes 6769664 | tf_op jit(solution)/shard_map/pallas_call | solution.py:99
  110.8 1.4 collective-permute-done.37
  113.5 5.1 %shard_map.297 = (f32[448,256]{1,0:T(8,128)}, f32[448,256]{1,0:T(8,128)}, f32[448,256]{1,0:T(8,128)S(1)}, f32[448,256]{1,0:T(8,128)S(1)}, f32[8,256]{1,0:T(8,128...) custom-call(s32[8]{0:T(128)S(1)} %copy-done.1, ...), custom_call_target="tpu_custom_call" | custom-call | flops 704643072 | bytes 7303168 | tf_op jit(solution)/shard_map/pallas_call | solution.py:99
  120.4 1.8 collective-permute-start.43
  123.8 1.5 collective-permute-done.43
  128.5 2.1 collective-permute-done.46
  130.7 3.7 %shard_map.298 = (f32[448,256]{1,0:T(8,128)}, f32[8,128]{1,0:T(8,128)S(1)}, f32[8,128]{1,0:T(8,128)S(1)}, f32[8,128]{1,0:T(8,128)S(1)}, f32[8,128]{1,0:T(8,128)S(1)}, /*index=5*/f32[80,128]{1,0:T(8,128)S(1)}) custom-call(s32[8]{0:T(128)S(1)} %copy-done.1, f32[448,256]{1,0:T(8,128)S(1)} %get-tuple-element.162.refs_0_, ...), custom_call_target="tpu_custom_call" | custom-call | flops 192937984 | bytes 6219776 | tf_op jit(solution)/shard_map/pallas_call | solution.py:99
  136.7 1.7 collective-permute-start.50
  138.8 2.4 collective-permute-done.49
  143.1 1.8 shard_map.299
  145.0 1.4 collective-permute-start.52
  148.5 2.2 collective-permute-done.53
  151.9 2.5 %shard_map.300 = (f32[448,512]{1,0:T(8,128)S(1)}, f32[456,128]{1,0:T(8,128)S(1)}, f32[456,128]{1,0:T(8,128)S(1)}, f32[456,128]{1,0:T(8,128)S(1)}, f32[456,128]{1...) custom-call(s32[8]{0:T(128)S(1)} %copy-done.1, ...), custom_call_target="tpu_custom_call" | custom-call | bytes 5100544 | tf_op jit(solution)/shard_map/pallas_call | solution.py:99
  156.5 5.4 %shard_map.301 = (f32[448,256]{1,0:T(8,128)}, f32[448,256]{1,0:T(8,128)}, f32[448,256]{1,0:T(8,128)}, f32[448,256]{1,0:T(8,128)}, f32[3136,128]{1,0:T(8,128)}) custom-call(s32[8]{0:T(128)S(1)} %copy-done.1, f32[448,256]{1,0:T(8,128)} %get-tuple-element.181.refs_0_, f32[448,256]{1,0:T(8,128)} %get-tuple-element.182.refs_1_, ...), custom_call_target="tpu_custom_call" | custom-call | bytes 6881280 | tf_op jit(solution)/shard_map/pallas_call | solution.py:99
  161.9 3.6 %shard_map.302 = (f32[448,256]{1,0:T(8,128)S(1)}, f32[2,256]{1,0:T(2,128)S(1)}) custom-call(s32[8]{0:T(128)S(1)} %copy-done.1, f32[448,512]{1,0:T(8,128)S(1)} %get-tuple-element.180.refs_0_, f32[448,256]{1,0:T(8,128)} %get-tuple-element.188.refs_0_.refs_1_, f32[2,256]{1,0:T(2,128)S(1)} %get-tuple-element.141.refs_1_.refs_2_.refs_9_, ...), custom_call_target="tpu_custom_call" | custom-call | flops 528482304 | bytes 3035136 | tf_op jit(solution)/shard_map/pallas_call | solution.py:99
  165.5 2.6 %shard_map.303 = (bf16[1792,256]{1,0:T(8,128)(2,1)S(1)}, bf16[1792,256]{1,0:T(8,128)(2,1)S(1)}) custom-call(s32[8]{0:T(128)S(1)} %copy-done.1, f32[4,448,256]{2,1,0:T(8,128)} %bitcast.78, f32[2,256]{1,0:T(2,128)S(1)} %get-tuple-element.141.refs_1_.refs_2_.refs_9_, f32[2,8,256]{2,1,0:T(8,128)S(1)} %get-tuple-element.142.refs_2_.refs_10_.refs_1_.refs_3_.refs_11_), custom_call_target="tpu_custom_call" | custom-call | bytes 3688448 | tf_op jit(solution)/shard_map/pallas_call | solution.py:99
  169.1 4.5 %shard_map.304 = (f32[896,128]{1,0:T(8,128)S(1)}, f32[896,128]{1,0:T(8,128)S(1)}, f32[2,256]{1,0:T(2,128)S(1)}) custom-call(s32[8]{0:T(128)S(1)} %copy-done.1, f32[456,128]{1,0:T(8,128)} %copy-done.2, f32[456,128]{1,0:T(8,128)} %collective-permute-done.57.refs_1_, f32[456,128]{1,0:T(8,128)} %collective-permute-done.58.refs_2_, ...), custom_call_target="tpu_custom_call" | custom-call | flops 1056964608 | bytes 3347456 | tf_op jit(solution)/shard_map/pallas_call | solution.py:99
  176.3 1.5 collective-permute-start.63
  179.7 1.3 collective-permute-done.54.refs_1_
  181.2 1.3 collective-permute-start.65
  183.2 3.0 %collective-permute-done.75.refs_1_ = f32[896,128]{1,0:T(8,128)S(1)} collective-permute-done((f32[896,128]{1,0:T(8,128)S(1)}, f32[896,128]{1,0:T(8,128)S(1)}, u32[]{:S(2)}, u32[]{:S(2)}) %collective-permute-start.75) | collective-permute-done | bytes 458784 | tf_op jit(solution)/shard_map/ppermute | solution.py:129
  188.8 2.0 collective-permute-start.77
  190.8 2.0 collective-permute-start.78
  192.8 2.7 %shard_map.305 = (f32[256,128]{1,0:T(8,128)S(1)}, f32[256,128]{1,0:T(8,128)S(1)}, bf16[448,256]{1,0:T(8,128)(2,1)S(1)}, bf16[448,256]{1,0:T(8,128)(2,1)S(1)}, bf...) custom-call(s32[8]{0:T(128)S(1)} %copy-done.1, f32[448,256]{1,0:T(8,128)S(1)} %get-tuple-element.192.refs_0_, ...), custom_call_target="tpu_custom_call" | custom-call | flops 234881024 | bytes 4870144 | tf_op jit(solution)/shard_map/pallas_call | solution.py:99
  196.3 4.2 %shard_map.306 = f32[3136,128]{1,0:T(8,128)} custom-call(s32[8]{0:T(128)S(1)} %copy-done.1, bf16[448,256]{1,0:T(8,128)(2,1)S(1)} %get-tuple-element.210.refs_0_, bf16[448,256]{1,0:T(8,128)(2,1)S(1)} %get-tuple-element.211.refs_1_, bf16[448,256]{1,0:T(8,128)(2,1)S(1)} %get-tuple-element.212.refs_2_, bf16[448,256]{1,0:T(8,128)(2,1)S(1)} %get-tuple-element.213.refs_3_, ...), custom_call_target="tpu_custom_call" | custom-call | flops 234881024 | bytes 4620288 | tf_op jit(solution)/shard_map/pallas_call | solution.py:99
  201.3 2.9 %collective-permute-start.79 = (f32[224,128]{1,0:T(8,128)S(1)}, f32[224,128]{1,0:T(8,128)S(1)}, u32[]{:S(2)}, u32[]{:S(2)}) collective-permute-start(f32[224,128]{1,0:T(8,128)S(1)} %shard_map.312.refs_0_), channel_id=1, source_target_pairs={{0,8},{4,12},{8,0},{12,4},{16,24},{20,28},{24,16},{28,20},{1,9},{5... | collective-permute-start | bytes 344072 | tf_op jit(solution)/shard_map/ppermute | solution.py:129
  205.1 2.1 collective-permute-start.81
  210.8 2.1 collective-permute-start.70
  213.5 3.9 %collective-permute-done.80.refs_2_ = f32[224,128]{1,0:T(8,128)S(1)} collective-permute-done((f32[224,128]{1,0:T(8,128)S(1)}, f32[224,128]{1,0:T(8,128)S(1)}, u32[]{:S(2)}, u32[]{:S(2)}) %collective-permute-start.80) | collective-permute-done | bytes 114720 | tf_op jit(solution)/shard_map/ppermute | solution.py:129
  218.7 1.5 collective-permute-done.69.refs_2_
  220.8 1.6 collective-permute-start.71
  223.2 2.1 collective-permute-start.73
  225.8 1.7 collective-permute-done.72.refs_2_
  227.5 1.4 collective-permute-done.73.refs_3_
  231.1 3.4 %collective-permute-done.74.refs_1_ = f32[256,128]{1,0:T(8,128)S(1)} collective-permute-done((f32[256,128]{1,0:T(8,128)S(1)}, f32[256,128]{1,0:T(8,128)S(1)}, u32[]{:S(2)}, u32[]{:S(2)}) %collective-permute-start.74) | collective-permute-done | bytes 131104 | tf_op jit(solution)/shard_map/ppermute | solution.py:129
  234.5 1.3 shard_map.310
  235.8 1.5 shard_map.314
  (216 shorter events, 70.4 us)
Async XLA Ops:
  7.2 61.8 %all-gather.8.cloned.1.call-start = ((), (), s32[]{:S(2)}) async-start(), calls=%async_computation.1 | async-start | bytes 1802240 | tf_op jit(solution)/shard_map/all_gather | solution.py:420
  13.3 13.8 %collective-permute-start.2 = (f32[448,256]{1,0:T(8,128)S(1)}, f32[448,256]{1,0:T(8,128)S(1)}, u32[]{:S(2)}, u32[]{:S(2)}) collective-permute-start(f32[448,256]{1,0:T(8,128)S(1)} %add.161), channel_id=1, source_target_pairs={{0,2},{1,3},{2,0},{3,1},{4,6},{5,7},{6,4},{7,5},{8,10},{9,11},{10,... | collective-permute-start | bytes 1376264 | tf_op jit(solution)/shard_map/ppermute | solution.py:129
  19.6 9.6 %collective-permute-start = (f32[448,256]{1,0:T(8,128)S(1)}, f32[448,256]{1,0:T(8,128)S(1)}, u32[]{:S(2)}, u32[]{:S(2)}) collective-permute-start(f32[448,256]{1,0:T(8,128)S(1)} %get-tuple-element.128), channel_id=1, source_target_pairs={{0,1},{1,0},{2,3},{3,2},{4,5},{5,4},{6,7},{7,6},{8,9},{9,8},{10,11... | collective-permute-start | bytes 1376264 | tf_op jit(solution)/shard_map/ppermute | solution.py:129
  27.1 15.0 %collective-permute-start.7 = (f32[1152,128]{1,0:T(8,128)S(1)}, f32[1152,128]{1,0:T(8,128)}, u32[]{:S(2)}, u32[]{:S(2)}) collective-permute-start(f32[1152,128]{1,0:T(8,128)S(1)} %bitcast.91), channel_id=1, source_target_pairs={{0,2},{1,3},{2,0},{3,1},{4,6},{5,7},{6,4},{7,5},{8,10},{9,11},{10,... | collective-permute-start | bytes 1769480 | tf_op jit(solution)/shard_map/ppermute | solution.py:129
  31.8 4.7 %collective-permute-start.5 = (f32[40,128]{1,0:T(8,128)S(1)}, f32[40,128]{1,0:T(8,128)S(1)}, u32[]{:S(2)}, u32[]{:S(2)}) collective-permute-start(f32[40,128]{1,0:T(8,128)S(1)} %add.162), channel_id=1, source_target_pairs={{0,17},{1,16},{2,19},{3,18},{4,21},{5,20},{6,23},{7,22},{8,25},{9,... | collective-permute-start | bytes 61448 | tf_op jit(solution)/shard_map/ppermute | solution.py:129
  34.2 5.1 %collective-permute-start.6 = (f32[40,128]{1,0:T(8,128)S(1)}, f32[40,128]{1,0:T(8,128)S(1)}, u32[]{:S(2)}, u32[]{:S(2)}) collective-permute-start(f32[40,128]{1,0:T(8,128)S(1)} %add.162), channel_id=1, source_target_pairs={{0,25},{1,24},{2,27},{3,26},{4,29},{5,28},{6,31},{7,30},{8,17},{9,... | collective-permute-start | bytes 61448 | tf_op jit(solution)/shard_map/ppermute | solution.py:129
  35.5 3.8 %collective-permute-start.4 = (f32[40,128]{1,0:T(8,128)S(1)}, f32[40,128]{1,0:T(8,128)S(1)}, u32[]{:S(2)}, u32[]{:S(2)}) collective-permute-start(f32[40,128]{1,0:T(8,128)S(1)} %add.162), channel_id=1, source_target_pairs={{0,9},{1,8},{2,11},{3,10},{4,13},{5,12},{6,15},{7,14},{8,1},{9,0},... | collective-permute-start | bytes 61448 | tf_op jit(solution)/shard_map/ppermute | solution.py:129
  42.1 101.0 %all-gather.6.cloned.1.call-start = ((), (), s32[]{:S(2)}) async-start(), calls=%async_computation | async-start | bytes 1081344 | tf_op jit(solution)/shard_map/all_gather | solution.py:533
  42.2 7.4 %collective-permute-start.11 = (f32[1152,128]{1,0:T(8,128)S(1)}, f32[1152,128]{1,0:T(8,128)S(1)}, u32[]{:S(2)}, u32[]{:S(2)}) collective-permute-start(f32[1152,128]{1,0:T(8,128)S(1)} %bitcast.92), channel_id=1, source_target_pairs={{0,1},{1,0},{2,3},{3,2},{4,5},{5,4},{6,7},{7,6},{8,9},{9,8},{10,11... | collective-permute-start | bytes 1769480 | tf_op jit(solution)/shard_map/ppermute | solution.py:129
  42.2 7.3 %collective-permute-start.12 = (f32[1152,128]{1,0:T(8,128)}, f32[1152,128]{1,0:T(8,128)S(1)}, u32[]{:S(2)}, u32[]{:S(2)}) collective-permute-start(f32[1152,128]{1,0:T(8,128)} %collective-permute-done.7.refs_4_), channel_id=1, source_target_pairs={{0,1},{1,0},{2,3},{3,2},{4,5},{5,4},{6,7},{7,6},{8,9},{9,8},{10,11... | collective-permute-start | bytes 1769480 | tf_op jit(solution)/shard_map/ppermute | solution.py:129
  43.8 4.1 %collective-permute-start.10 = (f32[40,128]{1,0:T(8,128)S(1)}, f32[40,128]{1,0:T(8,128)S(1)}, u32[]{:S(2)}, u32[]{:S(2)}) collective-permute-start(f32[40,128]{1,0:T(8,128)S(1)} %add_add_fusion.3), channel_id=1, source_target_pairs={{0,7},{1,6},{2,5},{3,4},{4,3},{5,2},{6,1},{7,0},{8,15},{9,14},{10,... | collective-permute-start | bytes 61448 | tf_op jit(solution)/shard_map/ppermute | solution.py:129
  45.4 3.6 %collective-permute-start.8 = (f32[40,128]{1,0:T(8,128)S(1)}, f32[40,128]{1,0:T(8,128)S(1)}, u32[]{:S(2)}, u32[]{:S(2)}) collective-permute-start(f32[40,128]{1,0:T(8,128)S(1)} %add_add_fusion.3), channel_id=1, source_target_pairs={{0,3},{1,2},{2,1},{3,0},{4,7},{5,6},{6,5},{7,4},{8,11},{9,10},{10,... | collective-permute-start | bytes 61448 | tf_op jit(solution)/shard_map/ppermute | solution.py:129
  56.6 4.0 %collective-permute-start.15 = (f32[2,512]{1,0:T(2,128)S(1)}, f32[2,512]{1,0:T(2,128)S(1)}, u32[]{:S(2)}, u32[]{:S(2)}) collective-permute-start(f32[2,512]{1,0:T(2,128)S(1)} %add.169), channel_id=1, source_target_pairs={{0,17},{1,16},{2,19},{3,18},{4,21},{5,20},{6,23},{7,22},{8,25},{9,... | collective-permute-start | bytes 12296 | tf_op jit(solution)/shard_map/ppermute | solution.py:129
  59.0 4.8 %collective-permute-start.16 = (f32[2,512]{1,0:T(2,128)S(1)}, f32[2,512]{1,0:T(2,128)S(1)}, u32[]{:S(2)}, u32[]{:S(2)}) collective-permute-start(f32[2,512]{1,0:T(2,128)S(1)} %add.169), channel_id=1, source_target_pairs={{0,25},{1,24},{2,27},{3,26},{4,29},{5,28},{6,31},{7,30},{8,17},{9,... | collective-permute-start | bytes 12296 | tf_op jit(solution)/shard_map/ppermute | solution.py:129
  60.2 3.6 %collective-permute-start.14 = (f32[2,512]{1,0:T(2,128)S(1)}, f32[2,512]{1,0:T(2,128)S(1)}, u32[]{:S(2)}, u32[]{:S(2)}) collective-permute-start(f32[2,512]{1,0:T(2,128)S(1)} %add.169), channel_id=1, source_target_pairs={{0,9},{1,8},{2,11},{3,10},{4,13},{5,12},{6,15},{7,14},{8,1},{9,0},... | collective-permute-start | bytes 12296 | tf_op jit(solution)/shard_map/ppermute | solution.py:129
  64.9 3.9 %collective-permute-start.19 = (f32[2,512]{1,0:T(2,128)S(1)}, f32[2,512]{1,0:T(2,128)S(1)}, u32[]{:S(2)}, u32[]{:S(2)}) collective-permute-start(f32[2,512]{1,0:T(2,128)S(1)} %add_add_fusion.9), channel_id=1, source_target_pairs={{0,7},{1,6},{2,5},{3,4},{4,3},{5,2},{6,1},{7,0},{8,15},{9,14},{10,... | collective-permute-start | bytes 12296 | tf_op jit(solution)/shard_map/ppermute | solution.py:129
  71.0 94.5 %all-gather.10.cloned.1.call-start = ((), (), s32[]{:S(2)}) async-start(), calls=%async_computation.2 | async-start | bytes 2293760 | tf_op jit(solution)/shard_map/all_gather | solution.py:535
  72.5 3.9 %collective-permute-start.22 = (f32[2,128]{1,0:T(2,128)S(1)}, f32[2,128]{1,0:T(2,128)S(1)}, u32[]{:S(2)}, u32[]{:S(2)}) collective-permute-start(f32[2,128]{1,0:T(2,128)S(1)} %add.176), channel_id=1, source_target_pairs={{0,17},{1,16},{2,19},{3,18},{4,21},{5,20},{6,23},{7,22},{8,25},{9,... | collective-permute-start | bytes 3080 | tf_op jit(solution)/shard_map/ppermute | solution.py:129
  73.4 4.8 %collective-permute-start.23 = (f32[2,128]{1,0:T(2,128)S(1)}, f32[2,128]{1,0:T(2,128)S(1)}, u32[]{:S(2)}, u32[]{:S(2)}) collective-permute-start(f32[2,128]{1,0:T(2,128)S(1)} %add.176), channel_id=1, source_target_pairs={{0,25},{1,24},{2,27},{3,26},{4,29},{5,28},{6,31},{7,30},{8,17},{9,... | collective-permute-start | bytes 3080 | tf_op jit(solution)/shard_map/ppermute | solution.py:129
  74.3 3.9 %collective-permute-start.21 = (f32[2,128]{1,0:T(2,128)S(1)}, f32[2,128]{1,0:T(2,128)S(1)}, u32[]{:S(2)}, u32[]{:S(2)}) collective-permute-start(f32[2,128]{1,0:T(2,128)S(1)} %add.176), channel_id=1, source_target_pairs={{0,9},{1,8},{2,11},{3,10},{4,13},{5,12},{6,15},{7,14},{8,1},{9,0},... | collective-permute-start | bytes 3080 | tf_op jit(solution)/shard_map/ppermute | solution.py:129
  79.5 3.9 %collective-permute-start.26 = (f32[2,128]{1,0:T(2,128)S(1)}, f32[2,128]{1,0:T(2,128)S(1)}, u32[]{:S(2)}, u32[]{:S(2)}) collective-permute-start(f32[2,128]{1,0:T(2,128)S(1)} %add_add_fusion.13), channel_id=1, source_target_pairs={{0,7},{1,6},{2,5},{3,4},{4,3},{5,2},{6,1},{7,0},{8,15},{9,14},{10,... | collective-permute-start | bytes 3080 | tf_op jit(solution)/shard_map/ppermute | solution.py:129
  85.9 13.3 %collective-permute-start.32 = (f32[448,256]{1,0:T(8,128)S(1)}, f32[448,256]{1,0:T(8,128)S(1)}, u32[]{:S(2)}, u32[]{:S(2)}) collective-permute-start(f32[448,256]{1,0:T(8,128)S(1)} %get-tuple-element.151.refs_0_.refs_1_.refs_3_), channel_id=1, source_target_pairs={{0,2},{1,3},{2,0},{3,1},{4,6},{5,7},{6,4},{7,5},{8,10},{9,11},{10,... | collective-permute-start | bytes 1376264 | tf_op jit(solution)/shard_map/ppermute | solution.py:129
  90.6 4.0 %collective-permute-start.30 = (f32[8,256]{1,0:T(8,128)S(1)}, f32[8,256]{1,0:T(8,128)S(1)}, u32[]{:S(2)}, u32[]{:S(2)}) collective-permute-start(f32[8,256]{1,0:T(8,128)S(1)} %add.183), channel_id=1, source_target_pairs={{0,17},{1,16},{2,19},{3,18},{4,21},{5,20},{6,23},{7,22},{8,25},{9,... | collective-permute-start | bytes 24584 | tf_op jit(solution)/shard_map/ppermute | solution.py:129
  91.4 4.9 %collective-permute-start.31 = (f32[8,256]{1,0:T(8,128)S(1)}, f32[8,256]{1,0:T(8,128)S(1)}, u32[]{:S(2)}, u32[]{:S(2)}) collective-permute-start(f32[8,256]{1,0:T(8,128)S(1)} %add.183), channel_id=1, source_target_pairs={{0,25},{1,24},{2,27},{3,26},{4,29},{5,28},{6,31},{7,30},{8,17},{9,... | collective-permute-start | bytes 24584 | tf_op jit(solution)/shard_map/ppermute | solution.py:129
  99.2 5.2 %collective-permute-start.36 = (f32[448,256]{1,0:T(8,128)S(1)}, f32[448,256]{1,0:T(8,128)S(1)}, u32[]{:S(2)}, u32[]{:S(2)}) collective-permute-start(f32[448,256]{1,0:T(8,128)S(1)} %collective-permute-done.32.refs_1_), channel_id=1, source_target_pairs={{0,1},{1,0},{2,3},{3,2},{4,5},{5,4},{6,7},{7,6},{8,9},{9,8},{10,11... | collective-permute-start | bytes 1376264 | tf_op jit(solution)/shard_map/ppermute | solution.py:129
  100.3 4.0 %collective-permute-start.35 = (f32[8,256]{1,0:T(8,128)S(1)}, f32[8,256]{1,0:T(8,128)S(1)}, u32[]{:S(2)}, u32[]{:S(2)}) collective-permute-start(f32[8,256]{1,0:T(8,128)S(1)} %add_add_fusion.7), channel_id=1, source_target_pairs={{0,7},{1,6},{2,5},{3,4},{4,3},{5,2},{6,1},{7,0},{8,15},{9,14},{10,... | collective-permute-start | bytes 24584 | tf_op jit(solution)/shard_map/ppermute | solution.py:129
  112.3 13.1 %collective-permute-start.39 = (f32[448,256]{1,0:T(8,128)S(1)}, f32[448,256]{1,0:T(8,128)S(1)}, u32[]{:S(2)}, u32[]{:S(2)}) collective-permute-start(f32[448,256]{1,0:T(8,128)S(1)} %add.190), channel_id=1, source_target_pairs={{0,2},{1,3},{2,0},{3,1},{4,6},{5,7},{6,4},{7,5},{8,10},{9,11},{10,... | collective-permute-start | bytes 1376264 | tf_op jit(solution)/shard_map/ppermute | solution.py:129
  119.8 4.0 %collective-permute-start.42 = (f32[8,256]{1,0:T(8,128)S(1)}, f32[8,256]{1,0:T(8,128)S(1)}, u32[]{:S(2)}, u32[]{:S(2)}) collective-permute-start(f32[8,256]{1,0:T(8,128)S(1)} %add.191), channel_id=1, source_target_pairs={{0,17},{1,16},{2,19},{3,18},{4,21},{5,20},{6,23},{7,22},{8,25},{9,... | collective-permute-start | bytes 24584 | tf_op jit(solution)/shard_map/ppermute | solution.py:129
  120.4 4.9 %collective-permute-start.43 = (f32[8,256]{1,0:T(8,128)S(1)}, f32[8,256]{1,0:T(8,128)S(1)}, u32[]{:S(2)}, u32[]{:S(2)}) collective-permute-start(f32[8,256]{1,0:T(8,128)S(1)} %add.191), channel_id=1, source_target_pairs={{0,25},{1,24},{2,27},{3,26},{4,29},{5,28},{6,31},{7,30},{8,17},{9,... | collective-permute-start | bytes 24584 | tf_op jit(solution)/shard_map/ppermute | solution.py:129
  122.8 7.9 %collective-permute-start.38 = (f32[448,256]{1,0:T(8,128)S(1)}, f32[448,256]{1,0:T(8,128)S(1)}, u32[]{:S(2)}, u32[]{:S(2)}) collective-permute-start(f32[448,256]{1,0:T(8,128)S(1)} %get-tuple-element.163), channel_id=1, source_target_pairs={{0,1},{1,0},{2,3},{3,2},{4,5},{5,4},{6,7},{7,6},{8,9},{9,8},{10,11... | collective-permute-start | bytes 1376264 | tf_op jit(solution)/shard_map/ppermute | solution.py:129
  126.6 4.0 %collective-permute-start.46 = (f32[8,256]{1,0:T(8,128)S(1)}, f32[8,256]{1,0:T(8,128)S(1)}, u32[]{:S(2)}, u32[]{:S(2)}) collective-permute-start(f32[8,256]{1,0:T(8,128)S(1)} %add_add_fusion.5), channel_id=1, source_target_pairs={{0,7},{1,6},{2,5},{3,4},{4,3},{5,2},{6,1},{7,0},{8,15},{9,14},{10,... | collective-permute-start | bytes 24584 | tf_op jit(solution)/shard_map/ppermute | solution.py:129
  135.7 5.5 %collective-permute-start.49 = (f32[80,128]{1,0:T(8,128)S(1)}, f32[80,128]{1,0:T(8,128)S(1)}, u32[]{:S(2)}, u32[]{:S(2)}) collective-permute-start(f32[80,128]{1,0:T(8,128)S(1)} %add.198), channel_id=1, source_target_pairs={{0,17},{1,16},{2,19},{3,18},{4,21},{5,20},{6,23},{7,22},{8,25},{9,... | collective-permute-start | bytes 122888 | tf_op jit(solution)/shard_map/ppermute | solution.py:129
  136.7 5.5 %collective-permute-start.50 = (f32[80,128]{1,0:T(8,128)S(1)}, f32[80,128]{1,0:T(8,128)S(1)}, u32[]{:S(2)}, u32[]{:S(2)}) collective-permute-start(f32[80,128]{1,0:T(8,128)S(1)} %add.198), channel_id=1, source_target_pairs={{0,25},{1,24},{2,27},{3,26},{4,29},{5,28},{6,31},{7,30},{8,17},{9,... | collective-permute-start | bytes 122888 | tf_op jit(solution)/shard_map/ppermute | solution.py:129
  138.4 4.6 %collective-permute-start.48 = (f32[80,128]{1,0:T(8,128)S(1)}, f32[80,128]{1,0:T(8,128)S(1)}, u32[]{:S(2)}, u32[]{:S(2)}) collective-permute-start(f32[80,128]{1,0:T(8,128)S(1)} %add.198), channel_id=1, source_target_pairs={{0,9},{1,8},{2,11},{3,10},{4,13},{5,12},{6,15},{7,14},{8,1},{9,0},... | collective-permute-start | bytes 122888 | tf_op jit(solution)/shard_map/ppermute | solution.py:129
  145.0 3.5 %collective-permute-start.52 = (f32[80,128]{1,0:T(8,128)S(1)}, f32[80,128]{1,0:T(8,128)S(1)}, u32[]{:S(2)}, u32[]{:S(2)}) collective-permute-start(f32[80,128]{1,0:T(8,128)S(1)} %add_add_fusion.1), channel_id=1, source_target_pairs={{0,5},{1,4},{2,7},{3,6},{4,1},{5,0},{6,3},{7,2},{8,13},{9,12},{10,... | collective-permute-start | bytes 122888 | tf_op jit(solution)/shard_map/ppermute | solution.py:129
  146.3 4.3 %collective-permute-start.53 = (f32[80,128]{1,0:T(8,128)S(1)}, f32[80,128]{1,0:T(8,128)S(1)}, u32[]{:S(2)}, u32[]{:S(2)}) collective-permute-start(f32[80,128]{1,0:T(8,128)S(1)} %add_add_fusion.1), channel_id=1, source_target_pairs={{0,7},{1,6},{2,5},{3,4},{4,3},{5,2},{6,1},{7,0},{8,15},{9,14},{10,... | collective-permute-start | bytes 122888 | tf_op jit(solution)/shard_map/ppermute | solution.py:129
  147.4 4.5 %collective-permute-start.51 = (f32[80,128]{1,0:T(8,128)S(1)}, f32[80,128]{1,0:T(8,128)S(1)}, u32[]{:S(2)}, u32[]{:S(2)}) collective-permute-start(f32[80,128]{1,0:T(8,128)S(1)} %add_add_fusion.1), channel_id=1, source_target_pairs={{0,3},{1,2},{2,1},{3,0},{4,7},{5,6},{6,5},{7,4},{8,11},{9,10},{10,... | collective-permute-start | bytes 122888 | tf_op jit(solution)/shard_map/ppermute | solution.py:129
  154.5 14.6 %collective-permute-start.57 = (f32[456,128]{1,0:T(8,128)S(1)}, f32[456,128]{1,0:T(8,128)}, u32[]{:S(2)}, u32[]{:S(2)}) collective-permute-start(f32[456,128]{1,0:T(8,128)S(1)} %get-tuple-element.200), channel_id=1, source_target_pairs={{0,1},{1,0},{2,3},{3,2},{4,5},{5,4},{6,7},{7,6},{8,9},{9,8},{10,11... | collective-permute-start | bytes 700424 | tf_op jit(solution)/shard_map/ppermute | solution.py:129
  154.7 14.4 %collective-permute-start.58 = (f32[456,128]{1,0:T(8,128)S(1)}, f32[456,128]{1,0:T(8,128)}, u32[]{:S(2)}, u32[]{:S(2)}) collective-permute-start(f32[456,128]{1,0:T(8,128)S(1)} %get-tuple-element.201), channel_id=1, source_target_pairs={{0,2},{1,3},{2,0},{3,1},{4,6},{5,7},{6,4},{7,5},{8,10},{9,11},{10,... | collective-permute-start | bytes 700424 | tf_op jit(solution)/shard_map/ppermute | solution.py:129
  155.7 13.4 %collective-permute-start.59 = (f32[456,128]{1,0:T(8,128)S(1)}, f32[456,128]{1,0:T(8,128)}, u32[]{:S(2)}, u32[]{:S(2)}) collective-permute-start(f32[456,128]{1,0:T(8,128)S(1)} %get-tuple-element.202), channel_id=1, source_target_pairs={{0,3},{1,2},{2,1},{3,0},{4,7},{5,6},{6,5},{7,4},{8,11},{9,10},{10,... | collective-permute-start | bytes 700424 | tf_op jit(solution)/shard_map/ppermute | solution.py:129
  168.1 12.9 %collective-permute-start.54 = (f32[448,256]{1,0:T(8,128)S(1)}, f32[448,256]{1,0:T(8,128)S(1)}, u32[]{:S(2)}, u32[]{:S(2)}) collective-permute-start(f32[448,256]{1,0:T(8,128)S(1)} %get-tuple-element.192.refs_0_), channel_id=1, source_target_pairs={{0,2},{1,3},{2,0},{3,1},{4,6},{5,7},{6,4},{7,5},{8,10},{9,11},{10,... | collective-permute-start | bytes 1376264 | tf_op jit(solution)/shard_map/ppermute | solution.py:129
  173.6 12.7 %collective-permute-start.75 = (f32[896,128]{1,0:T(8,128)S(1)}, f32[896,128]{1,0:T(8,128)S(1)}, u32[]{:S(2)}, u32[]{:S(2)}) collective-permute-start(f32[896,128]{1,0:T(8,128)S(1)} %get-tuple-element.208), channel_id=1, source_target_pairs={{0,4},{4,0},{8,12},{12,8},{16,20},{20,16},{24,28},{28,24},{1,5},{5... | collective-permute-start | bytes 1376264 | tf_op jit(solution)/shard_map/ppermute | solution.py:129
  175.6 3.9 %collective-permute-start.62 = (f32[2,256]{1,0:T(2,128)S(1)}, f32[2,256]{1,0:T(2,128)S(1)}, u32[]{:S(2)}, u32[]{:S(2)}) collective-permute-start(f32[2,256]{1,0:T(2,128)S(1)} %add.205), channel_id=1, source_target_pairs={{0,17},{1,16},{2,19},{3,18},{4,21},{5,20},{6,23},{7,22},{8,25},{9,... | collective-permute-start | bytes 6152 | tf_op jit(solution)/shard_map/ppermute | solution.py:129
  176.3 4.8 %collective-permute-start.63 = (f32[2,256]{1,0:T(2,128)S(1)}, f32[2,256]{1,0:T(2,128)S(1)}, u32[]{:S(2)}, u32[]{:S(2)}) collective-permute-start(f32[2,256]{1,0:T(2,128)S(1)} %add.205), channel_id=1, source_target_pairs={{0,25},{1,24},{2,27},{3,26},{4,29},{5,28},{6,31},{7,30},{8,17},{9,... | collective-permute-start | bytes 6152 | tf_op jit(solution)/shard_map/ppermute | solution.py:129
  179.5 13.3 %collective-permute-start.55 = (f32[448,256]{1,0:T(8,128)S(1)}, f32[448,256]{1,0:T(8,128)S(1)}, u32[]{:S(2)}, u32[]{:S(2)}) collective-permute-start(f32[448,256]{1,0:T(8,128)S(1)} %get-tuple-element.192.refs_0_), channel_id=1, source_target_pairs={{0,1},{1,0},{2,3},{3,2},{4,5},{5,4},{6,7},{7,6},{8,9},{9,8},{10,11... | collective-permute-start | bytes 1376264 | tf_op jit(solution)/shard_map/ppermute | solution.py:129
  181.0 11.8 %collective-permute-start.56 = (f32[448,256]{1,0:T(8,128)S(1)}, f32[448,256]{1,0:T(8,128)S(1)}, u32[]{:S(2)}, u32[]{:S(2)}) collective-permute-start(f32[448,256]{1,0:T(8,128)S(1)} %collective-permute-done.54.refs_1_), channel_id=1, source_target_pairs={{0,1},{1,0},{2,3},{3,2},{4,5},{5,4},{6,7},{7,6},{8,9},{9,8},{10,11... | collective-permute-start | bytes 1376264 | tf_op jit(solution)/shard_map/ppermute | solution.py:129
  181.2 7.1 %collective-permute-start.65 = (f32[2,256]{1,0:T(2,128)S(1)}, f32[2,256]{1,0:T(2,128)S(1)}, u32[]{:S(2)}, u32[]{:S(2)}) collective-permute-start(f32[2,256]{1,0:T(2,128)S(1)} %add_add_fusion.11), channel_id=1, source_target_pairs={{0,5},{1,4},{2,7},{3,6},{4,1},{5,0},{6,3},{7,2},{8,13},{9,12},{10,... | collective-permute-start | bytes 6152 | tf_op jit(solution)/shard_map/ppermute | solution.py:129
  182.5 6.3 %collective-permute-start.66 = (f32[2,256]{1,0:T(2,128)S(1)}, f32[2,256]{1,0:T(2,128)S(1)}, u32[]{:S(2)}, u32[]{:S(2)}) collective-permute-start(f32[2,256]{1,0:T(2,128)S(1)} %add_add_fusion.11), channel_id=1, source_target_pairs={{0,7},{1,6},{2,5},{3,4},{4,3},{5,2},{6,1},{7,0},{8,15},{9,14},{10,... | collective-permute-start | bytes 6152 | tf_op jit(solution)/shard_map/ppermute | solution.py:129
  186.3 4.5 %collective-permute-start.64 = (f32[2,256]{1,0:T(2,128)S(1)}, f32[2,256]{1,0:T(2,128)S(1)}, u32[]{:S(2)}, u32[]{:S(2)}) collective-permute-start(f32[2,256]{1,0:T(2,128)S(1)} %add_add_fusion.11), channel_id=1, source_target_pairs={{0,3},{1,2},{2,1},{3,0},{4,7},{5,6},{6,5},{7,4},{8,11},{9,10},{10,... | collective-permute-start | bytes 6152 | tf_op jit(solution)/shard_map/ppermute | solution.py:129
  188.3 12.3 %collective-permute-start.76 = (f32[224,128]{1,0:T(8,128)S(1)}, f32[224,128]{1,0:T(8,128)S(1)}, u32[]{:S(2)}, u32[]{:S(2)}) collective-permute-start(f32[224,128]{1,0:T(8,128)S(1)} %get-tuple-element.226), channel_id=1, source_target_pairs={{0,8},{4,12},{8,0},{12,4},{16,24},{20,28},{24,16},{28,20},{1,9},{5... | collective-permute-start | bytes 344072 | tf_op jit(solution)/shard_map/ppermute | solution.py:129
  188.8 11.9 %collective-permute-start.77 = (f32[224,128]{1,0:T(8,128)S(1)}, f32[224,128]{1,0:T(8,128)S(1)}, u32[]{:S(2)}, u32[]{:S(2)}) collective-permute-start(f32[224,128]{1,0:T(8,128)S(1)} %get-tuple-element.227), channel_id=1, source_target_pairs={{0,16},{4,20},{8,24},{12,28},{16,0},{20,4},{24,8},{28,12},{1,17},{... | collective-permute-start | bytes 344072 | tf_op jit(solution)/shard_map/ppermute | solution.py:129
  190.8 9.9 %collective-permute-start.78 = (f32[224,128]{1,0:T(8,128)S(1)}, f32[224,128]{1,0:T(8,128)S(1)}, u32[]{:S(2)}, u32[]{:S(2)}) collective-permute-start(f32[224,128]{1,0:T(8,128)S(1)} %get-tuple-element.228), channel_id=1, source_target_pairs={{0,24},{4,28},{8,16},{12,20},{16,8},{20,12},{24,0},{28,4},{1,25},{... | collective-permute-start | bytes 344072 | tf_op jit(solution)/shard_map/ppermute | solution.py:129
  195.5 12.3 %collective-permute-start.67 = (f32[256,128]{1,0:T(8,128)S(1)}, f32[256,128]{1,0:T(8,128)S(1)}, u32[]{:S(2)}, u32[]{:S(2)}) collective-permute-start(f32[256,128]{1,0:T(8,128)S(1)} %get-tuple-element.218), channel_id=1, source_target_pairs={{0,4},{4,0},{8,12},{12,8},{16,20},{20,16},{24,28},{28,24},{1,5},{5... | collective-permute-start | bytes 393224 | tf_op jit(solution)/shard_map/ppermute | solution.py:129
  201.3 9.5 %collective-permute-start.79 = (f32[224,128]{1,0:T(8,128)S(1)}, f32[224,128]{1,0:T(8,128)S(1)}, u32[]{:S(2)}, u32[]{:S(2)}) collective-permute-start(f32[224,128]{1,0:T(8,128)S(1)} %shard_map.312.refs_0_), channel_id=1, source_target_pairs={{0,8},{4,12},{8,0},{12,4},{16,24},{20,28},{24,16},{28,20},{1,9},{5... | collective-permute-start | bytes 344072 | tf_op jit(solution)/shard_map/ppermute | solution.py:129
  204.8 12.6 %collective-permute-start.80 = (f32[224,128]{1,0:T(8,128)S(1)}, f32[224,128]{1,0:T(8,128)S(1)}, u32[]{:S(2)}, u32[]{:S(2)}) collective-permute-start(f32[224,128]{1,0:T(8,128)S(1)} %shard_map.312.refs_0_), channel_id=1, source_target_pairs={{0,16},{4,20},{8,24},{12,28},{16,0},{20,4},{24,8},{28,12},{1,17},{... | collective-permute-start | bytes 344072 | tf_op jit(solution)/shard_map/ppermute | solution.py:129
  205.1 12.3 %collective-permute-start.81 = (f32[224,128]{1,0:T(8,128)S(1)}, f32[224,128]{1,0:T(8,128)S(1)}, u32[]{:S(2)}, u32[]{:S(2)}) collective-permute-start(f32[224,128]{1,0:T(8,128)S(1)} %shard_map.312.refs_0_), channel_id=1, source_target_pairs={{0,24},{4,28},{8,16},{12,20},{16,8},{20,12},{24,0},{28,4},{1,25},{... | collective-permute-start | bytes 344072 | tf_op jit(solution)/shard_map/ppermute | solution.py:129
  208.4 10.3 %collective-permute-start.68 = (f32[64,128]{1,0:T(8,128)S(1)}, f32[64,128]{1,0:T(8,128)S(1)}, u32[]{:S(2)}, u32[]{:S(2)}) collective-permute-start(f32[64,128]{1,0:T(8,128)S(1)} %get-tuple-element.220), channel_id=1, source_target_pairs={{0,8},{4,12},{8,0},{12,4},{16,24},{20,28},{24,16},{28,20},{1,9},{5... | collective-permute-start | bytes 98312 | tf_op jit(solution)/shard_map/ppermute | solution.py:129
  209.6 10.6 %collective-permute-start.69 = (f32[64,128]{1,0:T(8,128)S(1)}, f32[64,128]{1,0:T(8,128)S(1)}, u32[]{:S(2)}, u32[]{:S(2)}) collective-permute-start(f32[64,128]{1,0:T(8,128)S(1)} %get-tuple-element.221), channel_id=1, source_target_pairs={{0,16},{4,20},{8,24},{12,28},{16,0},{20,4},{24,8},{28,12},{1,17},{... | collective-permute-start | bytes 98312 | tf_op jit(solution)/shard_map/ppermute | solution.py:129
  210.8 9.4 %collective-permute-start.70 = (f32[64,128]{1,0:T(8,128)S(1)}, f32[64,128]{1,0:T(8,128)S(1)}, u32[]{:S(2)}, u32[]{:S(2)}) collective-permute-start(f32[64,128]{1,0:T(8,128)S(1)} %get-tuple-element.222), channel_id=1, source_target_pairs={{0,24},{4,28},{8,16},{12,20},{16,8},{20,12},{24,0},{28,4},{1,25},{... | collective-permute-start | bytes 98312 | tf_op jit(solution)/shard_map/ppermute | solution.py:129
  218.0 17.8 %collective-permute-start.82 = (f32[896,128]{1,0:T(8,128)S(1)}, f32[896,128]{1,0:T(8,128)S(1)}, u32[]{:S(2)}, u32[]{:S(2)}) collective-permute-start(f32[896,128]{1,0:T(8,128)S(1)} %shard_map.313.refs_0_), channel_id=1, source_target_pairs={{0,4},{4,0},{8,12},{12,8},{16,20},{20,16},{24,28},{28,24},{1,5},{5... | collective-permute-start | bytes 1376264 | tf_op jit(solution)/shard_map/ppermute | solution.py:129
  220.8 5.0 %collective-permute-start.71 = (f32[64,128]{1,0:T(8,128)S(1)}, f32[64,128]{1,0:T(8,128)S(1)}, u32[]{:S(2)}, u32[]{:S(2)}) collective-permute-start(f32[64,128]{1,0:T(8,128)S(1)} %shard_map.308.refs_0_), channel_id=1, source_target_pairs={{0,8},{4,12},{8,0},{12,4},{16,24},{20,28},{24,16},{28,20},{1,9},{5... | collective-permute-start | bytes 98312 | tf_op jit(solution)/shard_map/ppermute | solution.py:129
  222.3 5.1 %collective-permute-start.72 = (f32[64,128]{1,0:T(8,128)S(1)}, f32[64,128]{1,0:T(8,128)S(1)}, u32[]{:S(2)}, u32[]{:S(2)}) collective-permute-start(f32[64,128]{1,0:T(8,128)S(1)} %shard_map.308.refs_0_), channel_id=1, source_target_pairs={{0,16},{4,20},{8,24},{12,28},{16,0},{20,4},{24,8},{28,12},{1,17},{... | collective-permute-start | bytes 98312 | tf_op jit(solution)/shard_map/ppermute | solution.py:129
  223.2 5.7 %collective-permute-start.73 = (f32[64,128]{1,0:T(8,128)S(1)}, f32[64,128]{1,0:T(8,128)S(1)}, u32[]{:S(2)}, u32[]{:S(2)}) collective-permute-start(f32[64,128]{1,0:T(8,128)S(1)} %shard_map.308.refs_0_), channel_id=1, source_target_pairs={{0,24},{4,28},{8,16},{12,20},{16,8},{20,12},{24,0},{28,4},{1,25},{... | collective-permute-start | bytes 98312 | tf_op jit(solution)/shard_map/ppermute | solution.py:129
  229.4 5.0 %collective-permute-start.74 = (f32[256,128]{1,0:T(8,128)S(1)}, f32[256,128]{1,0:T(8,128)S(1)}, u32[]{:S(2)}, u32[]{:S(2)}) collective-permute-start(f32[256,128]{1,0:T(8,128)S(1)} %shard_map.309.refs_0_), channel_id=1, source_target_pairs={{0,4},{4,0},{8,12},{12,8},{16,20},{20,16},{24,28},{28,24},{1,5},{5... | collective-permute-start | bytes 393224 | tf_op jit(solution)/shard_map/ppermute | solution.py:129
  (40 other events, 305.6 us)
Sparse Core Ops, SparseCore 0:
  42.2 20.0 all-gather.7
  71.2 52.5 all-gather.5
  125.4 20.5 all-gather.9

commit v3 on v2

--- a/solution.py
+++ b/solution.py
@@ -594,8 +594,8 @@
             n = len(rels)
             atts, (x_ref, g_ref, w_ref, sums, eg) = refs[:n], refs[n : n + 5]
             prev, refs = refs[n + 5 : n + 5 + extra], refs[n + 5 + extra :]
-            bos, gas = refs[:n], refs[n : 2 * n]
-            sg, t1, t2, u1, scr = refs[2 * n :]
+            bos, gas, dzs = refs[:n], refs[n : 2 * n], refs[2 * n : 3 * n]
+            sg, t1, t2, u1, scr = refs[3 * n :]
             avg, inv, _ = stats(mine_of(sums), s)
             arrive(n + 2)
             w = split2(w_ref[...])
@@ -614,6 +614,7 @@
                 if k == 0:
                     arrive(n + 1)
                 g = load_quarter(g_ref, scr, r, on)
+                dzs[k][...] = g
                 sg_acc[0] += colsum(g)
                 sg_acc[1] += colsum(g * norm)
                 gb = g.astype(BF16)
@@ -640,21 +641,23 @@
                 [att_r[r] for r in rels] + [feats, gouts, expand_weight, s3, eg] + prev,
                 [((R, win), F32)] * n
                 + [((R, mid), F32)] * n
+                + [((R, win), F32)] * n
                 + [((2 * nc, win), F32), ((mid, win), F32), ((mid, win), F32), ((1, mid), F32)],
                 [quarter_scratch],
                 flops=12 * R * mid * win * n,
                 far=(n, n + 1, n + 2),
-                far_out=tuple(range(n)) + ((2 * n + 1, 2 * n + 2) if prev else ()),
+                far_out=tuple(range(n)) + tuple(range(2 * n, 3 * n)) + ((3 * n + 1, 3 * n + 2) if prev else ()),
                 lazy=True,
             )
 
-        bo3, bo1, ga3, ga1, *prev = expand_call((3, 1), [])
+        bo3, bo1, ga3, ga1, dz3, dz1_, *prev = expand_call((3, 1), [])
         gy1 = ga1 + swap(ga3, "chan", 1)
-        bo2, bo0, ga2, ga0, sg3, t1, t2, u1 = expand_call((2, 0), [after(prev[0], gy1)] + list(prev[1:]))
+        bo2, bo0, ga2, ga0, dz2, dz0, sg3, t1, t2, u1 = expand_call((2, 0), [after(prev[0], gy1)] + list(prev[1:]))
         gys = swap(gy1, "chan", 2)
         grc = swap(ga2, "chan", 1)
         sg3 = sum_steps(sg3, (gys,))[-1]
         bos = [bo0, bo1, bo2, bo3]
+        masked = [dz0, dz1_, dz2, dz3]
 
         def gatt_body(s, p, rc, ys, att, we, g3, sums, sg, spl, sums2, vec, wts, sfc, sq, sgb, wat, ga, l0, l1, l2, l3, merged, scr):
             m_acc, v_acc = 0.0, 0.0
@@ -899,23 +902,21 @@
             prep_body, image_counts, [after(red_g, gs), s1, vec], [((nc * R, mid), BF16)] * 2, far=(0,)
         )
 
-        def masked_body(s, b0, b1, b2, b3, go, m0, m1, m2, m3, out_bo, scr):
-            for r, (b, o) in enumerate(((b0, m0), (b1, m1), (b2, m2), (b3, m3))):
-                bo = b[...]
-                o[...] = load_quarter(go, scr, r, bo > 0)
-                store_quarter(out_bo, scr, r, bo)
-
-        *masked, block_out = call(
-            masked_body,
+        def store_body(s, b0, b1, b2, b3, out_bo, scr):
+            for r, b in enumerate((b0, b1, b2, b3)):
+                store_quarter(out_bo, scr, r, b[...])
+
+        (block_out,) = call(
+            store_body,
             image_counts,
-            [after(bos[0], gs)] + bos[1:] + [gouts],
-            [((R, win), F32)] * 4 + [(feats.shape, F32)],
+            [after(bos[0], gs)] + bos[1:],
+            [(feats.shape, F32)],
             [quarter_scratch],
-            far=(0, 1, 2, 3, 4),
-            far_out=(0, 1, 2, 3, 4),
-        )
-
-        dz1_y = swap(after(dz1, relu_all, masked[0]), "chan", 2)
+            far=(0, 1, 2, 3),
+            far_out=(0,),
+        )
+
+        dz1_y = swap(after(dz1, relu_all, block_out), "chan", 2)
 
         n_w = 9 * 2 * lw
         n_dws = padded_rows(n_w + lb * mid + 2 * lw)
@@ -951,7 +952,7 @@
         *dws, sg3l = call(
             dws_body,
             image_counts,
-            blks + [relu_all, after(hid_all, masked[0]), t1, t2, u1, s3, sg3, eg],
+            blks + [relu_all, after(hid_all, block_out), t1, t2, u1, s3, sg3, eg],
             chunk_outs(n_dws, groups[0]) + [((2, win), F32)],
             [pltpu.VMEM((3, slots, PAD, PAD, 2 * lw), BF16), pltpu.VMEM((n_dws, 128), F32)],
             flops=2 * nc * R * mid * 9 * 2 * lw,

time: 245 us -> 244 us (level)
  transfers between devices with their start and end apart: 86 -> 86, of which waited for: 49 -> 48; matrix products, arithmetic and copies ran while one was open for 2% -> 2% of each run, Pallas kernels for 25% -> 25%
where the time goes in v3:
time: 244 us
  starting transfers between devices  80.1 us (33%)
  waiting for transfers between devices  74 us (30%)
  Pallas kernels  68.4 us (28%)
  between operations  14.3 us (6%)
  local copies, waits for them, and re-layouts  5.59 us (2%)
    ppermute x83, starting transfers between devices, swap(): return lax.ppermute(x, axis, [(i, i ^ k) for i in range(n)])  79.8 us
    ppermute x83, waiting for transfers between devices, swap(): return lax.ppermute(x, axis, [(i, i ^ k) for i in range(n)])  73.9 us
    pallas_call x28, Pallas kernels, call(): pl.pallas_call(kernel, out_shape=[pltpu.HBM(s, d) if k in far_out else ja...  68.4 us
  transfers between devices with their start and end apart: 86, of which 48 were waited for; matrix products, arithmetic and copies ran while one was open for 2% of the time, Pallas kernels for 25%

profile of v3, /device:TPU:0, one launch (start us, length us, event | category | flops | bytes accessed | tf_op | source)
XLA Modules:
  0.0 243.5 jit_solution(472684414958680839)
XLA Ops:
  7.9 3.3 %shard_map.289 = (f32[448,256]{1,0:T(8,128)S(1)}, f32[448,256]{1,0:T(8,128)S(1)}, bf16[448,256]{1,0:T(8,128)(2,1)}, bf16[448,256]{1,0:T(8,128)(2,1)}) custom-call(s32[8]{0:T(128)S(1)} %copy-done, f32[3136,128]{1,0:T(8,128)} %bitcast.71, f32[256,256]{1,0:T(8,128)} %refs_8_.1), custom_call_target="tpu_custom_call" | custom-call | flops 704643072 | bytes 3244032 | tf_op jit(solution)/shard_map/pallas_call | solution.py:99
  11.7 1.4 collective-permute-done.1
  13.4 3.0 %collective-permute-start.2 = (f32[448,256]{1,0:T(8,128)S(1)}, f32[448,256]{1,0:T(8,128)S(1)}, u32[]{:S(2)}, u32[]{:S(2)}) collective-permute-start(f32[448,256]{1,0:T(8,128)S(1)} %add.161), channel_id=1, source_target_pairs={{0,2},{1,3},{2,0},{3,1},{4,6},{5,7},{6,4},{7,5},{8,10},{9,11},{10,... | collective-permute-start | bytes 1376264 | tf_op jit(solution)/shard_map/ppermute | solution.py:129
  16.3 3.3 %shard_map.288 = (f32[448,256]{1,0:T(8,128)S(1)}, f32[448,256]{1,0:T(8,128)S(1)}, bf16[448,256]{1,0:T(8,128)(2,1)}, bf16[448,256]{1,0:T(8,128)(2,1)}) custom-call(s32[8]{0:T(128)S(1)} %copy-done, f32[3136,128]{1,0:T(8,128)} %bitcast.72, f32[256,256]{1,0:T(8,128)} %refs_8_.1), custom_call_target="tpu_custom_call" | custom-call | flops 704643072 | bytes 3244032 | tf_op jit(solution)/shard_map/pallas_call | solution.py:99
  19.7 7.4 %collective-permute-done.2.refs_2_ = f32[448,256]{1,0:T(8,128)S(1)} collective-permute-done((f32[448,256]{1,0:T(8,128)S(1)}, f32[448,256]{1,0:T(8,128)S(1)}, u32[]{:S(2)}, u32[]{:S(2)}) %collective-permute-start.2) | collective-permute-done | bytes 458784 | tf_op jit(solution)/shard_map/ppermute | solution.py:129
  27.1 1.7 collective-permute-start.7
  29.3 1.4 shard_map.290
  31.8 2.4 collective-permute-start.5
  34.2 1.3 collective-permute-start.6
  36.5 2.8 %collective-permute-done.6 = f32[40,128]{1,0:T(8,128)S(1)} collective-permute-done((f32[40,128]{1,0:T(8,128)S(1)}, f32[40,128]{1,0:T(8,128)S(1)}, u32[]{:S(2)}, u32[]{:S(2)}) %collective-permute-start.6) | collective-permute-done | bytes 20512 | tf_op jit(solution)/shard_map/ppermute | solution.py:129
  39.3 2.8 %collective-permute-done.7.refs_4_ = f32[1152,128]{1,0:T(8,128)} collective-permute-done((f32[1152,128]{1,0:T(8,128)S(1)}, f32[1152,128]{1,0:T(8,128)}, u32[]{:S(2)}, u32[]{:S(2)}) %collective-permute-start.7) | collective-permute-done | bytes 589856 | tf_op jit(solution)/shard_map/ppermute | solution.py:129
  43.8 1.5 collective-permute-start.10
  46.0 2.0 collective-permute-done.10
  50.6 4.8 %shard_map.292 = (f32[448,512]{1,0:T(8,128)S(1)}, f32[2,512]{1,0:T(2,128)S(1)}, bf16[2,256,1152]{2,1,0:T(8,128)(2,1)}) custom-call(s32[8]{0:T(128)S(1)} %copy-done.1, f32[448,256]{1,0:T(8,128)} %get-tuple-element.186.refs_0_.refs_1_, f32[2,256]{1,0:T(2,128)S(1)} %get-tuple-element.140.refs_1_.refs_2_.refs_9_, ...), custom_call_target="tpu_custom_call" | custom-call | flops 1585446912 | bytes 4937728 | tf_op jit(solution)/shard_map/pallas_call | solution.py:99
  56.6 2.4 collective-permute-start.15
  60.6 3.3 %collective-permute-done.16 = f32[2,512]{1,0:T(2,128)S(1)} collective-permute-done((f32[2,512]{1,0:T(2,128)S(1)}, f32[2,512]{1,0:T(2,128)S(1)}, u32[]{:S(2)}, u32[]{:S(2)}) %collective-permute-start.16) | collective-permute-done | bytes 4128 | tf_op jit(solution)/shard_map/ppermute | solution.py:129
  67.1 1.8 collective-permute-done.19
  69.0 2.1 shard_map.293
  76.4 1.8 collective-permute-done.23
  79.5 1.3 collective-permute-start.26
  81.3 2.1 collective-permute-done.26
  83.8 2.0 shard_map.294
  86.7 2.7 %shard_map.295 = f32[8,256]{1,0:T(8,128)S(1)} custom-call(s32[8]{0:T(128)S(1)} %copy-done.1, f32[448,256]{1,0:T(8,128)S(1)} %get-tuple-element.150.refs_0_.refs_1_.refs_3_, f32[4,704,128]{2,1,0:T(8,128)} %bitcast.66), custom_call_target="tpu_custom_call" | custom-call | flops 704643072 | bytes 1908736 | tf_op jit(solution)/shard_map/pallas_call | solution.py:99
  91.4 1.7 collective-permute-start.31
  94.6 1.7 collective-permute-done.31
  96.3 2.9 %collective-permute-done.32.refs_1_ = f32[448,256]{1,0:T(8,128)S(1)} collective-permute-done((f32[448,256]{1,0:T(8,128)S(1)}, f32[448,256]{1,0:T(8,128)S(1)}, u32[]{:S(2)}, u32[]{:S(2)}) %collective-permute-start.32) | collective-permute-done | bytes 458784 | tf_op jit(solution)/shard_map/ppermute | solution.py:129
  102.5 1.7 collective-permute-done.35
  104.4 5.7 %shard_map.296 = (f32[448,256]{1,0:T(8,128)}, f32[448,256]{1,0:T(8,128)}, f32[448,256]{1,0:T(8,128)S(1)}, f32[448,256]{1,0:T(8,128)S(1)}, f32[448,256]{1,0:T(8,1...) custom-call(s32[8]{0:T(128)S(1)} %copy-done.1, ...), custom_call_target="tpu_custom_call" | custom-call | flops 704643072 | bytes 7687168 | tf_op jit(solution)/shard_map/pallas_call | solution.py:99
  111.1 1.4 collective-permute-done.37
  113.7 5.7 %shard_map.297 = (f32[448,256]{1,0:T(8,128)}, f32[448,256]{1,0:T(8,128)}, f32[448,256]{1,0:T(8,128)S(1)}, f32[448,256]{1,0:T(8,128)S(1)}, f32[448,256]{1,0:T(8,1...) custom-call(s32[8]{0:T(128)S(1)} %copy-done.1, ...), custom_call_target="tpu_custom_call" | custom-call | flops 704643072 | bytes 8220672 | tf_op jit(solution)/shard_map/pallas_call | solution.py:99
  121.3 1.8 collective-permute-start.43
  124.7 1.5 collective-permute-done.43
  129.4 2.1 collective-permute-done.46
  131.8 3.7 %shard_map.298 = (f32[448,256]{1,0:T(8,128)}, f32[8,128]{1,0:T(8,128)S(1)}, f32[8,128]{1,0:T(8,128)S(1)}, f32[8,128]{1,0:T(8,128)S(1)}, f32[8,128]{1,0:T(8,128)S(1)}, /*index=5*/f32[80,128]{1,0:T(8,128)S(1)}) custom-call(s32[8]{0:T(128)S(1)} %copy-done.1, f32[448,256]{1,0:T(8,128)S(1)} %get-tuple-element.161.refs_0_, ...), custom_call_target="tpu_custom_call" | custom-call | flops 192937984 | bytes 6219776 | tf_op jit(solution)/shard_map/pallas_call | solution.py:99
  137.5 1.8 collective-permute-start.50
  139.8 2.5 %collective-permute-done.49 = f32[80,128]{1,0:T(8,128)S(1)} collective-permute-done((f32[80,128]{1,0:T(8,128)S(1)}, f32[80,128]{1,0:T(8,128)S(1)}, u32[]{:S(2)}, u32[]{:S(2)}) %collective-permute-start.49) | collective-permute-done | bytes 40992 | tf_op jit(solution)/shard_map/ppermute | solution.py:129
  144.0 1.9 shard_map.299
  145.9 1.5 collective-permute-start.52
  149.4 2.3 collective-permute-done.53
  153.0 2.5 %shard_map.300 = (f32[448,512]{1,0:T(8,128)S(1)}, f32[456,128]{1,0:T(8,128)S(1)}, f32[456,128]{1,0:T(8,128)S(1)}, f32[456,128]{1,0:T(8,128)S(1)}, f32[456,128]{1...) custom-call(s32[8]{0:T(128)S(1)} %copy-done.1, ...), custom_call_target="tpu_custom_call" | custom-call | bytes 5100544 | tf_op jit(solution)/shard_map/pallas_call | solution.py:99
  157.5 3.8 %shard_map.301 = f32[3136,128]{1,0:T(8,128)} custom-call(s32[8]{0:T(128)S(1)} %copy-done.1, f32[448,256]{1,0:T(8,128)} %get-tuple-element.180.refs_0_, f32[448,256]{1,0:T(8,128)} %get-tuple-element.181.refs_1_, f32[448,256]{1,0:T(8,128)} %get-tuple-element.182.refs_2_, f32[448,256]{1,0:T(8,128)} %get-tuple-element.183.refs_3_), custom_call_target="tpu_custom_call" | custom-call | bytes 3440640 | tf_op jit(solution)/shard_map/pallas_call | solution.py:99
  161.3 3.8 %shard_map.302 = (f32[448,256]{1,0:T(8,128)S(1)}, f32[2,256]{1,0:T(2,128)S(1)}) custom-call(s32[8]{0:T(128)S(1)} %copy-done.1, f32[448,512]{1,0:T(8,128)S(1)} %get-tuple-element.179.refs_0_, f32[448,256]{1,0:T(8,128)} %get-tuple-element.186.refs_0_.refs_1_, f32[2,256]{1,0:T(2,128)S(1)} %get-tuple-element.140.refs_1_.refs_2_.refs_9_, ...), custom_call_target="tpu_custom_call" | custom-call | flops 528482304 | bytes 3035136 | tf_op jit(solution)/shard_map/pallas_call | solution.py:99
  165.2 2.6 %shard_map.303 = (bf16[1792,256]{1,0:T(8,128)(2,1)S(1)}, bf16[1792,256]{1,0:T(8,128)(2,1)S(1)}) custom-call(s32[8]{0:T(128)S(1)} %copy-done.1, f32[4,448,256]{2,1,0:T(8,128)} %bitcast.77, f32[2,256]{1,0:T(2,128)S(1)} %get-tuple-element.140.refs_1_.refs_2_.refs_9_, f32[2,8,256]{2,1,0:T(8,128)S(1)} %get-tuple-element.141.refs_2_.refs_10_.refs_1_.refs_3_.refs_11_), custom_call_target="tpu_custom_call" | custom-call | bytes 3688448 | tf_op jit(solution)/shard_map/pallas_call | solution.py:99
  168.4 4.5 %shard_map.304 = (f32[896,128]{1,0:T(8,128)S(1)}, f32[896,128]{1,0:T(8,128)S(1)}, f32[2,256]{1,0:T(2,128)S(1)}) custom-call(s32[8]{0:T(128)S(1)} %copy-done.1, f32[456,128]{1,0:T(8,128)} %copy-done.2, f32[456,128]{1,0:T(8,128)} %collective-permute-done.57.refs_1_, f32[456,128]{1,0:T(8,128)} %collective-permute-done.58.refs_2_, ...), custom_call_target="tpu_custom_call" | custom-call | flops 1056964608 | bytes 3347456 | tf_op jit(solution)/shard_map/pallas_call | solution.py:99
  175.8 1.8 collective-permute-start.63
  179.1 1.5 collective-permute-done.54.refs_1_
  180.6 1.4 collective-permute-start.65
  183.0 2.6 %collective-permute-done.75.refs_1_ = f32[896,128]{1,0:T(8,128)S(1)} collective-permute-done((f32[896,128]{1,0:T(8,128)S(1)}, f32[896,128]{1,0:T(8,128)S(1)}, u32[]{:S(2)}, u32[]{:S(2)}) %collective-permute-start.75) | collective-permute-done | bytes 458784 | tf_op jit(solution)/shard_map/ppermute | solution.py:129
  188.3 1.6 collective-permute-start.77
  189.9 2.3 collective-permute-start.78
  192.2 2.7 %shard_map.305 = (f32[256,128]{1,0:T(8,128)S(1)}, f32[256,128]{1,0:T(8,128)S(1)}, bf16[448,256]{1,0:T(8,128)(2,1)S(1)}, bf16[448,256]{1,0:T(8,128)(2,1)S(1)}, bf...) custom-call(s32[8]{0:T(128)S(1)} %copy-done.1, f32[448,256]{1,0:T(8,128)S(1)} %get-tuple-element.189.refs_0_, ...), custom_call_target="tpu_custom_call" | custom-call | flops 234881024 | bytes 4870144 | tf_op jit(solution)/shard_map/pallas_call | solution.py:99
  195.8 4.2 %shard_map.306 = f32[3136,128]{1,0:T(8,128)} custom-call(s32[8]{0:T(128)S(1)} %copy-done.1, bf16[448,256]{1,0:T(8,128)(2,1)S(1)} %get-tuple-element.207.refs_0_, bf16[448,256]{1,0:T(8,128)(2,1)S(1)} %get-tuple-element.208.refs_1_, bf16[448,256]{1,0:T(8,128)(2,1)S(1)} %get-tuple-element.209.refs_2_, bf16[448,256]{1,0:T(8,128)(2,1)S(1)} %get-tuple-element.210.refs_3_, ...), custom_call_target="tpu_custom_call" | custom-call | flops 234881024 | bytes 4620288 | tf_op jit(solution)/shard_map/pallas_call | solution.py:99
  200.7 3.1 %collective-permute-start.79 = (f32[224,128]{1,0:T(8,128)S(1)}, f32[224,128]{1,0:T(8,128)S(1)}, u32[]{:S(2)}, u32[]{:S(2)}) collective-permute-start(f32[224,128]{1,0:T(8,128)S(1)} %shard_map.312.refs_0_), channel_id=1, source_target_pairs={{0,8},{4,12},{8,0},{12,4},{16,24},{20,28},{24,16},{28,20},{1,9},{5... | collective-permute-start | bytes 344072 | tf_op jit(solution)/shard_map/ppermute | solution.py:129
  204.6 2.2 collective-permute-start.81
  210.2 2.2 collective-permute-start.70
  213.1 4.0 %collective-permute-done.80.refs_2_ = f32[224,128]{1,0:T(8,128)S(1)} collective-permute-done((f32[224,128]{1,0:T(8,128)S(1)}, f32[224,128]{1,0:T(8,128)S(1)}, u32[]{:S(2)}, u32[]{:S(2)}) %collective-permute-start.80) | collective-permute-done | bytes 114720 | tf_op jit(solution)/shard_map/ppermute | solution.py:129
  218.6 1.5 collective-permute-done.69.refs_2_
  220.6 1.3 collective-permute-start.71
  222.8 2.3 collective-permute-start.73
  225.6 1.4 collective-permute-done.72.refs_2_
  227.1 1.4 collective-permute-done.73.refs_3_
  230.7 3.4 %collective-permute-done.74.refs_1_ = f32[256,128]{1,0:T(8,128)S(1)} collective-permute-done((f32[256,128]{1,0:T(8,128)S(1)}, f32[256,128]{1,0:T(8,128)S(1)}, u32[]{:S(2)}, u32[]{:S(2)}) %collective-permute-start.74) | collective-permute-done | bytes 131104 | tf_op jit(solution)/shard_map/ppermute | solution.py:129
  234.1 1.3 shard_map.310
  235.4 1.5 shard_map.314
  (216 shorter events, 69.8 us)
Async XLA Ops:
  7.2 61.8 %all-gather.8.cloned.1.call-start = ((), (), s32[]{:S(2)}) async-start(), calls=%async_computation.1 | async-start | bytes 1802240 | tf_op jit(solution)/shard_map/all_gather | solution.py:420
  13.4 13.8 %collective-permute-start.2 = (f32[448,256]{1,0:T(8,128)S(1)}, f32[448,256]{1,0:T(8,128)S(1)}, u32[]{:S(2)}, u32[]{:S(2)}) collective-permute-start(f32[448,256]{1,0:T(8,128)S(1)} %add.161), channel_id=1, source_target_pairs={{0,2},{1,3},{2,0},{3,1},{4,6},{5,7},{6,4},{7,5},{8,10},{9,11},{10,... | collective-permute-start | bytes 1376264 | tf_op jit(solution)/shard_map/ppermute | solution.py:129
  19.6 9.6 %collective-permute-start = (f32[448,256]{1,0:T(8,128)S(1)}, f32[448,256]{1,0:T(8,128)S(1)}, u32[]{:S(2)}, u32[]{:S(2)}) collective-permute-start(f32[448,256]{1,0:T(8,128)S(1)} %get-tuple-element.127), channel_id=1, source_target_pairs={{0,1},{1,0},{2,3},{3,2},{4,5},{5,4},{6,7},{7,6},{8,9},{9,8},{10,11... | collective-permute-start | bytes 1376264 | tf_op jit(solution)/shard_map/ppermute | solution.py:129
  27.1 15.0 %collective-permute-start.7 = (f32[1152,128]{1,0:T(8,128)S(1)}, f32[1152,128]{1,0:T(8,128)}, u32[]{:S(2)}, u32[]{:S(2)}) collective-permute-start(f32[1152,128]{1,0:T(8,128)S(1)} %bitcast.90), channel_id=1, source_target_pairs={{0,2},{1,3},{2,0},{3,1},{4,6},{5,7},{6,4},{7,5},{8,10},{9,11},{10,... | collective-permute-start | bytes 1769480 | tf_op jit(solution)/shard_map/ppermute | solution.py:129
  31.8 4.7 %collective-permute-start.5 = (f32[40,128]{1,0:T(8,128)S(1)}, f32[40,128]{1,0:T(8,128)S(1)}, u32[]{:S(2)}, u32[]{:S(2)}) collective-permute-start(f32[40,128]{1,0:T(8,128)S(1)} %add.162), channel_id=1, source_target_pairs={{0,17},{1,16},{2,19},{3,18},{4,21},{5,20},{6,23},{7,22},{8,25},{9,... | collective-permute-start | bytes 61448 | tf_op jit(solution)/shard_map/ppermute | solution.py:129
  34.2 5.1 %collective-permute-start.6 = (f32[40,128]{1,0:T(8,128)S(1)}, f32[40,128]{1,0:T(8,128)S(1)}, u32[]{:S(2)}, u32[]{:S(2)}) collective-permute-start(f32[40,128]{1,0:T(8,128)S(1)} %add.162), channel_id=1, source_target_pairs={{0,25},{1,24},{2,27},{3,26},{4,29},{5,28},{6,31},{7,30},{8,17},{9,... | collective-permute-start | bytes 61448 | tf_op jit(solution)/shard_map/ppermute | solution.py:129
  35.5 3.8 %collective-permute-start.4 = (f32[40,128]{1,0:T(8,128)S(1)}, f32[40,128]{1,0:T(8,128)S(1)}, u32[]{:S(2)}, u32[]{:S(2)}) collective-permute-start(f32[40,128]{1,0:T(8,128)S(1)} %add.162), channel_id=1, source_target_pairs={{0,9},{1,8},{2,11},{3,10},{4,13},{5,12},{6,15},{7,14},{8,1},{9,0},... | collective-permute-start | bytes 61448 | tf_op jit(solution)/shard_map/ppermute | solution.py:129
  42.1 101.9 %all-gather.6.cloned.1.call-start = ((), (), s32[]{:S(2)}) async-start(), calls=%async_computation | async-start | bytes 1081344 | tf_op jit(solution)/shard_map/all_gather | solution.py:533
  42.2 7.4 %collective-permute-start.11 = (f32[1152,128]{1,0:T(8,128)S(1)}, f32[1152,128]{1,0:T(8,128)S(1)}, u32[]{:S(2)}, u32[]{:S(2)}) collective-permute-start(f32[1152,128]{1,0:T(8,128)S(1)} %bitcast.91), channel_id=1, source_target_pairs={{0,1},{1,0},{2,3},{3,2},{4,5},{5,4},{6,7},{7,6},{8,9},{9,8},{10,11... | collective-permute-start | bytes 1769480 | tf_op jit(solution)/shard_map/ppermute | solution.py:129
  42.3 7.3 %collective-permute-start.12 = (f32[1152,128]{1,0:T(8,128)}, f32[1152,128]{1,0:T(8,128)S(1)}, u32[]{:S(2)}, u32[]{:S(2)}) collective-permute-start(f32[1152,128]{1,0:T(8,128)} %collective-permute-done.7.refs_4_), channel_id=1, source_target_pairs={{0,1},{1,0},{2,3},{3,2},{4,5},{5,4},{6,7},{7,6},{8,9},{9,8},{10,11... | collective-permute-start | bytes 1769480 | tf_op jit(solution)/shard_map/ppermute | solution.py:129
  43.8 4.1 %collective-permute-start.10 = (f32[40,128]{1,0:T(8,128)S(1)}, f32[40,128]{1,0:T(8,128)S(1)}, u32[]{:S(2)}, u32[]{:S(2)}) collective-permute-start(f32[40,128]{1,0:T(8,128)S(1)} %add_add_fusion.3), channel_id=1, source_target_pairs={{0,7},{1,6},{2,5},{3,4},{4,3},{5,2},{6,1},{7,0},{8,15},{9,14},{10,... | collective-permute-start | bytes 61448 | tf_op jit(solution)/shard_map/ppermute | solution.py:129
  45.4 3.6 %collective-permute-start.8 = (f32[40,128]{1,0:T(8,128)S(1)}, f32[40,128]{1,0:T(8,128)S(1)}, u32[]{:S(2)}, u32[]{:S(2)}) collective-permute-start(f32[40,128]{1,0:T(8,128)S(1)} %add_add_fusion.3), channel_id=1, source_target_pairs={{0,3},{1,2},{2,1},{3,0},{4,7},{5,6},{6,5},{7,4},{8,11},{9,10},{10,... | collective-permute-start | bytes 61448 | tf_op jit(solution)/shard_map/ppermute | solution.py:129
  56.6 4.0 %collective-permute-start.15 = (f32[2,512]{1,0:T(2,128)S(1)}, f32[2,512]{1,0:T(2,128)S(1)}, u32[]{:S(2)}, u32[]{:S(2)}) collective-permute-start(f32[2,512]{1,0:T(2,128)S(1)} %add.169), channel_id=1, source_target_pairs={{0,17},{1,16},{2,19},{3,18},{4,21},{5,20},{6,23},{7,22},{8,25},{9,... | collective-permute-start | bytes 12296 | tf_op jit(solution)/shard_map/ppermute | solution.py:129
  59.0 4.8 %collective-permute-start.16 = (f32[2,512]{1,0:T(2,128)S(1)}, f32[2,512]{1,0:T(2,128)S(1)}, u32[]{:S(2)}, u32[]{:S(2)}) collective-permute-start(f32[2,512]{1,0:T(2,128)S(1)} %add.169), channel_id=1, source_target_pairs={{0,25},{1,24},{2,27},{3,26},{4,29},{5,28},{6,31},{7,30},{8,17},{9,... | collective-permute-start | bytes 12296 | tf_op jit(solution)/shard_map/ppermute | solution.py:129
  60.2 3.6 %collective-permute-start.14 = (f32[2,512]{1,0:T(2,128)S(1)}, f32[2,512]{1,0:T(2,128)S(1)}, u32[]{:S(2)}, u32[]{:S(2)}) collective-permute-start(f32[2,512]{1,0:T(2,128)S(1)} %add.169), channel_id=1, source_target_pairs={{0,9},{1,8},{2,11},{3,10},{4,13},{5,12},{6,15},{7,14},{8,1},{9,0},... | collective-permute-start | bytes 12296 | tf_op jit(solution)/shard_map/ppermute | solution.py:129
  64.9 3.9 %collective-permute-start.19 = (f32[2,512]{1,0:T(2,128)S(1)}, f32[2,512]{1,0:T(2,128)S(1)}, u32[]{:S(2)}, u32[]{:S(2)}) collective-permute-start(f32[2,512]{1,0:T(2,128)S(1)} %add_add_fusion.9), channel_id=1, source_target_pairs={{0,7},{1,6},{2,5},{3,4},{4,3},{5,2},{6,1},{7,0},{8,15},{9,14},{10,... | collective-permute-start | bytes 12296 | tf_op jit(solution)/shard_map/ppermute | solution.py:129
  71.1 94.1 %all-gather.10.cloned.1.call-start = ((), (), s32[]{:S(2)}) async-start(), calls=%async_computation.2 | async-start | bytes 2293760 | tf_op jit(solution)/shard_map/all_gather | solution.py:535
  72.5 3.9 %collective-permute-start.22 = (f32[2,128]{1,0:T(2,128)S(1)}, f32[2,128]{1,0:T(2,128)S(1)}, u32[]{:S(2)}, u32[]{:S(2)}) collective-permute-start(f32[2,128]{1,0:T(2,128)S(1)} %add.176), channel_id=1, source_target_pairs={{0,17},{1,16},{2,19},{3,18},{4,21},{5,20},{6,23},{7,22},{8,25},{9,... | collective-permute-start | bytes 3080 | tf_op jit(solution)/shard_map/ppermute | solution.py:129
  73.4 4.8 %collective-permute-start.23 = (f32[2,128]{1,0:T(2,128)S(1)}, f32[2,128]{1,0:T(2,128)S(1)}, u32[]{:S(2)}, u32[]{:S(2)}) collective-permute-start(f32[2,128]{1,0:T(2,128)S(1)} %add.176), channel_id=1, source_target_pairs={{0,25},{1,24},{2,27},{3,26},{4,29},{5,28},{6,31},{7,30},{8,17},{9,... | collective-permute-start | bytes 3080 | tf_op jit(solution)/shard_map/ppermute | solution.py:129
  74.3 3.9 %collective-permute-start.21 = (f32[2,128]{1,0:T(2,128)S(1)}, f32[2,128]{1,0:T(2,128)S(1)}, u32[]{:S(2)}, u32[]{:S(2)}) collective-permute-start(f32[2,128]{1,0:T(2,128)S(1)} %add.176), channel_id=1, source_target_pairs={{0,9},{1,8},{2,11},{3,10},{4,13},{5,12},{6,15},{7,14},{8,1},{9,0},... | collective-permute-start | bytes 3080 | tf_op jit(solution)/shard_map/ppermute | solution.py:129
  79.5 3.9 %collective-permute-start.26 = (f32[2,128]{1,0:T(2,128)S(1)}, f32[2,128]{1,0:T(2,128)S(1)}, u32[]{:S(2)}, u32[]{:S(2)}) collective-permute-start(f32[2,128]{1,0:T(2,128)S(1)} %add_add_fusion.13), channel_id=1, source_target_pairs={{0,7},{1,6},{2,5},{3,4},{4,3},{5,2},{6,1},{7,0},{8,15},{9,14},{10,... | collective-permute-start | bytes 3080 | tf_op jit(solution)/shard_map/ppermute | solution.py:129
  85.9 13.3 %collective-permute-start.32 = (f32[448,256]{1,0:T(8,128)S(1)}, f32[448,256]{1,0:T(8,128)S(1)}, u32[]{:S(2)}, u32[]{:S(2)}) collective-permute-start(f32[448,256]{1,0:T(8,128)S(1)} %get-tuple-element.150.refs_0_.refs_1_.refs_3_), channel_id=1, source_target_pairs={{0,2},{1,3},{2,0},{3,1},{4,6},{5,7},{6,4},{7,5},{8,10},{9,11},{10,... | collective-permute-start | bytes 1376264 | tf_op jit(solution)/shard_map/ppermute | solution.py:129
  90.6 4.0 %collective-permute-start.30 = (f32[8,256]{1,0:T(8,128)S(1)}, f32[8,256]{1,0:T(8,128)S(1)}, u32[]{:S(2)}, u32[]{:S(2)}) collective-permute-start(f32[8,256]{1,0:T(8,128)S(1)} %add.183), channel_id=1, source_target_pairs={{0,17},{1,16},{2,19},{3,18},{4,21},{5,20},{6,23},{7,22},{8,25},{9,... | collective-permute-start | bytes 24584 | tf_op jit(solution)/shard_map/ppermute | solution.py:129
  91.4 4.9 %collective-permute-start.31 = (f32[8,256]{1,0:T(8,128)S(1)}, f32[8,256]{1,0:T(8,128)S(1)}, u32[]{:S(2)}, u32[]{:S(2)}) collective-permute-start(f32[8,256]{1,0:T(8,128)S(1)} %add.183), channel_id=1, source_target_pairs={{0,25},{1,24},{2,27},{3,26},{4,29},{5,28},{6,31},{7,30},{8,17},{9,... | collective-permute-start | bytes 24584 | tf_op jit(solution)/shard_map/ppermute | solution.py:129
  99.2 5.2 %collective-permute-start.36 = (f32[448,256]{1,0:T(8,128)S(1)}, f32[448,256]{1,0:T(8,128)S(1)}, u32[]{:S(2)}, u32[]{:S(2)}) collective-permute-start(f32[448,256]{1,0:T(8,128)S(1)} %collective-permute-done.32.refs_1_), channel_id=1, source_target_pairs={{0,1},{1,0},{2,3},{3,2},{4,5},{5,4},{6,7},{7,6},{8,9},{9,8},{10,11... | collective-permute-start | bytes 1376264 | tf_op jit(solution)/shard_map/ppermute | solution.py:129
  100.3 4.0 %collective-permute-start.35 = (f32[8,256]{1,0:T(8,128)S(1)}, f32[8,256]{1,0:T(8,128)S(1)}, u32[]{:S(2)}, u32[]{:S(2)}) collective-permute-start(f32[8,256]{1,0:T(8,128)S(1)} %add_add_fusion.7), channel_id=1, source_target_pairs={{0,7},{1,6},{2,5},{3,4},{4,3},{5,2},{6,1},{7,0},{8,15},{9,14},{10,... | collective-permute-start | bytes 24584 | tf_op jit(solution)/shard_map/ppermute | solution.py:129
  112.5 13.7 %collective-permute-start.39 = (f32[448,256]{1,0:T(8,128)S(1)}, f32[448,256]{1,0:T(8,128)S(1)}, u32[]{:S(2)}, u32[]{:S(2)}) collective-permute-start(f32[448,256]{1,0:T(8,128)S(1)} %add.190), channel_id=1, source_target_pairs={{0,2},{1,3},{2,0},{3,1},{4,6},{5,7},{6,4},{7,5},{8,10},{9,11},{10,... | collective-permute-start | bytes 1376264 | tf_op jit(solution)/shard_map/ppermute | solution.py:129
  120.7 4.0 %collective-permute-start.42 = (f32[8,256]{1,0:T(8,128)S(1)}, f32[8,256]{1,0:T(8,128)S(1)}, u32[]{:S(2)}, u32[]{:S(2)}) collective-permute-start(f32[8,256]{1,0:T(8,128)S(1)} %add.191), channel_id=1, source_target_pairs={{0,17},{1,16},{2,19},{3,18},{4,21},{5,20},{6,23},{7,22},{8,25},{9,... | collective-permute-start | bytes 24584 | tf_op jit(solution)/shard_map/ppermute | solution.py:129
  121.3 4.9 %collective-permute-start.43 = (f32[8,256]{1,0:T(8,128)S(1)}, f32[8,256]{1,0:T(8,128)S(1)}, u32[]{:S(2)}, u32[]{:S(2)}) collective-permute-start(f32[8,256]{1,0:T(8,128)S(1)} %add.191), channel_id=1, source_target_pairs={{0,25},{1,24},{2,27},{3,26},{4,29},{5,28},{6,31},{7,30},{8,17},{9,... | collective-permute-start | bytes 24584 | tf_op jit(solution)/shard_map/ppermute | solution.py:129
  123.7 8.1 %collective-permute-start.38 = (f32[448,256]{1,0:T(8,128)S(1)}, f32[448,256]{1,0:T(8,128)S(1)}, u32[]{:S(2)}, u32[]{:S(2)}) collective-permute-start(f32[448,256]{1,0:T(8,128)S(1)} %get-tuple-element.162), channel_id=1, source_target_pairs={{0,1},{1,0},{2,3},{3,2},{4,5},{5,4},{6,7},{7,6},{8,9},{9,8},{10,11... | collective-permute-start | bytes 1376264 | tf_op jit(solution)/shard_map/ppermute | solution.py:129
  127.5 4.0 %collective-permute-start.46 = (f32[8,256]{1,0:T(8,128)S(1)}, f32[8,256]{1,0:T(8,128)S(1)}, u32[]{:S(2)}, u32[]{:S(2)}) collective-permute-start(f32[8,256]{1,0:T(8,128)S(1)} %add_add_fusion.5), channel_id=1, source_target_pairs={{0,7},{1,6},{2,5},{3,4},{4,3},{5,2},{6,1},{7,0},{8,15},{9,14},{10,... | collective-permute-start | bytes 24584 | tf_op jit(solution)/shard_map/ppermute | solution.py:129
  136.8 5.5 %collective-permute-start.49 = (f32[80,128]{1,0:T(8,128)S(1)}, f32[80,128]{1,0:T(8,128)S(1)}, u32[]{:S(2)}, u32[]{:S(2)}) collective-permute-start(f32[80,128]{1,0:T(8,128)S(1)} %add.198), channel_id=1, source_target_pairs={{0,17},{1,16},{2,19},{3,18},{4,21},{5,20},{6,23},{7,22},{8,25},{9,... | collective-permute-start | bytes 122888 | tf_op jit(solution)/shard_map/ppermute | solution.py:129
  137.5 5.4 %collective-permute-start.50 = (f32[80,128]{1,0:T(8,128)S(1)}, f32[80,128]{1,0:T(8,128)S(1)}, u32[]{:S(2)}, u32[]{:S(2)}) collective-permute-start(f32[80,128]{1,0:T(8,128)S(1)} %add.198), channel_id=1, source_target_pairs={{0,25},{1,24},{2,27},{3,26},{4,29},{5,28},{6,31},{7,30},{8,17},{9,... | collective-permute-start | bytes 122888 | tf_op jit(solution)/shard_map/ppermute | solution.py:129
  139.3 4.6 %collective-permute-start.48 = (f32[80,128]{1,0:T(8,128)S(1)}, f32[80,128]{1,0:T(8,128)S(1)}, u32[]{:S(2)}, u32[]{:S(2)}) collective-permute-start(f32[80,128]{1,0:T(8,128)S(1)} %add.198), channel_id=1, source_target_pairs={{0,9},{1,8},{2,11},{3,10},{4,13},{5,12},{6,15},{7,14},{8,1},{9,0},... | collective-permute-start | bytes 122888 | tf_op jit(solution)/shard_map/ppermute | solution.py:129
  145.9 3.5 %collective-permute-start.52 = (f32[80,128]{1,0:T(8,128)S(1)}, f32[80,128]{1,0:T(8,128)S(1)}, u32[]{:S(2)}, u32[]{:S(2)}) collective-permute-start(f32[80,128]{1,0:T(8,128)S(1)} %add_add_fusion.1), channel_id=1, source_target_pairs={{0,5},{1,4},{2,7},{3,6},{4,1},{5,0},{6,3},{7,2},{8,13},{9,12},{10,... | collective-permute-start | bytes 122888 | tf_op jit(solution)/shard_map/ppermute | solution.py:129
  147.3 4.4 %collective-permute-start.53 = (f32[80,128]{1,0:T(8,128)S(1)}, f32[80,128]{1,0:T(8,128)S(1)}, u32[]{:S(2)}, u32[]{:S(2)}) collective-permute-start(f32[80,128]{1,0:T(8,128)S(1)} %add_add_fusion.1), channel_id=1, source_target_pairs={{0,7},{1,6},{2,5},{3,4},{4,3},{5,2},{6,1},{7,0},{8,15},{9,14},{10,... | collective-permute-start | bytes 122888 | tf_op jit(solution)/shard_map/ppermute | solution.py:129
  148.4 4.6 %collective-permute-start.51 = (f32[80,128]{1,0:T(8,128)S(1)}, f32[80,128]{1,0:T(8,128)S(1)}, u32[]{:S(2)}, u32[]{:S(2)}) collective-permute-start(f32[80,128]{1,0:T(8,128)S(1)} %add_add_fusion.1), channel_id=1, source_target_pairs={{0,3},{1,2},{2,1},{3,0},{4,7},{5,6},{6,5},{7,4},{8,11},{9,10},{10,... | collective-permute-start | bytes 122888 | tf_op jit(solution)/shard_map/ppermute | solution.py:129
  155.5 12.8 %collective-permute-start.57 = (f32[456,128]{1,0:T(8,128)S(1)}, f32[456,128]{1,0:T(8,128)}, u32[]{:S(2)}, u32[]{:S(2)}) collective-permute-start(f32[456,128]{1,0:T(8,128)S(1)} %get-tuple-element.197), channel_id=1, source_target_pairs={{0,1},{1,0},{2,3},{3,2},{4,5},{5,4},{6,7},{7,6},{8,9},{9,8},{10,11... | collective-permute-start | bytes 700424 | tf_op jit(solution)/shard_map/ppermute | solution.py:129
  155.7 12.6 %collective-permute-start.58 = (f32[456,128]{1,0:T(8,128)S(1)}, f32[456,128]{1,0:T(8,128)}, u32[]{:S(2)}, u32[]{:S(2)}) collective-permute-start(f32[456,128]{1,0:T(8,128)S(1)} %get-tuple-element.198), channel_id=1, source_target_pairs={{0,2},{1,3},{2,0},{3,1},{4,6},{5,7},{6,4},{7,5},{8,10},{9,11},{10,... | collective-permute-start | bytes 700424 | tf_op jit(solution)/shard_map/ppermute | solution.py:129
  156.4 12.0 %collective-permute-start.59 = (f32[456,128]{1,0:T(8,128)S(1)}, f32[456,128]{1,0:T(8,128)}, u32[]{:S(2)}, u32[]{:S(2)}) collective-permute-start(f32[456,128]{1,0:T(8,128)S(1)} %get-tuple-element.199), channel_id=1, source_target_pairs={{0,3},{1,2},{2,1},{3,0},{4,7},{5,6},{6,5},{7,4},{8,11},{9,10},{10,... | collective-permute-start | bytes 700424 | tf_op jit(solution)/shard_map/ppermute | solution.py:129
  167.7 12.8 %collective-permute-start.54 = (f32[448,256]{1,0:T(8,128)S(1)}, f32[448,256]{1,0:T(8,128)S(1)}, u32[]{:S(2)}, u32[]{:S(2)}) collective-permute-start(f32[448,256]{1,0:T(8,128)S(1)} %get-tuple-element.189.refs_0_), channel_id=1, source_target_pairs={{0,2},{1,3},{2,0},{3,1},{4,6},{5,7},{6,4},{7,5},{8,10},{9,11},{10,... | collective-permute-start | bytes 1376264 | tf_op jit(solution)/shard_map/ppermute | solution.py:129
  172.8 12.8 %collective-permute-start.75 = (f32[896,128]{1,0:T(8,128)S(1)}, f32[896,128]{1,0:T(8,128)S(1)}, u32[]{:S(2)}, u32[]{:S(2)}) collective-permute-start(f32[896,128]{1,0:T(8,128)S(1)} %get-tuple-element.205), channel_id=1, source_target_pairs={{0,4},{4,0},{8,12},{12,8},{16,20},{20,16},{24,28},{28,24},{1,5},{5... | collective-permute-start | bytes 1376264 | tf_op jit(solution)/shard_map/ppermute | solution.py:129
  175.0 3.9 %collective-permute-start.62 = (f32[2,256]{1,0:T(2,128)S(1)}, f32[2,256]{1,0:T(2,128)S(1)}, u32[]{:S(2)}, u32[]{:S(2)}) collective-permute-start(f32[2,256]{1,0:T(2,128)S(1)} %add.205), channel_id=1, source_target_pairs={{0,17},{1,16},{2,19},{3,18},{4,21},{5,20},{6,23},{7,22},{8,25},{9,... | collective-permute-start | bytes 6152 | tf_op jit(solution)/shard_map/ppermute | solution.py:129
  175.8 4.8 %collective-permute-start.63 = (f32[2,256]{1,0:T(2,128)S(1)}, f32[2,256]{1,0:T(2,128)S(1)}, u32[]{:S(2)}, u32[]{:S(2)}) collective-permute-start(f32[2,256]{1,0:T(2,128)S(1)} %add.205), channel_id=1, source_target_pairs={{0,25},{1,24},{2,27},{3,26},{4,29},{5,28},{6,31},{7,30},{8,17},{9,... | collective-permute-start | bytes 6152 | tf_op jit(solution)/shard_map/ppermute | solution.py:129
  178.9 13.3 %collective-permute-start.55 = (f32[448,256]{1,0:T(8,128)S(1)}, f32[448,256]{1,0:T(8,128)S(1)}, u32[]{:S(2)}, u32[]{:S(2)}) collective-permute-start(f32[448,256]{1,0:T(8,128)S(1)} %get-tuple-element.189.refs_0_), channel_id=1, source_target_pairs={{0,1},{1,0},{2,3},{3,2},{4,5},{5,4},{6,7},{7,6},{8,9},{9,8},{10,11... | collective-permute-start | bytes 1376264 | tf_op jit(solution)/shard_map/ppermute | solution.py:129
  180.6 11.6 %collective-permute-start.56 = (f32[448,256]{1,0:T(8,128)S(1)}, f32[448,256]{1,0:T(8,128)S(1)}, u32[]{:S(2)}, u32[]{:S(2)}) collective-permute-start(f32[448,256]{1,0:T(8,128)S(1)} %collective-permute-done.54.refs_1_), channel_id=1, source_target_pairs={{0,1},{1,0},{2,3},{3,2},{4,5},{5,4},{6,7},{7,6},{8,9},{9,8},{10,11... | collective-permute-start | bytes 1376264 | tf_op jit(solution)/shard_map/ppermute | solution.py:129
  180.6 7.1 %collective-permute-start.65 = (f32[2,256]{1,0:T(2,128)S(1)}, f32[2,256]{1,0:T(2,128)S(1)}, u32[]{:S(2)}, u32[]{:S(2)}) collective-permute-start(f32[2,256]{1,0:T(2,128)S(1)} %add_add_fusion.11), channel_id=1, source_target_pairs={{0,5},{1,4},{2,7},{3,6},{4,1},{5,0},{6,3},{7,2},{8,13},{9,12},{10,... | collective-permute-start | bytes 6152 | tf_op jit(solution)/shard_map/ppermute | solution.py:129
  182.0 6.4 %collective-permute-start.66 = (f32[2,256]{1,0:T(2,128)S(1)}, f32[2,256]{1,0:T(2,128)S(1)}, u32[]{:S(2)}, u32[]{:S(2)}) collective-permute-start(f32[2,256]{1,0:T(2,128)S(1)} %add_add_fusion.11), channel_id=1, source_target_pairs={{0,7},{1,6},{2,5},{3,4},{4,3},{5,2},{6,1},{7,0},{8,15},{9,14},{10,... | collective-permute-start | bytes 6152 | tf_op jit(solution)/shard_map/ppermute | solution.py:129
  185.7 4.3 %collective-permute-start.64 = (f32[2,256]{1,0:T(2,128)S(1)}, f32[2,256]{1,0:T(2,128)S(1)}, u32[]{:S(2)}, u32[]{:S(2)}) collective-permute-start(f32[2,256]{1,0:T(2,128)S(1)} %add_add_fusion.11), channel_id=1, source_target_pairs={{0,3},{1,2},{2,1},{3,0},{4,7},{5,6},{6,5},{7,4},{8,11},{9,10},{10,... | collective-permute-start | bytes 6152 | tf_op jit(solution)/shard_map/ppermute | solution.py:129
  187.7 12.3 %collective-permute-start.76 = (f32[224,128]{1,0:T(8,128)S(1)}, f32[224,128]{1,0:T(8,128)S(1)}, u32[]{:S(2)}, u32[]{:S(2)}) collective-permute-start(f32[224,128]{1,0:T(8,128)S(1)} %get-tuple-element.224), channel_id=1, source_target_pairs={{0,8},{4,12},{8,0},{12,4},{16,24},{20,28},{24,16},{28,20},{1,9},{5... | collective-permute-start | bytes 344072 | tf_op jit(solution)/shard_map/ppermute | solution.py:129
  188.3 11.8 %collective-permute-start.77 = (f32[224,128]{1,0:T(8,128)S(1)}, f32[224,128]{1,0:T(8,128)S(1)}, u32[]{:S(2)}, u32[]{:S(2)}) collective-permute-start(f32[224,128]{1,0:T(8,128)S(1)} %get-tuple-element.225), channel_id=1, source_target_pairs={{0,16},{4,20},{8,24},{12,28},{16,0},{20,4},{24,8},{28,12},{1,17},{... | collective-permute-start | bytes 344072 | tf_op jit(solution)/shard_map/ppermute | solution.py:129
  189.9 10.2 %collective-permute-start.78 = (f32[224,128]{1,0:T(8,128)S(1)}, f32[224,128]{1,0:T(8,128)S(1)}, u32[]{:S(2)}, u32[]{:S(2)}) collective-permute-start(f32[224,128]{1,0:T(8,128)S(1)} %get-tuple-element.226), channel_id=1, source_target_pairs={{0,24},{4,28},{8,16},{12,20},{16,8},{20,12},{24,0},{28,4},{1,25},{... | collective-permute-start | bytes 344072 | tf_op jit(solution)/shard_map/ppermute | solution.py:129
  194.9 12.5 %collective-permute-start.67 = (f32[256,128]{1,0:T(8,128)S(1)}, f32[256,128]{1,0:T(8,128)S(1)}, u32[]{:S(2)}, u32[]{:S(2)}) collective-permute-start(f32[256,128]{1,0:T(8,128)S(1)} %get-tuple-element.216), channel_id=1, source_target_pairs={{0,4},{4,0},{8,12},{12,8},{16,20},{20,16},{24,28},{28,24},{1,5},{5... | collective-permute-start | bytes 393224 | tf_op jit(solution)/shard_map/ppermute | solution.py:129
  200.7 9.5 %collective-permute-start.79 = (f32[224,128]{1,0:T(8,128)S(1)}, f32[224,128]{1,0:T(8,128)S(1)}, u32[]{:S(2)}, u32[]{:S(2)}) collective-permute-start(f32[224,128]{1,0:T(8,128)S(1)} %shard_map.312.refs_0_), channel_id=1, source_target_pairs={{0,8},{4,12},{8,0},{12,4},{16,24},{20,28},{24,16},{28,20},{1,9},{5... | collective-permute-start | bytes 344072 | tf_op jit(solution)/shard_map/ppermute | solution.py:129
  204.4 12.7 %collective-permute-start.80 = (f32[224,128]{1,0:T(8,128)S(1)}, f32[224,128]{1,0:T(8,128)S(1)}, u32[]{:S(2)}, u32[]{:S(2)}) collective-permute-start(f32[224,128]{1,0:T(8,128)S(1)} %shard_map.312.refs_0_), channel_id=1, source_target_pairs={{0,16},{4,20},{8,24},{12,28},{16,0},{20,4},{24,8},{28,12},{1,17},{... | collective-permute-start | bytes 344072 | tf_op jit(solution)/shard_map/ppermute | solution.py:129
  204.6 12.6 %collective-permute-start.81 = (f32[224,128]{1,0:T(8,128)S(1)}, f32[224,128]{1,0:T(8,128)S(1)}, u32[]{:S(2)}, u32[]{:S(2)}) collective-permute-start(f32[224,128]{1,0:T(8,128)S(1)} %shard_map.312.refs_0_), channel_id=1, source_target_pairs={{0,24},{4,28},{8,16},{12,20},{16,8},{20,12},{24,0},{28,4},{1,25},{... | collective-permute-start | bytes 344072 | tf_op jit(solution)/shard_map/ppermute | solution.py:129
  208.0 10.5 %collective-permute-start.68 = (f32[64,128]{1,0:T(8,128)S(1)}, f32[64,128]{1,0:T(8,128)S(1)}, u32[]{:S(2)}, u32[]{:S(2)}) collective-permute-start(f32[64,128]{1,0:T(8,128)S(1)} %get-tuple-element.218), channel_id=1, source_target_pairs={{0,8},{4,12},{8,0},{12,4},{16,24},{20,28},{24,16},{28,20},{1,9},{5... | collective-permute-start | bytes 98312 | tf_op jit(solution)/shard_map/ppermute | solution.py:129
  209.2 10.9 %collective-permute-start.69 = (f32[64,128]{1,0:T(8,128)S(1)}, f32[64,128]{1,0:T(8,128)S(1)}, u32[]{:S(2)}, u32[]{:S(2)}) collective-permute-start(f32[64,128]{1,0:T(8,128)S(1)} %get-tuple-element.219), channel_id=1, source_target_pairs={{0,16},{4,20},{8,24},{12,28},{16,0},{20,4},{24,8},{28,12},{1,17},{... | collective-permute-start | bytes 98312 | tf_op jit(solution)/shard_map/ppermute | solution.py:129
  210.2 9.8 %collective-permute-start.70 = (f32[64,128]{1,0:T(8,128)S(1)}, f32[64,128]{1,0:T(8,128)S(1)}, u32[]{:S(2)}, u32[]{:S(2)}) collective-permute-start(f32[64,128]{1,0:T(8,128)S(1)} %get-tuple-element.220), channel_id=1, source_target_pairs={{0,24},{4,28},{8,16},{12,20},{16,8},{20,12},{24,0},{28,4},{1,25},{... | collective-permute-start | bytes 98312 | tf_op jit(solution)/shard_map/ppermute | solution.py:129
  217.7 17.7 %collective-permute-start.82 = (f32[896,128]{1,0:T(8,128)S(1)}, f32[896,128]{1,0:T(8,128)S(1)}, u32[]{:S(2)}, u32[]{:S(2)}) collective-permute-start(f32[896,128]{1,0:T(8,128)S(1)} %shard_map.313.refs_0_), channel_id=1, source_target_pairs={{0,4},{4,0},{8,12},{12,8},{16,20},{20,16},{24,28},{28,24},{1,5},{5... | collective-permute-start | bytes 1376264 | tf_op jit(solution)/shard_map/ppermute | solution.py:129
  220.6 5.0 %collective-permute-start.71 = (f32[64,128]{1,0:T(8,128)S(1)}, f32[64,128]{1,0:T(8,128)S(1)}, u32[]{:S(2)}, u32[]{:S(2)}) collective-permute-start(f32[64,128]{1,0:T(8,128)S(1)} %shard_map.308.refs_0_), channel_id=1, source_target_pairs={{0,8},{4,12},{8,0},{12,4},{16,24},{20,28},{24,16},{28,20},{1,9},{5... | collective-permute-start | bytes 98312 | tf_op jit(solution)/shard_map/ppermute | solution.py:129
  221.9 5.2 %collective-permute-start.72 = (f32[64,128]{1,0:T(8,128)S(1)}, f32[64,128]{1,0:T(8,128)S(1)}, u32[]{:S(2)}, u32[]{:S(2)}) collective-permute-start(f32[64,128]{1,0:T(8,128)S(1)} %shard_map.308.refs_0_), channel_id=1, source_target_pairs={{0,16},{4,20},{8,24},{12,28},{16,0},{20,4},{24,8},{28,12},{1,17},{... | collective-permute-start | bytes 98312 | tf_op jit(solution)/shard_map/ppermute | solution.py:129
  222.8 5.7 %collective-permute-start.73 = (f32[64,128]{1,0:T(8,128)S(1)}, f32[64,128]{1,0:T(8,128)S(1)}, u32[]{:S(2)}, u32[]{:S(2)}) collective-permute-start(f32[64,128]{1,0:T(8,128)S(1)} %shard_map.308.refs_0_), channel_id=1, source_target_pairs={{0,24},{4,28},{8,16},{12,20},{16,8},{20,12},{24,0},{28,4},{1,25},{... | collective-permute-start | bytes 98312 | tf_op jit(solution)/shard_map/ppermute | solution.py:129
  229.1 5.0 %collective-permute-start.74 = (f32[256,128]{1,0:T(8,128)S(1)}, f32[256,128]{1,0:T(8,128)S(1)}, u32[]{:S(2)}, u32[]{:S(2)}) collective-permute-start(f32[256,128]{1,0:T(8,128)S(1)} %shard_map.309.refs_0_), channel_id=1, source_target_pairs={{0,4},{4,0},{8,12},{12,8},{16,20},{20,16},{24,28},{28,24},{1,5},{5... | collective-permute-start | bytes 393224 | tf_op jit(solution)/shard_map/ppermute | solution.py:129
  (40 other events, 303.6 us)
Sparse Core Ops, SparseCore 0:
  42.2 20.0 all-gather.7
  71.2 52.5 all-gather.5
  125.4 20.2 all-gather.9
